TPU v7x, 32 devices: a whole 2x2x4 slice. The times are simulated.
32 devices in a mesh: tm: 8 (over z, x), height: 4 (over y, core).
Axes of the slice: x: 2, y: 2, z: 4, core: 2. Of those that a mesh axis runs over, the one named last changes fastest.
Arguments:
- query_tok: bfloat16 [8, 8, 64, 1536], P('tm', 'height'), may hold values from -6 to 6
- key_tok: bfloat16 [8, 8, 64, 1536], P('tm', 'height'), may hold values from -6 to 6
- value_tok: bfloat16 [8, 8, 64, 1536], P('tm', 'height'), may hold values from -6 to 6
- grad_out: bfloat16 [8, 8, 64, 1536], P('tm', 'height'), may hold values from -6 to 6
- far_picks: int32 [8, 4, 12, 2], P('tm', 'height'), may hold values from 0 to 3
Outputs:
- grad_query: bfloat16 [8, 8, 64, 1536], P('tm', 'height')
- grad_key: bfloat16 [8, 8, 64, 1536], P('tm', 'height')
- grad_value: bfloat16 [8, 8, 64, 1536], P('tm', 'height')
All inputs are finite; a program needn't handle non-finite values.
Results may differ from a plain program's by a relative error of at most 0.012.
The roundings to bfloat16 on the way count: a program that leaves them out, or rounds other values in their place, can miss the bound.
Values may be sent and summed in bfloat16 or wider, within the bound.
No kernel may reach another device: no remote copies, remote signals or barrier semaphores. Data moves between devices by JAX's collectives and lax.ppermute only.
A program may use at most 64 MiB of HBM per device.

v0:
```python
import jax
import jax.numpy as jnp
from jax import lax
from jax.sharding import PartitionSpec as P

HEAD_DIM = 128
REACH = 2


def shifted(block, axis, distance):
    devices = range(lax.axis_size(axis))
    route = [((i - distance) % len(devices), i) for i in devices]
    return lax.ppermute(block, axis, route)


def padded_2(value, sides, width):
    for axis, dim in sides:
        size, length = (lax.axis_size(axis), value.shape[dim])
        up = [(i, (i + 1) % size) for i in range(size - 1)]
        down = [(j, i) for i, j in up]
        last = lax.slice_in_dim(value, length - width, length, axis=dim)
        first = lax.slice_in_dim(value, 0, width, axis=dim)
        before = lax.ppermute(last, axis, up)
        after = lax.ppermute(first, axis, down)
        value = jnp.concatenate([before, value, after], axis=dim)
    return value


def pair_grads(query_rows, key_rows, value_rows, grad_rows, usable):
    score_scale = HEAD_DIM ** (-0.5)
    query_h = query_rows.transpose(1, 0, 2)
    key_h = key_rows.transpose(1, 0, 2)
    value_h = value_rows.transpose(1, 0, 2)
    grad_h = grad_rows.transpose(1, 0, 2)
    mask_bias = jnp.where(usable, 0.0, -jnp.inf).astype(jnp.float32)[:, None, :]
    scores = (
        jnp.einsum("hqd,hkd->hqk", query_h, key_h, preferred_element_type=jnp.float32) * score_scale
        + mask_bias
    )
    row_top = jnp.max(scores, axis=2, keepdims=True)
    expo = jnp.exp(scores - row_top)
    weights = expo / jnp.sum(expo, axis=2, keepdims=True)
    weights_b = weights.astype(jnp.bfloat16)
    attended = jnp.einsum("hqk,hkd->hqd", weights_b, value_h, preferred_element_type=jnp.float32)
    row_delta = jnp.sum(grad_h.astype(jnp.float32) * attended, axis=2)
    value_grad = jnp.einsum("hqk,hqd->hkd", weights_b, grad_h, preferred_element_type=jnp.float32)
    grad_weights = jnp.einsum("hqd,hkd->hqk", grad_h, value_h, preferred_element_type=jnp.float32)
    dscore = (weights * (grad_weights - row_delta[:, :, None]) * score_scale).astype(jnp.bfloat16)
    query_grad = jnp.einsum("hqk,hkd->hqd", dscore, key_h, preferred_element_type=jnp.float32)
    key_grad = jnp.einsum("hqk,hqd->hkd", dscore, query_h, preferred_element_type=jnp.float32)
    return (
        query_grad.transpose(1, 0, 2),
        key_grad.transpose(1, 0, 2),
        value_grad.transpose(1, 0, 2),
    )


def fetch_direct(key_value, shift_by):
    return shifted(key_value, "tm", -shift_by)


def send_back(piece, shift_by):
    return shifted(piece, "tm", shift_by)


def per_device(query_tok, key_tok, value_tok, grad_out, far_picks):
    frames_dev, rows_dev, columns, width = query_tok.shape
    tile = frames_dev * rows_dev * columns
    face = frames_dev * columns
    heads = width // HEAD_DIM
    offset_list = [shift_by for shift_by in range(-REACH, REACH + 1) if shift_by != 0]
    offset_arr = jnp.array(offset_list, dtype=jnp.int32)
    cycle_pos = lax.axis_index("tm")
    cycle_size = lax.axis_size("tm")
    key_value = jnp.concatenate([key_tok, value_tok], axis=3)
    padded = padded_2(key_value, (("height", 1),), 1)
    upper_face = padded[:, 0]
    lower_face = padded[:, rows_dev + 1]
    remote = {}
    for shift_by in offset_list:
        remote[shift_by] = fetch_direct(key_value, shift_by)
    blocks = [
        key_value.reshape(tile, 2 * width),
        upper_face.reshape(face, 2 * width),
        lower_face.reshape(face, 2 * width),
    ]
    for shift_by in offset_list:
        blocks.append(remote[shift_by].reshape(tile, 2 * width))
    stacked = jnp.concatenate(blocks, axis=0)
    total_keys = stacked.shape[0]
    line_pos = lax.axis_index("height")
    line_size = lax.axis_size("height")
    target = cycle_pos + offset_arr
    far_ok = (target >= 0) & (target < cycle_size)
    choose = jnp.arange(2 * REACH, dtype=jnp.int32)
    chosen = jnp.any(far_picks[0, 0][:, :, None] == choose, axis=1) & far_ok[None, :]
    usable = jnp.concatenate(
        [
            jnp.ones((heads, tile), jnp.bool_),
            jnp.broadcast_to(line_pos > 0, (heads, face)),
            jnp.broadcast_to(line_pos < line_size - 1, (heads, face)),
            jnp.repeat(chosen, tile, axis=1),
        ],
        axis=1,
    )
    query_grad, key_grad, value_grad = pair_grads(
        query_tok.reshape(tile, heads, HEAD_DIM),
        stacked[:, :width].reshape(total_keys, heads, HEAD_DIM),
        stacked[:, width:].reshape(total_keys, heads, HEAD_DIM),
        grad_out.reshape(tile, heads, HEAD_DIM),
        usable,
    )
    key_grads = jnp.concatenate(
        [key_grad.reshape(total_keys, width), value_grad.reshape(total_keys, width)], axis=1
    )
    own_part = key_grads[:tile].reshape(frames_dev, rows_dev, columns, 2 * width)
    face_parts = jnp.stack(
        [
            key_grads[tile : tile + face].reshape(frames_dev, columns, 2 * width),
            key_grads[tile + face : tile + 2 * face].reshape(frames_dev, columns, 2 * width),
        ],
        axis=1,
    ).astype(jnp.bfloat16)
    returned = padded_2(face_parts, (("height", 1),), 1).astype(jnp.float32)
    own_part = own_part.at[:, 0].add(returned[:, 0]).at[:, rows_dev - 1].add(returned[:, 3])
    for slot_index, shift_by in enumerate(offset_list):
        start = tile + 2 * face + slot_index * tile
        piece = (
            key_grads[start : start + tile]
            .astype(jnp.bfloat16)
            .reshape(frames_dev, rows_dev, columns, 2 * width)
        )
        own_part = own_part + send_back(piece, shift_by).astype(jnp.float32)
    grad_query = query_grad.reshape(frames_dev, rows_dev, columns, width).astype(jnp.bfloat16)
    return (
        grad_query,
        own_part[..., :width].astype(jnp.bfloat16),
        own_part[..., width:].astype(jnp.bfloat16),
    )


def solution(mesh):
    return jax.shard_map(
        per_device,
        mesh=mesh,
        in_specs=(
            P("tm", "height", None, None),
            P("tm", "height", None, None),
            P("tm", "height", None, None),
            P("tm", "height", None, None),
            P("tm", "height", None, None),
        ),
        out_specs=(
            P("tm", "height", None, None),
            P("tm", "height", None, None),
            P("tm", "height", None, None),
        ),
        check_vma=False,
    )
```

profile of v0, /device:TPU:1, one launch (start us, length us, event | category | flops | bytes accessed | tf_op | source)
XLA Modules:
  0.0 171.2 jit_solution(15182272240148818674)
XLA Ops:
  0.6 1.0 constant_dynamic-update-slice_fusion.1
  1.7 1.0 constant_dynamic-update-slice_fusion
  2.7 2.2 %collective-permute-start.2 = (bf16[1,2,64,3072]{3,2,1,0:T(8,128)(2,1)S(1)}, bf16[1,2,64,3072]{3,2,1,0:T(8,128)(2,1)}, u32[]{:S(2)}, u32[]{:S(2)}) collective-permute-start(bf16[1,2,64,3072]{3,2,1,0:T(8,128)(2,1)S(1)} %constant_dynamic-update-slice_fusion), channel_id=1, source_target_pairs={{24,0},{28,4},{0,8},{4,12},{8,16},{12,20},{16,24},{20,28},{25,1},{... | collective-permute-start | bytes 2359304 | tf_op jit(solution)/shard_map/ppermute | solution.py:13
  4.9 1.2 collective-permute-start.3
  6.1 3.0 %collective-permute-start.4 = (bf16[1,2,64,3072]{3,2,1,0:T(8,128)(2,1)S(1)}, bf16[1,2,64,3072]{3,2,1,0:T(8,128)(2,1)}, u32[]{:S(2)}, u32[]{:S(2)}) collective-permute-start(bf16[1,2,64,3072]{3,2,1,0:T(8,128)(2,1)S(1)} %constant_dynamic-update-slice_fusion), channel_id=1, source_target_pairs={{4,0},{8,4},{12,8},{16,12},{20,16},{24,20},{28,24},{0,28},{5,1},{9... | collective-permute-start | bytes 2359304 | tf_op jit(solution)/shard_map/ppermute | solution.py:13
  9.1 0.3 collective-permute-start.5
  9.3 0.9 fusion.41
  10.3 4.7 %collective-permute-start = (bf16[1,1,64,3072]{3,2,1,0:T(8,128)(2,1)}, bf16[1,1,64,3072]{3,2,1,0:T(8,128)(2,1)}, u32[]{:S(2)}, u32[]{:S(2)}) collective-permute-start(bf16[1,1,64,3072]{3,2,1,0:T(8,128)(2,1)} %get-tuple-element.38), channel_id=1, source_target_pairs={{0,1},{1,2},{2,3},{4,5},{5,6},{6,7},{8,9},{9,10},{10,11},{12,13},{... | collective-permute-start | bytes 1179656 | tf_op jit(solution)/shard_map/ppermute | solution.py:23
  15.0 0.7 fusion.36
  15.7 0.7 compare_and_fusion
  16.3 0.1 broadcast_and_fusion
  16.4 0.1 copy.62
  16.5 0.1 broadcast_in_dim.29
  16.7 0.1 add_add_fusion
  16.8 1.3 reshape.273
  18.1 0.4 copy.72
  18.5 1.3 reshape.275
  19.7 1.1 copy.65
  20.9 1.9 %collective-permute-start.1 = (bf16[1,1,64,3072]{3,2,1,0:T(8,128)(2,1)}, bf16[1,1,64,3072]{3,2,1,0:T(8,128)(2,1)S(1)}, u32[]{:S(2)}, u32[]{:S(2)}) collective-permute-start(bf16[1,1,64,3072]{3,2,1,0:T(8,128)(2,1)} %get-tuple-element.37), channel_id=1, source_target_pairs={{1,0},{2,1},{3,2},{5,4},{6,5},{7,6},{9,8},{10,9},{11,10},{13,12},{... | collective-permute-start | bytes 1179656 | tf_op jit(solution)/shard_map/ppermute | solution.py:24
  22.8 1.0 bitcast_dynamic-update-slice_fusion.1
  23.9 6.8 %collective-permute-done.1 = bf16[1,1,64,3072]{3,2,1,0:T(8,128)(2,1)S(1)} collective-permute-done((bf16[1,1,64,3072]{3,2,1,0:T(8,128)(2,1)}, bf16[1,1,64,3072]{3,2,1,0:T(8,128)(2,1)S(1)}, u32[]{:S(2)}, u32[]{:S(2)}) %collective-permute-start.1) | collective-permute-done | bytes 393248 | tf_op jit(solution)/shard_map/ppermute | solution.py:24
  30.7 1.2 constant_dynamic-update-slice_fusion.5
  31.8 10.0 %collective-permute-done.3 = bf16[1,2,64,3072]{3,2,1,0:T(8,128)(2,1)} collective-permute-done((bf16[1,2,64,3072]{3,2,1,0:T(8,128)(2,1)S(1)}, bf16[1,2,64,3072]{3,2,1,0:T(8,128)(2,1)}, u32[]{:S(2)}, u32[]{:S(2)}) %collective-permute-start.3) | collective-permute-done | bytes 786464 | tf_op jit(solution)/shard_map/ppermute | solution.py:13
  41.9 1.2 constant_dynamic-update-slice_fusion.4
  43.1 1.2 constant_dynamic-update-slice_fusion.3
  44.3 14.4 %collective-permute-done.5 = bf16[1,2,64,3072]{3,2,1,0:T(8,128)(2,1)S(1)} collective-permute-done((bf16[1,2,64,3072]{3,2,1,0:T(8,128)(2,1)S(1)}, bf16[1,2,64,3072]{3,2,1,0:T(8,128)(2,1)S(1)}, u32[]{:S(2)}, u32[]{:S(2)}) %collective-permute-start.5) | collective-permute-done | bytes 786464 | tf_op jit(solution)/shard_map/ppermute | solution.py:13
  58.7 1.8 %fusion.39 = (bf16[768,1536]{1,0:T(8,128)(2,1)S(1)}, bf16[768,1536]{1,0:T(8,128)(2,1)}) fusion(bf16[768,3072]{1,0:T(8,128)(2,1)S(1)} %constant_dynamic-update-slice_fusion.2), kind=kLoop, calls=%fused_computation.64 | loop fusion | bytes 9437184 | tf_op jit(solution)/shard_map/slice | solution.py:108
  60.5 4.3 %copy.63 = bf16[768,1536]{0,1:T(8,128)(2,1)} copy(bf16[768,1536]{1,0:T(8,128)(2,1)} %get-tuple-element.34) | data formatting | bytes 4718592 | tf_op jit(solution)/shard_map/slice | solution.py:109
  64.7 2.5 %copy.59 = bf16[768,1536]{0,1:T(8,128)(2,1)} copy(bf16[768,1536]{1,0:T(8,128)(2,1)S(1)} %get-tuple-element.33) | data formatting | bytes 4718592 | tf_op jit(solution)/shard_map/slice | solution.py:108
  67.2 3.0 %copy.60 = bf16[768,12,128]{2,0,1:T(8,128)(2,1)S(1)} copy(bf16[768,12,128]{0,2,1:T(8,128)(2,1)} %bitcast.93) | data formatting | bytes 4718592 | tf_op jit(solution)/shard_map/reshape | solution.py:108
  70.2 0.8 fusion.12
  71.0 3.6 %fusion.42 = (f32[12,128]{1,0:T(8,128)S(1)}, f32[12,128,768]{1,2,0:T(8,128)S(1)}) fusion(f32[12,768,128]{2,1,0:T(8,128)S(1)} %fusion.12, f32[12,768]{1,0:T(8,128)S(1)} %add_select_fusion), kind=kOutput, calls=%fused_computation.67 | output fusion | flops 7078655 | bytes 9480192 | tf_op jit(solution)/shard_map/sub | solution.py:41
  74.6 0.5 fusion.18
  75.1 0.8 copy-done.2
  75.9 2.9 %fusion.34 = f32[12,768,128]{1,2,0:T(8,128)} fusion(bf16[12,128,768]{1,2,0:T(8,128)(2,1)S(1)} %fusion.18, bf16[128,12,128]{0,2,1:T(8,128)(2,1)S(1)} %copy-done.2), kind=kOutput, calls=%fused_computation.45 | convolution fusion | flops 301989888 | bytes 7471104 | tf_op jit(solution)/shard_map/hqk,hqd->hkd/dot_general | solution.py:46
  78.8 0.1 copy-done.1
  78.9 0.8 fusion.23
  79.7 4.3 %copy.64 = bf16[768,12,128]{2,0,1:T(8,128)(2,1)} copy(bf16[768,12,128]{0,2,1:T(8,128)(2,1)} %bitcast.91) | data formatting | bytes 4718592 | tf_op jit(solution)/shard_map/reshape | solution.py:109
  83.9 4.1 %fusion.3 = bf16[12,128,768]{1,2,0:T(8,128)(2,1)S(1)} fusion(f32[12,128]{1,0:T(8,128)S(1)} %fusion.23, bf16[768,12,128]{2,0,1:T(8,128)(2,1)} %copy.64, f32[12,128,768]{1,2,0:T(8,128)} %copy-done, f32[12,128]{1,0:T(8,128)S(1)} %get-tuple-element.39, bf16[12,128,128]{2,0,1:T(8,128)(2,1)S(1)} %bitcast.95), kind=kOutput, calls=%fused_computation.11 | convolution fusion | flops 307888128 | bytes 9842688 | tf_op jit(solution)/shard_map/hqd,hkd->hqk/dot_general | solution.py:47
  88.1 0.8 fusion.24
  88.9 3.0 %fusion.43 = f32[12,768,128]{1,2,0:T(8,128)} fusion(bf16[12,128,768]{1,2,0:T(8,128)(2,1)S(1)} %fusion.3, bf16[12,128,128]{1,2,0:T(8,128)(2,1)S(1)} %copy.72), kind=kOutput, calls=%fused_computation.68 | convolution fusion | flops 301989888 | bytes 7471104 | tf_op jit(solution)/shard_map/hqk,hqd->hkd/dot_general | solution.py:50
  92.0 6.1 %copy.75 = f32[768,1536]{1,0:T(8,128)} copy(f32[768,1536]{0,1:T(8,128)} %bitcast.88) | data formatting | bytes 9437184 | tf_op jit(solution)/shard_map/reshape | solution.py:114
  98.1 6.1 %copy.74 = f32[768,1536]{1,0:T(8,128)} copy(f32[768,1536]{0,1:T(8,128)} %bitcast.89) | data formatting | bytes 9437184 | tf_op jit(solution)/shard_map/reshape | solution.py:114
  104.2 6.8 %fusion.1 = bf16[768,3072]{1,0:T(8,128)(2,1)} fusion(f32[768,1536]{1,0:T(8,128)} %copy.75, f32[768,1536]{1,0:T(8,128)} %copy.74), kind=kLoop, calls=%fused_computation.8 | loop fusion | flops 9437184 | bytes 14155776 | tf_op jit(solution)/shard_map/convert.5
  111.0 1.2 fusion.32
  112.2 0.3 copy.70
  112.5 1.0 convert_element_type.76
  113.5 2.2 %fusion.38 = (bf16[128,3072]{1,0:T(8,128)(2,1)S(1)}, bf16[128,3072]{1,0:T(8,128)(2,1)S(1)}, bf16[128,3072]{1,0:T(8,128)(2,1)S(1)}, bf16[128,3072]{1,0:T(8,128)(2,1)S(1)}) fusion(bf16[768,3072]{1,0:T(8,128)(2,1)} %fusion.1), kind=kLoop, calls=%fused_computation.63 | loop fusion | bytes 6291456 | tf_op jit(solution)/shard_map/slice | solution.py:129
  115.7 0.4 collective-permute-start.11
  116.1 1.2 collective-permute-start.10
  117.3 3.0 %collective-permute-start.9 = (bf16[1,2,64,3072]{3,2,1,0:T(8,128)(2,1)S(1)}, bf16[1,2,64,3072]{3,2,1,0:T(8,128)(2,1)S(1)}, u32[]{:S(2)}, u32[]{:S(2)}) collective-permute-start(bf16[1,2,64,3072]{3,2,1,0:T(8,128)(2,1)S(1)} %bitcast.102), channel_id=1, source_target_pairs={{4,0},{8,4},{12,8},{16,12},{20,16},{24,20},{28,24},{0,28},{5,1},{9... | collective-permute-start | bytes 2359304 | tf_op jit(solution)/shard_map/ppermute | solution.py:13
  120.3 3.2 %collective-permute-start.7 = (bf16[1,1,64,3072]{3,2,1,0:T(8,128)(2,1)S(1)}, bf16[1,1,64,3072]{3,2,1,0:T(8,128)(2,1)S(1)}, u32[]{:S(2)}, u32[]{:S(2)}) collective-permute-start(bf16[1,1,64,3072]{3,2,1,0:T(8,128)(2,1)S(1)} %bitcast.99), channel_id=1, source_target_pairs={{1,0},{2,1},{3,2},{5,4},{6,5},{7,6},{9,8},{10,9},{11,10},{13,12},{... | collective-permute-start | bytes 1179656 | tf_op jit(solution)/shard_map/ppermute | solution.py:24
  123.5 3.0 %collective-permute-start.6 = (bf16[1,1,64,3072]{3,2,1,0:T(8,128)(2,1)S(1)}, bf16[1,1,64,3072]{3,2,1,0:T(8,128)(2,1)S(1)}, u32[]{:S(2)}, u32[]{:S(2)}) collective-permute-start(bf16[1,1,64,3072]{3,2,1,0:T(8,128)(2,1)S(1)} %bitcast.97), channel_id=1, source_target_pairs={{0,1},{1,2},{2,3},{4,5},{5,6},{6,7},{8,9},{9,10},{10,11},{12,13},{... | collective-permute-start | bytes 1179656 | tf_op jit(solution)/shard_map/ppermute | solution.py:23
  126.6 0.1 maximum_bitcast_fusion
  126.7 1.2 fusion.19
  127.9 2.5 %collective-permute-done.7 = bf16[1,1,64,3072]{3,2,1,0:T(8,128)(2,1)S(1)} collective-permute-done((bf16[1,1,64,3072]{3,2,1,0:T(8,128)(2,1)S(1)}, bf16[1,1,64,3072]{3,2,1,0:T(8,128)(2,1)S(1)}, u32[]{:S(2)}, u32[]{:S(2)}) %collective-permute-start.7) | collective-permute-done | bytes 393248 | tf_op jit(solution)/shard_map/ppermute | solution.py:24
  130.4 2.8 %collective-permute-start.8 = (bf16[1,2,64,3072]{3,2,1,0:T(8,128)(2,1)S(1)}, bf16[1,2,64,3072]{3,2,1,0:T(8,128)(2,1)S(1)}, u32[]{:S(2)}, u32[]{:S(2)}) collective-permute-start(bf16[1,2,64,3072]{3,2,1,0:T(8,128)(2,1)S(1)} %bitcast.101), channel_id=1, source_target_pairs={{8,0},{12,4},{16,8},{20,12},{24,16},{28,20},{0,24},{4,28},{9,1},{1... | collective-permute-start | bytes 2359304 | tf_op jit(solution)/shard_map/ppermute | solution.py:13
  133.2 0.2 fusion.30
  133.4 0.2 fusion.29
  133.6 1.0 collective-permute-done.11
  134.6 19.3 %collective-permute-done.10 = bf16[1,2,64,3072]{3,2,1,0:T(8,128)(2,1)S(1)} collective-permute-done((bf16[1,2,64,3072]{3,2,1,0:T(8,128)(2,1)S(1)}, bf16[1,2,64,3072]{3,2,1,0:T(8,128)(2,1)S(1)}, u32[]{:S(2)}, u32[]{:S(2)}) %collective-permute-start.10) | collective-permute-done | bytes 786464 | tf_op jit(solution)/shard_map/ppermute | solution.py:13
  153.9 15.8 %collective-permute-done.8 = bf16[1,2,64,3072]{3,2,1,0:T(8,128)(2,1)S(1)} collective-permute-done((bf16[1,2,64,3072]{3,2,1,0:T(8,128)(2,1)S(1)}, bf16[1,2,64,3072]{3,2,1,0:T(8,128)(2,1)S(1)}, u32[]{:S(2)}, u32[]{:S(2)}) %collective-permute-start.8) | collective-permute-done | bytes 786464 | tf_op jit(solution)/shard_map/ppermute | solution.py:13
  169.7 0.6 add_convert_fusion
  170.3 0.9 fusion.40
  (28 shorter events, 0.2 us)
Async XLA Ops:
  2.7 27.9 %collective-permute-start.2 = (bf16[1,2,64,3072]{3,2,1,0:T(8,128)(2,1)S(1)}, bf16[1,2,64,3072]{3,2,1,0:T(8,128)(2,1)}, u32[]{:S(2)}, u32[]{:S(2)}) collective-permute-start(bf16[1,2,64,3072]{3,2,1,0:T(8,128)(2,1)S(1)} %constant_dynamic-update-slice_fusion), channel_id=1, source_target_pairs={{24,0},{28,4},{0,8},{4,12},{8,16},{12,20},{16,24},{20,28},{25,1},{... | collective-permute-start | bytes 2359304 | tf_op jit(solution)/shard_map/ppermute | solution.py:13
  4.9 37.0 %collective-permute-start.3 = (bf16[1,2,64,3072]{3,2,1,0:T(8,128)(2,1)S(1)}, bf16[1,2,64,3072]{3,2,1,0:T(8,128)(2,1)}, u32[]{:S(2)}, u32[]{:S(2)}) collective-permute-start(bf16[1,2,64,3072]{3,2,1,0:T(8,128)(2,1)S(1)} %constant_dynamic-update-slice_fusion), channel_id=1, source_target_pairs={{28,0},{0,4},{4,8},{8,12},{12,16},{16,20},{20,24},{24,28},{29,1},{... | collective-permute-start | bytes 2359304 | tf_op jit(solution)/shard_map/ppermute | solution.py:13
  6.1 37.0 %collective-permute-start.4 = (bf16[1,2,64,3072]{3,2,1,0:T(8,128)(2,1)S(1)}, bf16[1,2,64,3072]{3,2,1,0:T(8,128)(2,1)}, u32[]{:S(2)}, u32[]{:S(2)}) collective-permute-start(bf16[1,2,64,3072]{3,2,1,0:T(8,128)(2,1)S(1)} %constant_dynamic-update-slice_fusion), channel_id=1, source_target_pairs={{4,0},{8,4},{12,8},{16,12},{20,16},{24,20},{28,24},{0,28},{5,1},{9... | collective-permute-start | bytes 2359304 | tf_op jit(solution)/shard_map/ppermute | solution.py:13
  9.1 49.6 %collective-permute-start.5 = (bf16[1,2,64,3072]{3,2,1,0:T(8,128)(2,1)S(1)}, bf16[1,2,64,3072]{3,2,1,0:T(8,128)(2,1)S(1)}, u32[]{:S(2)}, u32[]{:S(2)}) collective-permute-start(bf16[1,2,64,3072]{3,2,1,0:T(8,128)(2,1)S(1)} %constant_dynamic-update-slice_fusion), channel_id=1, source_target_pairs={{8,0},{12,4},{16,8},{20,12},{24,16},{28,20},{0,24},{4,28},{9,1},{1... | collective-permute-start | bytes 2359304 | tf_op jit(solution)/shard_map/ppermute | solution.py:13
  10.3 10.6 %collective-permute-start = (bf16[1,1,64,3072]{3,2,1,0:T(8,128)(2,1)}, bf16[1,1,64,3072]{3,2,1,0:T(8,128)(2,1)}, u32[]{:S(2)}, u32[]{:S(2)}) collective-permute-start(bf16[1,1,64,3072]{3,2,1,0:T(8,128)(2,1)} %get-tuple-element.38), channel_id=1, source_target_pairs={{0,1},{1,2},{2,3},{4,5},{5,6},{6,7},{8,9},{9,10},{10,11},{12,13},{... | collective-permute-start | bytes 1179656 | tf_op jit(solution)/shard_map/ppermute | solution.py:23
  20.9 9.7 %collective-permute-start.1 = (bf16[1,1,64,3072]{3,2,1,0:T(8,128)(2,1)}, bf16[1,1,64,3072]{3,2,1,0:T(8,128)(2,1)S(1)}, u32[]{:S(2)}, u32[]{:S(2)}) collective-permute-start(bf16[1,1,64,3072]{3,2,1,0:T(8,128)(2,1)} %get-tuple-element.37), channel_id=1, source_target_pairs={{1,0},{2,1},{3,2},{5,4},{6,5},{7,6},{9,8},{10,9},{11,10},{13,12},{... | collective-permute-start | bytes 1179656 | tf_op jit(solution)/shard_map/ppermute | solution.py:24
  74.6 4.2 %copy-start = (f32[12,128,768]{1,2,0:T(8,128)}, f32[12,128,768]{1,2,0:T(8,128)S(1)}, u32[]{:S(2)}) copy-start(f32[12,128,768]{1,2,0:T(8,128)S(1)} %get-tuple-element.40) | copy-start | bytes 14155780
  74.6 1.3 copy-start.2
  75.9 3.0 %copy-start.1 = (bf16[768,1536]{0,1:T(8,128)(2,1)S(1)}, bf16[768,1536]{0,1:T(8,128)(2,1)}, u32[]{:S(2)}) copy-start(bf16[768,1536]{0,1:T(8,128)(2,1)} %copy.63) | copy-start | bytes 7077892
  98.1 12.9 %slice-start = ((s8[4718592]{0:T(1024)(128)(4,1)}), s8[524288]{0:T(1024)(128)(4,1)S(1)}, s32[]{:S(2)}) async-start(s8[4718592]{0:T(1024)(128)(4,1)} %bitcast.84), calls=%async_computation | async-start | bytes 1048576
  104.2 6.8 %slice-start.1 = ((s8[4718592]{0:T(1024)(128)(4,1)}), s8[4194304]{0:T(1024)(128)(4,1)S(1)}, s32[]{:S(2)}) async-start(s8[4718592]{0:T(1024)(128)(4,1)} %bitcast.84), calls=%async_computation.1 | async-start | bytes 8388608
  112.2 14.4 %slice-start.2 = ((s8[4718592]{0:T(1024)(128)(4,1)}), s8[524288]{0:T(1024)(128)(4,1)S(1)}, s32[]{:S(2)}) async-start(s8[4718592]{0:T(1024)(128)(4,1)} %bitcast.86), calls=%async_computation.2 | async-start | bytes 1048576
  113.5 13.1 %slice-start.3 = ((s8[4718592]{0:T(1024)(128)(4,1)}), s8[4194304]{0:T(1024)(128)(4,1)S(1)}, s32[]{:S(2)}) async-start(s8[4718592]{0:T(1024)(128)(4,1)} %bitcast.86), calls=%async_computation.3 | async-start | bytes 8388608
  115.7 18.9 %collective-permute-start.11 = (bf16[1,2,64,3072]{3,2,1,0:T(8,128)(2,1)S(1)}, bf16[1,2,64,3072]{3,2,1,0:T(8,128)(2,1)S(1)}, u32[]{:S(2)}, u32[]{:S(2)}) collective-permute-start(bf16[1,2,64,3072]{3,2,1,0:T(8,128)(2,1)S(1)} %bitcast.104), channel_id=1, source_target_pairs={{24,0},{28,4},{0,8},{4,12},{8,16},{12,20},{16,24},{20,28},{25,1},{... | collective-permute-start | bytes 2359304 | tf_op jit(solution)/shard_map/ppermute | solution.py:13
  116.1 37.8 %collective-permute-start.10 = (bf16[1,2,64,3072]{3,2,1,0:T(8,128)(2,1)S(1)}, bf16[1,2,64,3072]{3,2,1,0:T(8,128)(2,1)S(1)}, u32[]{:S(2)}, u32[]{:S(2)}) collective-permute-start(bf16[1,2,64,3072]{3,2,1,0:T(8,128)(2,1)S(1)} %bitcast.103), channel_id=1, source_target_pairs={{28,0},{0,4},{4,8},{8,12},{12,16},{16,20},{20,24},{24,28},{29,1},{... | collective-permute-start | bytes 2359304 | tf_op jit(solution)/shard_map/ppermute | solution.py:13
  117.3 36.6 %collective-permute-start.9 = (bf16[1,2,64,3072]{3,2,1,0:T(8,128)(2,1)S(1)}, bf16[1,2,64,3072]{3,2,1,0:T(8,128)(2,1)S(1)}, u32[]{:S(2)}, u32[]{:S(2)}) collective-permute-start(bf16[1,2,64,3072]{3,2,1,0:T(8,128)(2,1)S(1)} %bitcast.102), channel_id=1, source_target_pairs={{4,0},{8,4},{12,8},{16,12},{20,16},{24,20},{28,24},{0,28},{5,1},{9... | collective-permute-start | bytes 2359304 | tf_op jit(solution)/shard_map/ppermute | solution.py:13
  120.3 10.1 %collective-permute-start.7 = (bf16[1,1,64,3072]{3,2,1,0:T(8,128)(2,1)S(1)}, bf16[1,1,64,3072]{3,2,1,0:T(8,128)(2,1)S(1)}, u32[]{:S(2)}, u32[]{:S(2)}) collective-permute-start(bf16[1,1,64,3072]{3,2,1,0:T(8,128)(2,1)S(1)} %bitcast.99), channel_id=1, source_target_pairs={{1,0},{2,1},{3,2},{5,4},{6,5},{7,6},{9,8},{10,9},{11,10},{13,12},{... | collective-permute-start | bytes 1179656 | tf_op jit(solution)/shard_map/ppermute | solution.py:24
  123.5 9.7 %collective-permute-start.6 = (bf16[1,1,64,3072]{3,2,1,0:T(8,128)(2,1)S(1)}, bf16[1,1,64,3072]{3,2,1,0:T(8,128)(2,1)S(1)}, u32[]{:S(2)}, u32[]{:S(2)}) collective-permute-start(bf16[1,1,64,3072]{3,2,1,0:T(8,128)(2,1)S(1)} %bitcast.97), channel_id=1, source_target_pairs={{0,1},{1,2},{2,3},{4,5},{5,6},{6,7},{8,9},{9,10},{10,11},{12,13},{... | collective-permute-start | bytes 1179656 | tf_op jit(solution)/shard_map/ppermute | solution.py:23
  130.4 39.3 %collective-permute-start.8 = (bf16[1,2,64,3072]{3,2,1,0:T(8,128)(2,1)S(1)}, bf16[1,2,64,3072]{3,2,1,0:T(8,128)(2,1)S(1)}, u32[]{:S(2)}, u32[]{:S(2)}) collective-permute-start(bf16[1,2,64,3072]{3,2,1,0:T(8,128)(2,1)S(1)} %bitcast.101), channel_id=1, source_target_pairs={{8,0},{12,4},{16,8},{20,12},{24,16},{28,20},{0,24},{4,28},{9,1},{1... | collective-permute-start | bytes 2359304 | tf_op jit(solution)/shard_map/ppermute | solution.py:13
where the time goes:
time: 173 us; the launch traced here: 171 us
  waiting for transfers between devices  69.7 us (40%)
  local copies, waits for them, and re-layouts  45.4 us (26%)
  starting transfers between devices  26.9 us (16%)
  other arithmetic  15.9 us (9%)
  matrix products  12.5 us (7%)
    ppermute x8, waiting for transfers between devices, shifted(): return lax.ppermute(block, axis, route)  60.5 us
    ppermute x8, starting transfers between devices, shifted(): return lax.ppermute(block, axis, route)  14 us
    ppermute x2, waiting for transfers between devices, padded_2(): after = lax.ppermute(first, axis, down)  9.2 us
    another operation x3, other arithmetic  8.61 us
    ppermute x2, starting transfers between devices, padded_2(): before = lax.ppermute(last, axis, up)  7.74 us
    unnamed x23, local copies, waits for them, and re-layouts  6.58 us
    reshape x1, local copies, waits for them, and re-layouts, per_device(): value_grad.reshape(total_keys, width)  6.13 us
    reshape x1, local copies, waits for them, and re-layouts, per_device(): key_grad.reshape(total_keys, width)  6.12 us
  transfers between devices with their start and end apart: 12, of which 7 were waited for; matrix products, arithmetic and copies ran while one was open for 8% of the time, Pallas kernels for 0%

commit v1 on v0

v1 whole, which is shorter than its diff:
```python
import functools

import jax
import jax.numpy as jnp
from jax import lax
from jax.experimental import pallas as pl
from jax.experimental.pallas import tpu as pltpu
from jax.sharding import PartitionSpec as P

HEAD_DIM = 128
REACH = 2
SCALE = HEAD_DIM**-0.5
FAR_AWAY = 3e38
VMEM_BYTES = 40 * 1024 * 1024

NT = (((1,), (1,)), ((), ()))
NN = (((1,), (0,)), ((), ()))
TN = (((0,), (0,)), ((), ()))


def dot(left, right, dims):
    return lax.dot_general(left, right, dims, preferred_element_type=jnp.float32)


def routes(size):
    def keep(move):
        return [(i, move(i)) for i in range(size) if 0 <= move(i) < size]

    partner = keep(lambda i: i ^ 1)
    route_a = keep(lambda i: i - 2 if i % 2 == 0 else i + 2)
    route_b = keep(lambda i: i + 2 if i % 2 == 0 else i - 2)
    outer = keep(lambda i: i - 1 if i % 2 == 0 else i + 1)
    return partner, route_a, route_b, outer


def spread(pair, axis):
    size = lax.axis_size(axis)
    partner, route_a, route_b, outer = routes(size)
    from_partner = lax.ppermute(pair, axis, partner)
    from_b = lax.ppermute(pair, axis, route_b)
    from_a = lax.ppermute(pair, axis, route_a)
    if size % 2 == 0:
        first = lax.ppermute(from_partner[0], axis, route_b)
        second = lax.ppermute(from_a[1], axis, partner)
    else:
        first = lax.ppermute(pair[0], axis, outer)
        second = lax.ppermute(pair[1], axis, outer)
    return from_partner, from_a, from_b, first, second


def query_kernel(
    n_tm, n_height, query, grad, own, face_1, face_2, part, a, b, outer_k, outer_v, picks,
    grad_query, own_grads, face_1_grads, face_2_grads, to_part, to_a, to_b, to_outer,
):
    heads = query.shape[1] // HEAD_DIM
    tile, face = query.shape[0], face_1.shape[1]
    at, line = lax.axis_index("tm"), lax.axis_index("height")
    odd, line_odd = lax.rem(at, 2), lax.rem(line, 2)
    slot_part, slot_a, slot_b, slot_outer = 2 - odd, 3 - 3 * odd, 3 * odd, 1 + odd
    slots = (slot_part, slot_a, slot_b, slot_outer)

    def target(slot):
        return at + slot - jnp.where(slot < REACH, REACH, REACH - 1)

    inside = [(target(s) >= 0) & (target(s) < n_tm) for s in slots]
    face_1_ok = (line_odd == 1) | (line + 1 < n_height)
    face_2_ok = jnp.where(line_odd == 1, line + 1 < n_height, line > 0)

    def head(e, carry):
        cols = pl.ds(pl.multiple_of(e * HEAD_DIM, HEAD_DIM), HEAD_DIM)
        q, g = query[:, cols], grad[:, cols]
        keys = [own[0, :, cols], face_1[0, :, cols], face_2[0, :, cols],
                part[0, :, cols], a[0, :, cols], b[0, :, cols], outer_k[:, cols]]
        values = [own[1, :, cols], face_1[1, :, cols], face_2[1, :, cols],
                  part[1, :, cols], a[1, :, cols], b[1, :, cols], outer_v[:, cols]]
        chosen = [ok & ((picks[e, 0] == s) | (picks[e, 1] == s)) for s, ok in zip(slots, inside)]
        present = [None, face_1_ok, face_2_ok] + chosen
        scores = []
        for k, ok in zip(keys, present):
            s = dot(k, q, NT) * SCALE
            scores.append(s if ok is None else s + jnp.where(ok, 0.0, -jnp.inf))
        top = functools.reduce(jnp.maximum, [jnp.max(s, axis=0, keepdims=True) for s in scores])
        expo = [jnp.exp(s - top) for s in scores]
        total = functools.reduce(jnp.add, [jnp.sum(x, axis=0, keepdims=True) for x in expo])
        inverse = 1.0 / total
        weights = [x * inverse for x in expo]
        weights_b = [w.astype(jnp.bfloat16) for w in weights]
        grad_weights = [dot(v, g, NT) for v in values]
        delta = functools.reduce(
            jnp.add,
            [jnp.sum(w.astype(jnp.float32) * x, axis=0, keepdims=True) for w, x in zip(weights_b, grad_weights)],
        )
        dscore = [(w * (x - delta) * SCALE).astype(jnp.bfloat16) for w, x in zip(weights, grad_weights)]
        dq = functools.reduce(jnp.add, [dot(d, k, TN) for d, k in zip(dscore, keys)])
        grad_query[:, cols] = dq.astype(grad_query.dtype)
        own_grads[0, :, cols] = dot(dscore[0], q, NN)
        own_grads[1, :, cols] = dot(weights_b[0], g, NN)
        for out, at_key in ((face_1_grads, 1), (face_2_grads, 2)):
            out[0, :, cols] = dot(dscore[at_key], q, NN).astype(out.dtype)
            out[1, :, cols] = dot(weights_b[at_key], g, NN).astype(out.dtype)
        level = top + jnp.log(total)
        for out, ok in ((to_part, chosen[0]), (to_a, chosen[2]), (to_b, chosen[1]), (to_outer, chosen[3])):
            out[pl.ds(e, 1), :] = jnp.where(ok, level, FAR_AWAY)
            out[pl.ds(e + heads, 1), :] = delta
        return carry

    lax.fori_loop(0, heads, head, 0, unroll=False)


def key_kernel(
    keys, own_grads, face_1_grads, face_2_grads, part, a, b, outer_q, outer_g,
    of_part, of_a, of_b, of_outer, grad_key, grad_value,
):
    heads = keys.shape[2] // HEAD_DIM
    tile, face = keys.shape[1], face_1_grads.shape[1]
    last_first = lax.rem(lax.axis_index("height"), 2) == 0

    def head(e, carry):
        cols = pl.ds(pl.multiple_of(e * HEAD_DIM, HEAD_DIM), HEAD_DIM)
        k, v = keys[0, :, cols], keys[1, :, cols]
        sums = [own_grads[0, :, cols], own_grads[1, :, cols]]
        pairs = [(r[0, :, cols], r[1, :, cols], s) for r, s in ((part, of_part), (a, of_a), (b, of_b))]
        pairs.append((outer_q[:, cols], outer_g[:, cols], of_outer))
        for q, g, stats in pairs:
            level, delta = stats[pl.ds(e, 1), :], stats[pl.ds(e + heads, 1), :]
            weights = jnp.exp(dot(k, q, NT) * SCALE - level)
            grad_weights = dot(v, g, NT)
            dscore = (weights * (grad_weights - delta) * SCALE).astype(jnp.bfloat16)
            sums[0] += dot(dscore, q, NN).astype(jnp.bfloat16).astype(jnp.float32)
            sums[1] += dot(weights.astype(jnp.bfloat16), g, NN).astype(jnp.bfloat16).astype(jnp.float32)
        for at, out in ((0, grad_key), (1, grad_value)):
            one = face_1_grads[at, :, cols].astype(jnp.float32)
            two = face_2_grads[at, :, cols].astype(jnp.float32)
            first = jnp.where(last_first, two, one)
            last = jnp.where(last_first, one, two)
            out[:face, cols] = (sums[at][:face] + first).astype(out.dtype)
            out[face:, cols] = (sums[at][face:] + last).astype(out.dtype)
        return carry

    lax.fori_loop(0, heads, head, 0, unroll=False)


def per_device(query_tok, key_tok, value_tok, grad_out, far_picks):
    frames_dev, rows_dev, columns, width = query_tok.shape
    tile, face = frames_dev * rows_dev * columns, frames_dev * columns
    heads = width // HEAD_DIM
    n_tm, n_height = lax.axis_size("tm"), lax.axis_size("height")
    query, key = query_tok.reshape(tile, width), key_tok.reshape(tile, width)
    value, grad = value_tok.reshape(tile, width), grad_out.reshape(tile, width)
    key_value = jnp.stack([key, value])
    query_grad = jnp.stack([query, grad])
    line_odd = lax.rem(lax.axis_index("height"), 2)
    rows = key_value.reshape(2, rows_dev, face, width)
    pairs_1 = [(i, i ^ 1) for i in range(n_height) if i ^ 1 < n_height]
    pairs_2 = [(i, i - 1 if i % 2 == 0 else i + 1) for i in range(n_height)]
    pairs_2 = [(i, j) for i, j in pairs_2 if 0 <= j < n_height]
    first_row, last_row = rows[:, 0], rows[:, rows_dev - 1]
    face_1 = lax.ppermute(jnp.where(line_odd == 0, last_row, first_row), "height", pairs_1)
    face_2 = lax.ppermute(jnp.where(line_odd == 0, first_row, last_row), "height", pairs_2)
    kv_part, kv_a, kv_b, outer_k, outer_v = spread(key_value, "tm")
    qg_part, qg_a, qg_b, outer_q, outer_g = spread(query_grad, "tm")

    f32, bf16 = jnp.float32, jnp.bfloat16
    vmem = pl.BlockSpec(memory_space=pltpu.VMEM)
    stats = jax.ShapeDtypeStruct((2 * heads, tile), f32)
    block = 2 * tile * tile * HEAD_DIM * heads
    grad_query, own_grads, face_1_grads, face_2_grads, to_part, to_a, to_b, to_outer = pl.pallas_call(
        functools.partial(query_kernel, n_tm, n_height),
        out_shape=(
            jax.ShapeDtypeStruct((tile, width), bf16),
            jax.ShapeDtypeStruct((2, tile, width), f32),
            jax.ShapeDtypeStruct((2, face, width), bf16),
            jax.ShapeDtypeStruct((2, face, width), bf16),
            stats, stats, stats, stats,
        ),
        in_specs=[vmem] * 10 + [pl.BlockSpec(memory_space=pltpu.SMEM)],
        out_specs=[vmem] * 8,
        compiler_params=pltpu.CompilerParams(vmem_limit_bytes=VMEM_BYTES),
        cost_estimate=pl.CostEstimate(flops=22 * block, bytes_accessed=8 << 20, transcendentals=0),
        name="query_side",
    )(query, grad, key_value, face_1, face_2, kv_part, kv_a, kv_b, outer_k, outer_v,
      far_picks.reshape(heads, far_picks.shape[3]))

    partner, route_a, route_b, outer = routes(n_tm)
    of_part = lax.ppermute(to_part, "tm", partner)
    of_a = lax.ppermute(to_a, "tm", route_a)
    of_b = lax.ppermute(to_b, "tm", route_b)
    of_outer = lax.ppermute(to_outer, "tm", outer)
    back_1 = lax.ppermute(face_1_grads, "height", pairs_1)
    back_2 = lax.ppermute(face_2_grads, "height", pairs_2)

    grad_key, grad_value = pl.pallas_call(
        key_kernel,
        out_shape=(jax.ShapeDtypeStruct((tile, width), bf16),) * 2,
        in_specs=[vmem] * 13,
        out_specs=[vmem] * 2,
        compiler_params=pltpu.CompilerParams(vmem_limit_bytes=VMEM_BYTES),
        cost_estimate=pl.CostEstimate(flops=16 * block, bytes_accessed=8 << 20, transcendentals=0),
        name="key_side",
    )(key_value, own_grads, back_1, back_2, qg_part, qg_a, qg_b, outer_q, outer_g,
      of_part, of_a, of_b, of_outer)
    return tuple(x.reshape(query_tok.shape) for x in (grad_query, grad_key, grad_value))


def solution(mesh):
    spec = P("tm", "height", None, None)
    return jax.shard_map(
        per_device, mesh=mesh, in_specs=(spec,) * 5, out_specs=(spec,) * 3, check_vma=False
    )
```

time: 173 us -> 95 us (0.55)
  the two profiles are of different devices: /device:TPU:1 before, /device:TPU:22 now
where the time goes in v1:
time: 95 us; the launch traced here: 94.5 us
  starting transfers between devices  35.2 us (37%)
  waiting for transfers between devices  30.2 us (32%)
  Pallas kernels  23.3 us (25%)
  other arithmetic  3.65 us (4%)
  local copies, waits for them, and re-layouts  1.22 us (1%)
    ppermute x2, waiting for transfers between devices, spread(): from_partner = lax.ppermute(pair, axis, partner)  19.2 us
    pallas_call x1, Pallas kernels, per_device(): pl.pallas_call(functools.partial(query_kernel, n_tm, n_height), out_shape...  12.4 us
    pallas_call x1, Pallas kernels, per_device(): pl.pallas_call(key_kernel, out_shape=(jax.ShapeDtypeStruct((tile, width),...  11 us
    ppermute x2, starting transfers between devices, spread(): from_a = lax.ppermute(pair, axis, route_a)  5.49 us
    ppermute x2, starting transfers between devices, spread(): from_b = lax.ppermute(pair, axis, route_b)  4.7 us
    ppermute x2, starting transfers between devices, spread(): first = lax.ppermute(from_partner[0], axis, route_b)  4.7 us
    ppermute x1, waiting for transfers between devices, per_device(): of_outer = lax.ppermute(to_outer, 'tm', outer)  4.54 us
    ppermute x1, starting transfers between devices, per_device(): of_b = lax.ppermute(to_b, 'tm', route_b)  3.7 us
  transfers between devices with their start and end apart: 18, of which 7 were waited for; matrix products, arithmetic and copies ran while one was open for 4% of the time, Pallas kernels for 13%

profile of v1, /device:TPU:22, one launch (start us, length us, event | category | flops | bytes accessed | tf_op | source)
XLA Modules:
  0.0 94.5 jit_solution(9944993824912866760)
XLA Ops:
  0.6 0.0 copy-start.1
  0.6 0.0 copy-start
  0.7 0.0 copy-start.3
  0.7 1.3 %pad_maximum_fusion.own.keys = bf16[2,128,1536]{2,1,0:T(8,128)(2,1)S(1)} fusion(bf16[1,128,1536]{2,1,0:T(8,128)(2,1)} %bitcast.28, bf16[1,128,1536]{2,1,0:T(8,128)(2,1)} %bitcast.30), kind=kLoop, calls=%fused_computation | loop fusion | flops 393216 | bytes 1572864 | tf_op jit(solution)/shard_map/stack | solution.py:150
  1.9 0.6 collective-permute-start.2
  2.5 3.5 %collective-permute-start.3 = (bf16[2,128,1536]{2,1,0:T(8,128)(2,1)S(1)}, bf16[2,128,1536]{2,1,0:T(8,128)(2,1)}, u32[]{:S(2)}, u32[]{:S(2)}) collective-permute-start(bf16[2,128,1536]{2,1,0:T(8,128)(2,1)S(1)} %pad_maximum_fusion.own.keys), channel_id=1, source_target_pairs={{4,12},{8,0},{12,20},{16,8},{20,28},{24,16},{5,13},{9,1},{13,21},{... | collective-permute-start | bytes 2359304 | tf_op jit(solution)/shard_map/ppermute | solution.py:41
  6.0 2.4 %collective-permute-start.4 = (bf16[2,128,1536]{2,1,0:T(8,128)(2,1)S(1)}, bf16[2,128,1536]{2,1,0:T(8,128)(2,1)}, u32[]{:S(2)}, u32[]{:S(2)}) collective-permute-start(bf16[2,128,1536]{2,1,0:T(8,128)(2,1)S(1)} %pad_maximum_fusion.own.keys), channel_id=1, source_target_pairs={{0,8},{8,16},{12,4},{16,24},{20,12},{28,20},{1,9},{9,17},{13,5},{1... | collective-permute-start | bytes 2359304 | tf_op jit(solution)/shard_map/ppermute | solution.py:40
  8.4 0.0 copy-done.1
  8.4 0.0 copy-done
  8.4 1.0 %pad_maximum_fusion.1 = bf16[2,128,1536]{2,1,0:T(8,128)(2,1)} fusion(bf16[1,128,1536]{2,1,0:T(8,128)(2,1)S(1)} %bitcast.26, bf16[1,128,1536]{2,1,0:T(8,128)(2,1)S(1)} %bitcast.24), kind=kLoop, calls=%fused_computation.3 | loop fusion | flops 393216 | bytes 1572864 | tf_op jit(solution)/shard_map/stack | solution.py:151
  9.4 2.4 %collective-permute-start.9 = (bf16[2,128,1536]{2,1,0:T(8,128)(2,1)}, bf16[2,128,1536]{2,1,0:T(8,128)(2,1)S(1)}, u32[]{:S(2)}, u32[]{:S(2)}) collective-permute-start(bf16[2,128,1536]{2,1,0:T(8,128)(2,1)} %pad_maximum_fusion.1), channel_id=1, source_target_pairs={{0,4},{4,0},{8,12},{12,8},{16,20},{20,16},{24,28},{28,24},{1,5},{5... | collective-permute-start | bytes 2359304 | tf_op jit(solution)/shard_map/ppermute | solution.py:39
  11.7 2.0 %collective-permute-start.10 = (bf16[2,128,1536]{2,1,0:T(8,128)(2,1)}, bf16[2,128,1536]{2,1,0:T(8,128)(2,1)S(1)}, u32[]{:S(2)}, u32[]{:S(2)}) collective-permute-start(bf16[2,128,1536]{2,1,0:T(8,128)(2,1)} %pad_maximum_fusion.1), channel_id=1, source_target_pairs={{4,12},{8,0},{12,20},{16,8},{20,28},{24,16},{5,13},{9,1},{13,21},{... | collective-permute-start | bytes 2359304 | tf_op jit(solution)/shard_map/ppermute | solution.py:41
  13.7 0.0 copy-done.3
  13.8 0.1 copy.10.picks
  13.8 1.4 %select_bitcast_fusion = (bf16[2,64,1536]{2,1,0:T(8,128)(2,1)S(1)}, bf16[2,64,1536]{2,1,0:T(8,128)(2,1)S(1)}) fusion(pred[]{:T(512)S(6)} %eq.4, bf16[1,2,64,1536]{3,2,0,1:T(8,128)(2,1)} %bitcast.29, bf16[1,2,64,1536]{3,2,0,1:T(8,128)(2,1)} %bitcast.31), kind=kLoop, calls=%fused_computation.10 | loop fusion | flops 983040 | bytes 1572865 | tf_op jit(solution)/shard_map/jit(_where)/select_n | solution.py:159
  15.3 0.0 copy-start.2
  15.3 7.1 %collective-permute-done.2.part = bf16[2,128,1536]{2,1,0:T(8,128)(2,1)S(1)} collective-permute-done((bf16[2,128,1536]{2,1,0:T(8,128)(2,1)S(1)}, bf16[2,128,1536]{2,1,0:T(8,128)(2,1)S(1)}, u32[]{:S(2)}, u32[]{:S(2)}) %collective-permute-start.2) | collective-permute-done | bytes 786464 | tf_op jit(solution)/shard_map/ppermute | solution.py:39
  22.4 2.3 %collective-permute-start.11 = (bf16[2,128,1536]{2,1,0:T(8,128)(2,1)}, bf16[2,128,1536]{2,1,0:T(8,128)(2,1)S(1)}, u32[]{:S(2)}, u32[]{:S(2)}) collective-permute-start(bf16[2,128,1536]{2,1,0:T(8,128)(2,1)} %pad_maximum_fusion.1), channel_id=1, source_target_pairs={{0,8},{8,16},{12,4},{16,24},{20,12},{28,20},{1,9},{9,17},{13,5},{1... | collective-permute-start | bytes 2359304 | tf_op jit(solution)/shard_map/ppermute | solution.py:40
  24.8 0.2 collective-permute-done.3.a
  25.0 0.0 collective-permute-start
  25.0 1.0 %slice_bitcast_fusion.2 = bf16[128,1536]{1,0:T(8,128)(2,1)S(1)} fusion(bf16[2,128,1536]{2,1,0:T(8,128)(2,1)} %collective-permute-done.3.a), kind=kLoop, calls=%fused_computation.7 | loop fusion | bytes 786432 | tf_op jit(solution)/shard_map/squeeze | solution.py:44
  26.0 12.1 %collective-permute-done.9.part = bf16[2,128,1536]{2,1,0:T(8,128)(2,1)S(1)} collective-permute-done((bf16[2,128,1536]{2,1,0:T(8,128)(2,1)}, bf16[2,128,1536]{2,1,0:T(8,128)(2,1)S(1)}, u32[]{:S(2)}, u32[]{:S(2)}) %collective-permute-start.9) | collective-permute-done | bytes 786464 | tf_op jit(solution)/shard_map/ppermute | solution.py:39
  38.1 1.9 %collective-permute-start.1 = (bf16[2,64,1536]{2,1,0:T(8,128)(2,1)S(1)}, bf16[2,64,1536]{2,1,0:T(8,128)(2,1)S(1)}, u32[]{:S(2)}, u32[]{:S(2)}) collective-permute-start(bf16[2,64,1536]{2,1,0:T(8,128)(2,1)S(1)} %get-tuple-element.23), channel_id=1, source_target_pairs={{1,2},{2,1},{5,6},{6,5},{9,10},{10,9},{13,14},{14,13},{17,18},{18,... | collective-permute-start | bytes 1179656 | tf_op jit(solution)/shard_map/ppermute | solution.py:159
  40.1 0.0 collective-permute-done.face_1
  40.1 2.4 %collective-permute-start.5 = (bf16[128,1536]{1,0:T(8,128)(2,1)S(1)}, bf16[128,1536]{1,0:T(8,128)(2,1)S(1)}, u32[]{:S(2)}, u32[]{:S(2)}) collective-permute-start(bf16[128,1536]{1,0:T(8,128)(2,1)S(1)} %slice_bitcast_fusion.3), channel_id=1, source_target_pairs={{0,8},{8,16},{12,4},{16,24},{20,12},{28,20},{1,9},{9,17},{13,5},{1... | collective-permute-start | bytes 1179656 | tf_op jit(solution)/shard_map/ppermute | solution.py:43
  42.5 0.0 collective-permute-done.10.a
  42.5 1.7 %collective-permute-start.6 = (bf16[128,1536]{1,0:T(8,128)(2,1)S(1)}, bf16[128,1536]{1,0:T(8,128)(2,1)S(1)}, u32[]{:S(2)}, u32[]{:S(2)}) collective-permute-start(bf16[128,1536]{1,0:T(8,128)(2,1)S(1)} %slice_bitcast_fusion.2), channel_id=1, source_target_pairs={{0,4},{4,0},{8,12},{12,8},{16,20},{20,16},{24,28},{28,24},{1,5},{5... | collective-permute-start | bytes 1179656 | tf_op jit(solution)/shard_map/ppermute | solution.py:44
  44.2 3.0 %collective-permute-done.1.face_2 = bf16[2,64,1536]{2,1,0:T(8,128)(2,1)S(1)} collective-permute-done((bf16[2,64,1536]{2,1,0:T(8,128)(2,1)S(1)}, bf16[2,64,1536]{2,1,0:T(8,128)(2,1)S(1)}, u32[]{:S(2)}, u32[]{:S(2)}) %collective-permute-start.1) | collective-permute-done | bytes 393248 | tf_op jit(solution)/shard_map/ppermute | solution.py:159
  47.2 2.3 %collective-permute-start.12 = (bf16[128,1536]{1,0:T(8,128)(2,1)S(1)}, bf16[128,1536]{1,0:T(8,128)(2,1)S(1)}, u32[]{:S(2)}, u32[]{:S(2)}) collective-permute-start(bf16[128,1536]{1,0:T(8,128)(2,1)S(1)} %slice_bitcast_fusion.1), channel_id=1, source_target_pairs={{0,8},{8,16},{12,4},{16,24},{20,12},{28,20},{1,9},{9,17},{13,5},{1... | collective-permute-start | bytes 1179656 | tf_op jit(solution)/shard_map/ppermute | solution.py:43
  49.6 0.0 collective-permute-done.4.b
  49.6 1.7 %collective-permute-start.13 = (bf16[128,1536]{1,0:T(8,128)(2,1)S(1)}, bf16[128,1536]{1,0:T(8,128)(2,1)S(1)}, u32[]{:S(2)}, u32[]{:S(2)}) collective-permute-start(bf16[128,1536]{1,0:T(8,128)(2,1)S(1)} %slice_bitcast_fusion), channel_id=1, source_target_pairs={{0,4},{4,0},{8,12},{12,8},{16,20},{20,16},{24,28},{28,24},{1,5},{5... | collective-permute-start | bytes 1179656 | tf_op jit(solution)/shard_map/ppermute | solution.py:44
  51.3 2.7 %collective-permute-done.5.outer_k = bf16[128,1536]{1,0:T(8,128)(2,1)S(1)} collective-permute-done((bf16[128,1536]{1,0:T(8,128)(2,1)S(1)}, bf16[128,1536]{1,0:T(8,128)(2,1)S(1)}, u32[]{:S(2)}, u32[]{:S(2)}) %collective-permute-start.5) | collective-permute-done | bytes 393248 | tf_op jit(solution)/shard_map/ppermute | solution.py:43
  54.0 0.5 collective-permute-done.6.outer_v
  54.6 0.0 copy-done.2
  54.6 12.4 %query_side.1 = (bf16[128,1536]{1,0:T(8,128)(2,1)}, f32[2,128,1536]{2,1,0:T(8,128)S(1)}, bf16[2,64,1536]{2,1,0:T(8,128)(2,1)S(1)}, bf16[2,64,1536]{2,1,0:T(8,128...) custom-call(bf16[128,1536]{1,0:T(8,128)(2,1)S(1)} %bitcast.25, ...), custom_call_target="tpu_custom_call" | custom-call | flops 1107296256 | bytes 8388608 | tf_op jit(solution)/shard_map/query_side/pallas_call | solution.py:167
  66.9 0.0 collective-permute-start.7
  66.9 2.5 %collective-permute-start.8 = (bf16[2,64,1536]{2,1,0:T(8,128)(2,1)S(1)}, bf16[2,64,1536]{2,1,0:T(8,128)(2,1)S(1)}, u32[]{:S(2)}, u32[]{:S(2)}) collective-permute-start(bf16[2,64,1536]{2,1,0:T(8,128)(2,1)S(1)} %get-tuple-element.16), channel_id=1, source_target_pairs={{1,2},{2,1},{5,6},{6,5},{9,10},{10,9},{13,14},{14,13},{17,18},{18,... | collective-permute-start | bytes 1179656 | tf_op jit(solution)/shard_map/ppermute | solution.py:190
  69.4 0.0 collective-permute-done.11.b
  69.5 1.7 %collective-permute-start.14 = (f32[24,128]{1,0:T(8,128)S(1)}, f32[24,128]{1,0:T(8,128)S(1)}, u32[]{:S(2)}, u32[]{:S(2)}) collective-permute-start(f32[24,128]{1,0:T(8,128)S(1)} %get-tuple-element.17), channel_id=1, source_target_pairs={{0,4},{4,0},{8,12},{12,8},{16,20},{20,16},{24,28},{28,24},{1,5},{5... | collective-permute-start | bytes 36872 | tf_op jit(solution)/shard_map/ppermute | solution.py:185
  71.2 0.0 collective-permute-done.12.outer_q
  71.2 2.1 %collective-permute-start.15 = (f32[24,128]{1,0:T(8,128)S(1)}, f32[24,128]{1,0:T(8,128)S(1)}, u32[]{:S(2)}, u32[]{:S(2)}) collective-permute-start(f32[24,128]{1,0:T(8,128)S(1)} %get-tuple-element.18), channel_id=1, source_target_pairs={{4,12},{8,0},{12,20},{16,8},{20,28},{24,16},{5,13},{9,1},{13,21},{... | collective-permute-start | bytes 36872 | tf_op jit(solution)/shard_map/ppermute | solution.py:186
  73.3 0.0 collective-permute-done.13.outer_g
  73.3 3.7 %collective-permute-start.16 = (f32[24,128]{1,0:T(8,128)S(1)}, f32[24,128]{1,0:T(8,128)S(1)}, u32[]{:S(2)}, u32[]{:S(2)}) collective-permute-start(f32[24,128]{1,0:T(8,128)S(1)} %get-tuple-element.19), channel_id=1, source_target_pairs={{0,8},{8,16},{12,4},{16,24},{20,12},{28,20},{1,9},{9,17},{13,5},{1... | collective-permute-start | bytes 36872 | tf_op jit(solution)/shard_map/ppermute | solution.py:187
  77.0 0.0 collective-permute-done.14.of_part
  77.1 1.9 %collective-permute-start.17 = (f32[24,128]{1,0:T(8,128)S(1)}, f32[24,128]{1,0:T(8,128)S(1)}, u32[]{:S(2)}, u32[]{:S(2)}) collective-permute-start(f32[24,128]{1,0:T(8,128)S(1)} %get-tuple-element.20), channel_id=1, source_target_pairs={{4,8},{8,4},{12,16},{16,12},{20,24},{24,20},{5,9},{9,5},{13,17},{1... | collective-permute-start | bytes 36872 | tf_op jit(solution)/shard_map/ppermute | solution.py:188
  79.0 0.0 collective-permute-done.15.of_a
  79.0 0.0 collective-permute-done.16.of_b
  79.0 4.5 %collective-permute-done.17.of_outer = f32[24,128]{1,0:T(8,128)S(1)} collective-permute-done((f32[24,128]{1,0:T(8,128)S(1)}, f32[24,128]{1,0:T(8,128)S(1)}, u32[]{:S(2)}, u32[]{:S(2)}) %collective-permute-start.17) | collective-permute-done | bytes 12320 | tf_op jit(solution)/shard_map/ppermute | solution.py:188
  83.5 0.0 collective-permute-done.7.face_1_grads
  83.5 0.0 collective-permute-done.8.face_2_grads
  83.5 11.0 %key_side.1 = (bf16[128,1536]{1,0:T(8,128)(2,1)}, bf16[128,1536]{1,0:T(8,128)(2,1)}) custom-call(bf16[2,128,1536]{2,1,0:T(8,128)(2,1)S(1)} %pad_maximum_fusion.own.keys, f32[2,128,1536]{2,1,0:T(8,128)S(1)} %get-tuple-element.14.own_grads, bf16[2,64,1536]{2,1,0:T(8,128)(2,1)S(1)} %collective-permute-done.7.face_1_grads, ...), custom_call_target="tpu_custom_call" | custom-call | flops 805306368 | bytes 8388608 | tf_op jit(solution)/shard_map/key_side/pallas_call | solution.py:192
  (3 shorter events, 0.1 us)
Async XLA Ops:
  0.6 7.7 %copy-start.1 = (bf16[1,2,64,1536]{3,2,1,0:T(8,128)(2,1)S(1)}, bf16[1,2,64,1536]{3,2,1,0:T(8,128)(2,1)}, u32[]{:S(2)}) copy-start(bf16[1,2,64,1536]{3,2,1,0:T(8,128)(2,1)} %param.8) | copy-start | bytes 1179652
  0.6 7.7 %copy-start = (bf16[1,2,64,1536]{3,2,1,0:T(8,128)(2,1)S(1)}, bf16[1,2,64,1536]{3,2,1,0:T(8,128)(2,1)}, u32[]{:S(2)}) copy-start(bf16[1,2,64,1536]{3,2,1,0:T(8,128)(2,1)} %param.5) | copy-start | bytes 1179652
  0.7 13.1 %copy-start.3 = (s32[1,1,12,2]{2,3,1,0:T(2,128)S(1)}, s32[1,1,12,2]{2,3,1,0:T(2,128)}, u32[]{:S(2)}) copy-start(s32[1,1,12,2]{2,3,1,0:T(2,128)} %param.9) | copy-start | bytes 292
  1.9 20.5 %collective-permute-start.2 = (bf16[2,128,1536]{2,1,0:T(8,128)(2,1)S(1)}, bf16[2,128,1536]{2,1,0:T(8,128)(2,1)S(1)}, u32[]{:S(2)}, u32[]{:S(2)}) collective-permute-start(bf16[2,128,1536]{2,1,0:T(8,128)(2,1)S(1)} %pad_maximum_fusion.own.keys), channel_id=1, source_target_pairs={{0,4},{4,0},{8,12},{12,8},{16,20},{20,16},{24,28},{28,24},{1,5},{5... | collective-permute-start | bytes 2359304 | tf_op jit(solution)/shard_map/ppermute | solution.py:39
  2.5 22.5 %collective-permute-start.3 = (bf16[2,128,1536]{2,1,0:T(8,128)(2,1)S(1)}, bf16[2,128,1536]{2,1,0:T(8,128)(2,1)}, u32[]{:S(2)}, u32[]{:S(2)}) collective-permute-start(bf16[2,128,1536]{2,1,0:T(8,128)(2,1)S(1)} %pad_maximum_fusion.own.keys), channel_id=1, source_target_pairs={{4,12},{8,0},{12,20},{16,8},{20,28},{24,16},{5,13},{9,1},{13,21},{... | collective-permute-start | bytes 2359304 | tf_op jit(solution)/shard_map/ppermute | solution.py:41
  6.0 43.6 %collective-permute-start.4 = (bf16[2,128,1536]{2,1,0:T(8,128)(2,1)S(1)}, bf16[2,128,1536]{2,1,0:T(8,128)(2,1)}, u32[]{:S(2)}, u32[]{:S(2)}) collective-permute-start(bf16[2,128,1536]{2,1,0:T(8,128)(2,1)S(1)} %pad_maximum_fusion.own.keys), channel_id=1, source_target_pairs={{0,8},{8,16},{12,4},{16,24},{20,12},{28,20},{1,9},{9,17},{13,5},{1... | collective-permute-start | bytes 2359304 | tf_op jit(solution)/shard_map/ppermute | solution.py:40
  9.4 28.8 %collective-permute-start.9 = (bf16[2,128,1536]{2,1,0:T(8,128)(2,1)}, bf16[2,128,1536]{2,1,0:T(8,128)(2,1)S(1)}, u32[]{:S(2)}, u32[]{:S(2)}) collective-permute-start(bf16[2,128,1536]{2,1,0:T(8,128)(2,1)} %pad_maximum_fusion.1), channel_id=1, source_target_pairs={{0,4},{4,0},{8,12},{12,8},{16,20},{20,16},{24,28},{28,24},{1,5},{5... | collective-permute-start | bytes 2359304 | tf_op jit(solution)/shard_map/ppermute | solution.py:39
  11.7 30.7 %collective-permute-start.10 = (bf16[2,128,1536]{2,1,0:T(8,128)(2,1)}, bf16[2,128,1536]{2,1,0:T(8,128)(2,1)S(1)}, u32[]{:S(2)}, u32[]{:S(2)}) collective-permute-start(bf16[2,128,1536]{2,1,0:T(8,128)(2,1)} %pad_maximum_fusion.1), channel_id=1, source_target_pairs={{4,12},{8,0},{12,20},{16,8},{20,28},{24,16},{5,13},{9,1},{13,21},{... | collective-permute-start | bytes 2359304 | tf_op jit(solution)/shard_map/ppermute | solution.py:41
  15.3 39.3 %copy-start.2 = (bf16[1,2,64,1536]{3,2,1,0:T(8,128)(2,1)S(1)}, bf16[1,2,64,1536]{3,2,1,0:T(8,128)(2,1)}, u32[]{:S(2)}) copy-start(bf16[1,2,64,1536]{3,2,1,0:T(8,128)(2,1)} %param.8) | copy-start | bytes 1179652
  22.4 47.0 %collective-permute-start.11 = (bf16[2,128,1536]{2,1,0:T(8,128)(2,1)}, bf16[2,128,1536]{2,1,0:T(8,128)(2,1)S(1)}, u32[]{:S(2)}, u32[]{:S(2)}) collective-permute-start(bf16[2,128,1536]{2,1,0:T(8,128)(2,1)} %pad_maximum_fusion.1), channel_id=1, source_target_pairs={{0,8},{8,16},{12,4},{16,24},{20,12},{28,20},{1,9},{9,17},{13,5},{1... | collective-permute-start | bytes 2359304 | tf_op jit(solution)/shard_map/ppermute | solution.py:40
  25.0 15.1 %collective-permute-start = (bf16[2,64,1536]{2,1,0:T(8,128)(2,1)S(1)}, bf16[2,64,1536]{2,1,0:T(8,128)(2,1)S(1)}, u32[]{:S(2)}, u32[]{:S(2)}) collective-permute-start(bf16[2,64,1536]{2,1,0:T(8,128)(2,1)S(1)} %get-tuple-element.24), channel_id=1, source_target_pairs={{0,1},{1,0},{2,3},{3,2},{4,5},{5,4},{6,7},{7,6},{8,9},{9,8},{10,11... | collective-permute-start | bytes 1179656 | tf_op jit(solution)/shard_map/ppermute | solution.py:158
  38.1 9.1 %collective-permute-start.1 = (bf16[2,64,1536]{2,1,0:T(8,128)(2,1)S(1)}, bf16[2,64,1536]{2,1,0:T(8,128)(2,1)S(1)}, u32[]{:S(2)}, u32[]{:S(2)}) collective-permute-start(bf16[2,64,1536]{2,1,0:T(8,128)(2,1)S(1)} %get-tuple-element.23), channel_id=1, source_target_pairs={{1,2},{2,1},{5,6},{6,5},{9,10},{10,9},{13,14},{14,13},{17,18},{18,... | collective-permute-start | bytes 1179656 | tf_op jit(solution)/shard_map/ppermute | solution.py:159
  40.1 13.9 %collective-permute-start.5 = (bf16[128,1536]{1,0:T(8,128)(2,1)S(1)}, bf16[128,1536]{1,0:T(8,128)(2,1)S(1)}, u32[]{:S(2)}, u32[]{:S(2)}) collective-permute-start(bf16[128,1536]{1,0:T(8,128)(2,1)S(1)} %slice_bitcast_fusion.3), channel_id=1, source_target_pairs={{0,8},{8,16},{12,4},{16,24},{20,12},{28,20},{1,9},{9,17},{13,5},{1... | collective-permute-start | bytes 1179656 | tf_op jit(solution)/shard_map/ppermute | solution.py:43
  42.5 12.1 %collective-permute-start.6 = (bf16[128,1536]{1,0:T(8,128)(2,1)S(1)}, bf16[128,1536]{1,0:T(8,128)(2,1)S(1)}, u32[]{:S(2)}, u32[]{:S(2)}) collective-permute-start(bf16[128,1536]{1,0:T(8,128)(2,1)S(1)} %slice_bitcast_fusion.2), channel_id=1, source_target_pairs={{0,4},{4,0},{8,12},{12,8},{16,20},{20,16},{24,28},{28,24},{1,5},{5... | collective-permute-start | bytes 1179656 | tf_op jit(solution)/shard_map/ppermute | solution.py:44
  47.2 24.0 %collective-permute-start.12 = (bf16[128,1536]{1,0:T(8,128)(2,1)S(1)}, bf16[128,1536]{1,0:T(8,128)(2,1)S(1)}, u32[]{:S(2)}, u32[]{:S(2)}) collective-permute-start(bf16[128,1536]{1,0:T(8,128)(2,1)S(1)} %slice_bitcast_fusion.1), channel_id=1, source_target_pairs={{0,8},{8,16},{12,4},{16,24},{20,12},{28,20},{1,9},{9,17},{13,5},{1... | collective-permute-start | bytes 1179656 | tf_op jit(solution)/shard_map/ppermute | solution.py:43
  49.6 23.8 %collective-permute-start.13 = (bf16[128,1536]{1,0:T(8,128)(2,1)S(1)}, bf16[128,1536]{1,0:T(8,128)(2,1)S(1)}, u32[]{:S(2)}, u32[]{:S(2)}) collective-permute-start(bf16[128,1536]{1,0:T(8,128)(2,1)S(1)} %slice_bitcast_fusion), channel_id=1, source_target_pairs={{0,4},{4,0},{8,12},{12,8},{16,20},{20,16},{24,28},{28,24},{1,5},{5... | collective-permute-start | bytes 1179656 | tf_op jit(solution)/shard_map/ppermute | solution.py:44
  66.9 16.6 %collective-permute-start.7 = (bf16[2,64,1536]{2,1,0:T(8,128)(2,1)S(1)}, bf16[2,64,1536]{2,1,0:T(8,128)(2,1)S(1)}, u32[]{:S(2)}, u32[]{:S(2)}) collective-permute-start(bf16[2,64,1536]{2,1,0:T(8,128)(2,1)S(1)} %get-tuple-element.15), channel_id=1, source_target_pairs={{0,1},{1,0},{2,3},{3,2},{4,5},{5,4},{6,7},{7,6},{8,9},{9,8},{10,11... | collective-permute-start | bytes 1179656 | tf_op jit(solution)/shard_map/ppermute | solution.py:189
  66.9 16.6 %collective-permute-start.8 = (bf16[2,64,1536]{2,1,0:T(8,128)(2,1)S(1)}, bf16[2,64,1536]{2,1,0:T(8,128)(2,1)S(1)}, u32[]{:S(2)}, u32[]{:S(2)}) collective-permute-start(bf16[2,64,1536]{2,1,0:T(8,128)(2,1)S(1)} %get-tuple-element.16), channel_id=1, source_target_pairs={{1,2},{2,1},{5,6},{6,5},{9,10},{10,9},{13,14},{14,13},{17,18},{18,... | collective-permute-start | bytes 1179656 | tf_op jit(solution)/shard_map/ppermute | solution.py:190
  69.5 7.6 %collective-permute-start.14 = (f32[24,128]{1,0:T(8,128)S(1)}, f32[24,128]{1,0:T(8,128)S(1)}, u32[]{:S(2)}, u32[]{:S(2)}) collective-permute-start(f32[24,128]{1,0:T(8,128)S(1)} %get-tuple-element.17), channel_id=1, source_target_pairs={{0,4},{4,0},{8,12},{12,8},{16,20},{20,16},{24,28},{28,24},{1,5},{5... | collective-permute-start | bytes 36872 | tf_op jit(solution)/shard_map/ppermute | solution.py:185
  71.2 7.8 %collective-permute-start.15 = (f32[24,128]{1,0:T(8,128)S(1)}, f32[24,128]{1,0:T(8,128)S(1)}, u32[]{:S(2)}, u32[]{:S(2)}) collective-permute-start(f32[24,128]{1,0:T(8,128)S(1)} %get-tuple-element.18), channel_id=1, source_target_pairs={{4,12},{8,0},{12,20},{16,8},{20,28},{24,16},{5,13},{9,1},{13,21},{... | collective-permute-start | bytes 36872 | tf_op jit(solution)/shard_map/ppermute | solution.py:186
  73.3 5.7 %collective-permute-start.16 = (f32[24,128]{1,0:T(8,128)S(1)}, f32[24,128]{1,0:T(8,128)S(1)}, u32[]{:S(2)}, u32[]{:S(2)}) collective-permute-start(f32[24,128]{1,0:T(8,128)S(1)} %get-tuple-element.19), channel_id=1, source_target_pairs={{0,8},{8,16},{12,4},{16,24},{20,12},{28,20},{1,9},{9,17},{13,5},{1... | collective-permute-start | bytes 36872 | tf_op jit(solution)/shard_map/ppermute | solution.py:187
  77.1 6.5 %collective-permute-start.17 = (f32[24,128]{1,0:T(8,128)S(1)}, f32[24,128]{1,0:T(8,128)S(1)}, u32[]{:S(2)}, u32[]{:S(2)}) collective-permute-start(f32[24,128]{1,0:T(8,128)S(1)} %get-tuple-element.20), channel_id=1, source_target_pairs={{4,8},{8,4},{12,16},{16,12},{20,24},{24,20},{5,9},{9,5},{13,17},{1... | collective-permute-start | bytes 36872 | tf_op jit(solution)/shard_map/ppermute | solution.py:188

commit v2 on v1

v2 whole, which is shorter than its diff:
```python
import functools

import jax
import jax.numpy as jnp
from jax import lax
from jax.experimental import pallas as pl
from jax.experimental.pallas import tpu as pltpu
from jax.sharding import PartitionSpec as P

HEAD_DIM = 128
REACH = 2
SCALE = HEAD_DIM**-0.5
LOG2E = 1.4426950408889634
FAR_AWAY = 3e38
VMEM_BYTES = 10 * 1024 * 1024
NT = (((1,), (1,)), ((), ()))
NN = (((1,), (0,)), ((), ()))
TN = (((0,), (0,)), ((), ()))


def dot(left, right, dims):
    return lax.dot_general(left, right, dims, preferred_element_type=jnp.float32)


def corners(first, second):
    zero = jnp.zeros_like(first)
    top = jnp.concatenate([first, zero], axis=1)
    return jnp.concatenate([top, jnp.concatenate([zero, second], axis=1)], axis=0)


def routes(size):
    def keep(move):
        return [(i, move(i)) for i in range(size) if 0 <= move(i) < size]

    partner = keep(lambda i: i ^ 1)
    route_a = keep(lambda i: i - 2 if i % 2 == 0 else i + 2)
    route_b = keep(lambda i: i + 2 if i % 2 == 0 else i - 2)
    outer = keep(lambda i: i - 1 if i % 2 == 0 else i + 1)
    return partner, route_a, route_b, outer


def after(value, *done):
    return lax.optimization_barrier((value, *done))[0]


class Either:
    def __init__(self, second, if_second, if_first):
        self.second, self.if_second, self.if_first = second == 1, if_second, if_first
        self.shape = if_first.shape

    def __getitem__(self, at):
        return jnp.where(self.second, self.if_second[at], self.if_first[at])


def query_kernel(
    n_tm, n_height, mine, own, face_1, face_2, part, a, b, outer_even, outer_odd, picks,
    grad_query, own_grads, face_1_grads, face_2_grads, stats, scores,
):
    query, grad = mine.at[0], mine.at[1]
    heads = query.shape[1] // HEAD_DIM
    at, line = lax.axis_index("tm"), lax.axis_index("height")
    odd, line_odd = lax.rem(at, 2), lax.rem(line, 2)
    slots = (2 - odd, 3 - 3 * odd, 3 * odd, 1 + odd)

    def inside(slot):
        target = at + slot - jnp.where(slot < REACH, REACH, REACH - 1)
        return (target >= 0) & (target < n_tm)

    slot_ok = [inside(s) for s in slots]
    face_1_ok = (line_odd == 1) | (line + 1 < n_height)
    face_2_ok = jnp.where(line_odd == 1, line + 1 < n_height, line > 0)
    row_1, row_2 = line_odd, 1 - line_odd
    sets = [(own.at[0], own.at[1])]
    sets += [(f.at[0, r], f.at[1, r]) for f, r in ((face_1, row_1), (face_2, row_2))]
    sets += [(x.at[0], x.at[1]) for x in (part, a, b)]
    sets += [tuple(Either(line_odd, outer_odd.at[i], outer_even.at[i]) for i in (0, 1))]
    spans, start = [], 0
    for keys, _ in sets:
        spans.append(pl.ds(start, keys.shape[0]))
        start += keys.shape[0]

    def columns(e):
        return pl.ds(e * HEAD_DIM, HEAD_DIM)

    def products(e):
        cols = columns(e)
        both = corners(query[:, cols], grad[:, cols])
        for (keys, values), span in zip(sets, spans):
            pair = jnp.concatenate([keys[:, cols], values[:, cols]], axis=1)
            scores[e % 2, span, :] = dot(pair, both, NT)

    def finish(e):
        cols = columns(e)
        q, g = query[:, cols], grad[:, cols]
        chosen = [ok & ((picks[e, 0] == s) | (picks[e, 1] == s)) for s, ok in zip(slots, slot_ok)]
        present = [None, face_1_ok, face_2_ok] + chosen
        score = [scores.at[e % 2, span, pl.ds(0, HEAD_DIM)] for span in spans]
        grad_weight = [scores.at[e % 2, span, pl.ds(HEAD_DIM, HEAD_DIM)] for span in spans]
        tops = [jnp.max(s[...], axis=0, keepdims=True) for s in score]
        tops = [t if ok is None else jnp.where(ok, t, -jnp.inf) for t, ok in zip(tops, present)]
        top = functools.reduce(jnp.maximum, tops) * (SCALE * LOG2E)
        expo = [
            jnp.exp2(s[...] * (SCALE * LOG2E) - (top if ok is None else jnp.where(ok, top, FAR_AWAY)))
            for s, ok in zip(score, present)
        ]
        total = sum(jnp.sum(x, axis=0, keepdims=True) for x in expo)
        inverse = 1.0 / total
        delta = sum(jnp.sum(x * w[...], axis=0, keepdims=True) for x, w in zip(expo, grad_weight))
        delta = delta * inverse
        level = top + jnp.log2(total)
        stats[0, e : e + 1, :] = delta
        for i, ok in enumerate(chosen):
            stats[1 + i, e : e + 1, :] = jnp.where(ok, level, FAR_AWAY)
        weights = [x * inverse for x in expo]
        dscore = [
            (w * (x[...] - delta) * SCALE).astype(jnp.bfloat16) for w, x in zip(weights, grad_weight)
        ]
        all_keys = jnp.concatenate([keys[:, cols] for keys, _ in sets], axis=0)
        dq = dot(jnp.concatenate(dscore, axis=0), all_keys, TN)
        grad_query[:, cols] = dq.astype(grad_query.dtype)
        both = corners(q, g)
        for i, out in enumerate((own_grads, face_1_grads, face_2_grads)):
            pair = jnp.concatenate([dscore[i], weights[i].astype(jnp.bfloat16)], axis=1)
            grads = dot(pair, both, NN)
            out[0, :, cols] = grads[:, :HEAD_DIM].astype(out.dtype)
            out[1, :, cols] = grads[:, HEAD_DIM:].astype(out.dtype)

    products(0)
    for e in range(heads):
        if e + 1 < heads:
            products(e + 1)
        finish(e)


def far_grads(keys, pairs, sums, store, scratch):
    heads = keys.shape[2] // HEAD_DIM

    def columns(e):
        return pl.ds(e * HEAD_DIM, HEAD_DIM)

    def products(e):
        cols = columns(e)
        pair = jnp.concatenate([keys[0, :, cols], keys[1, :, cols]], axis=1)
        for i, (query, grad, _, _) in enumerate(pairs):
            scratch[e % 2, i] = dot(pair, corners(query[:, cols], grad[:, cols]), NT)

    def finish(e):
        cols = columns(e)
        total = sums(cols)
        for i, (query, grad, levels, deltas) in enumerate(pairs):
            score, grad_weights = scratch.at[e % 2, i, :, :HEAD_DIM], scratch.at[e % 2, i, :, HEAD_DIM:]
            weights = jnp.exp2(score[...] * (SCALE * LOG2E) - levels[e : e + 1, :])
            dscore = weights * (grad_weights[...] - deltas[e : e + 1, :]) * SCALE
            both = jnp.concatenate([dscore.astype(jnp.bfloat16), weights.astype(jnp.bfloat16)], axis=1)
            total += dot(both, corners(query[:, cols], grad[:, cols]), NN)
        store(cols, total)

    products(0)
    for e in range(heads):
        if e + 1 < heads:
            products(e + 1)
        finish(e)


def key_kernel(keys, own_grads, part, a, of_part, of_a, sums_out, scratch):
    def sums(cols):
        return jnp.concatenate([own_grads[0, :, cols], own_grads[1, :, cols]], axis=1)

    def store(cols, total):
        sums_out[0, :, cols] = total[:, :HEAD_DIM]
        sums_out[1, :, cols] = total[:, HEAD_DIM:]

    pairs = (
        (part.at[0], part.at[1], of_part.at[1], of_part.at[0]),
        (a.at[0], a.at[1], of_a.at[3], of_a.at[0]),
    )
    far_grads(keys, pairs, sums, store, scratch)


def last_kernel(
    keys, sums_in, face_1_grads, face_2_grads, b, outer_even, outer_odd, of_b, grad_key, grad_value,
    scratch,
):
    face = face_1_grads.shape[1]
    line_odd = lax.rem(lax.axis_index("height"), 2)
    last_first = line_odd == 0
    outer = [Either(line_odd, outer_odd.at[i], outer_even.at[i]) for i in (0, 1)]

    def sums(cols):
        return jnp.concatenate([sums_in[0, :, cols], sums_in[1, :, cols]], axis=1)

    def store(cols, total):
        for at, out in ((0, grad_key), (1, grad_value)):
            one = face_1_grads[at, :, cols].astype(jnp.float32)
            two = face_2_grads[at, :, cols].astype(jnp.float32)
            first, last = jnp.where(last_first, two, one), jnp.where(last_first, one, two)
            part = total[:, at * HEAD_DIM : (at + 1) * HEAD_DIM]
            out[:face, cols] = (part[:face] + first).astype(out.dtype)
            out[face:, cols] = (part[face:] + last).astype(out.dtype)

    pairs = (
        (b.at[0], b.at[1], of_b.at[0, 2], of_b.at[0, 0]),
        (*outer, of_b.at[1, 4], of_b.at[1, 0]),
    )
    far_grads(keys, pairs, sums, store, scratch)


def per_device(query_tok, key_tok, value_tok, grad_out, far_picks):
    frames_dev, rows_dev, columns, width = query_tok.shape
    tile, face = frames_dev * rows_dev * columns, frames_dev * columns
    heads = width // HEAD_DIM
    n_tm, n_height = lax.axis_size("tm"), lax.axis_size("height")
    query, key = query_tok.reshape(tile, width), key_tok.reshape(tile, width)
    value, grad = value_tok.reshape(tile, width), grad_out.reshape(tile, width)
    partner, route_a, route_b, outer = routes(n_tm)

    def move(block, route):
        return lax.ppermute(block, "tm", route)

    def relay(own, from_partner, from_a):
        if n_tm % 2:
            return (move(own, outer),) * 2

        def of_line(route, odd):
            lines = range(odd, n_height, 2)
            return [(i * n_height + h, j * n_height + h) for h in lines for i, j in route]

        even = lax.ppermute(from_partner, ("tm", "height"), of_line(route_b, 0))
        return even, lax.ppermute(from_a, ("tm", "height"), of_line(partner, 1))

    pairs_1 = [(i, i ^ 1) for i in range(n_height) if i ^ 1 < n_height]
    pairs_2 = [(i, i - 1 if i % 2 == 0 else i + 1) for i in range(n_height)]
    pairs_2 = [(i, j) for i, j in pairs_2 if 0 <= j < n_height]

    key_value, query_grad = jnp.stack([key, value]), jnp.stack([query, grad])
    kv_part, kv_a, kv_b = move(key_value, partner), move(key_value, route_a), move(key_value, route_b)
    face_1 = lax.ppermute(key_value, "height", pairs_1)
    face_2 = lax.ppermute(key_value, "height", pairs_2)
    kv_even, kv_odd = relay(key_value, kv_part, kv_a)
    qg_part = move(after(query_grad, kv_a), partner)
    qg_a = move(after(query_grad, kv_a), route_a)
    qg_b = move(after(query_grad, kv_part), route_b)

    f32, bf16 = jnp.float32, jnp.bfloat16
    vmem = pl.BlockSpec(memory_space=pltpu.VMEM)
    block = 2 * tile * tile * HEAD_DIM * heads
    total_keys = tile * (1 + 2 * REACH) + 2 * face
    params = pltpu.CompilerParams(vmem_limit_bytes=VMEM_BYTES)
    by_row = (2, rows_dev, face, width)
    grad_query, own_grads, face_1_grads, face_2_grads, stats = pl.pallas_call(
        functools.partial(query_kernel, n_tm, n_height),
        out_shape=(
            jax.ShapeDtypeStruct((tile, width), bf16),
            jax.ShapeDtypeStruct((2, tile, width), f32),
            jax.ShapeDtypeStruct((2, face, width), bf16),
            jax.ShapeDtypeStruct((2, face, width), bf16),
            jax.ShapeDtypeStruct((1 + 2 * REACH, heads, tile), f32),
        ),
        in_specs=[vmem] * 9 + [pl.BlockSpec(memory_space=pltpu.SMEM)],
        out_specs=[vmem] * 5,
        scratch_shapes=[pltpu.VMEM((2, total_keys, 2 * HEAD_DIM), f32)],
        compiler_params=params,
        cost_estimate=pl.CostEstimate(flops=22 * block, bytes_accessed=8 << 20, transcendentals=0),
        name="query_side",
    )(query_grad, key_value, face_1.reshape(by_row), face_2.reshape(by_row), kv_part, kv_a, kv_b,
      kv_even, kv_odd, far_picks.reshape(heads, far_picks.shape[3]))

    of_part, of_a = move(stats, partner), move(stats, route_a)
    qg_even, qg_odd = relay(query_grad, after(qg_part, of_part), after(qg_a, stats))
    of_b = move(jnp.stack([stats, of_part]), route_b)
    if n_tm % 2:
        of_b = jnp.stack([of_b[0], move(stats, outer)])
    back_1 = lax.ppermute(face_1_grads, "height", pairs_1)
    back_2 = lax.ppermute(face_2_grads, "height", pairs_2)

    scratch = [pltpu.VMEM((2, 2, tile, 2 * HEAD_DIM), f32)]
    sums = pl.pallas_call(
        key_kernel,
        out_shape=jax.ShapeDtypeStruct((2, tile, width), f32),
        in_specs=[vmem] * 6,
        out_specs=vmem,
        scratch_shapes=scratch,
        compiler_params=params,
        cost_estimate=pl.CostEstimate(flops=8 * block, bytes_accessed=8 << 20, transcendentals=0),
        name="key_side",
    )(key_value, own_grads, qg_part, qg_a, of_part, of_a)
    grad_key, grad_value = pl.pallas_call(
        last_kernel,
        out_shape=(jax.ShapeDtypeStruct((tile, width), bf16),) * 2,
        in_specs=[vmem] * 8,
        out_specs=[vmem] * 2,
        scratch_shapes=scratch,
        compiler_params=params,
        cost_estimate=pl.CostEstimate(flops=8 * block, bytes_accessed=8 << 20, transcendentals=0),
        name="last_side",
    )(key_value, sums, back_1, back_2, qg_b, qg_even, qg_odd, of_b)
    return tuple(x.reshape(query_tok.shape) for x in (grad_query, grad_key, grad_value))


def solution(mesh):
    spec = P("tm", "height", None, None)
    return jax.shard_map(
        per_device, mesh=mesh, in_specs=(spec,) * 5, out_specs=(spec,) * 3, check_vma=False
    )
```

time: 95 us -> 78.6 us (0.83)
  the two profiles are of different devices: /device:TPU:22 before, /device:TPU:1 now
where the time goes in v2:
time: 78.6 us; the launch traced here: 78 us
  starting transfers between devices  39.4 us (50%)
  waiting for transfers between devices  16.8 us (21%)
  Pallas kernels  13.4 us (17%)
  local copies, waits for them, and re-layouts  6.17 us (8%)
  other arithmetic  1.34 us (2%)
  between operations  0.9 us (1%)
    ppermute x9, starting transfers between devices, move(): return lax.ppermute(block, 'tm', route)  21 us
    ppermute x9, waiting for transfers between devices, move(): return lax.ppermute(block, 'tm', route)  14.1 us
    pallas_call x1, Pallas kernels, per_device(): pl.pallas_call(functools.partial(query_kernel, n_tm, n_height), out_shape...  8.17 us
    unnamed x18, local copies, waits for them, and re-layouts  6.07 us
    ppermute x2, starting transfers between devices, relay(): return (even, lax.ppermute(from_a, ('tm', 'height'), of_line(partner, 1)))  5.27 us
    ppermute x1, starting transfers between devices, per_device(): back_1 = lax.ppermute(face_1_grads, 'height', pairs_1)  3.9 us
    ppermute x1, starting transfers between devices, per_device(): face_2 = lax.ppermute(key_value, 'height', pairs_2)  3.05 us
    ppermute x1, starting transfers between devices, per_device(): back_2 = lax.ppermute(face_2_grads, 'height', pairs_2)  2.94 us
  transfers between devices with their start and end apart: 17, of which 4 were waited for; matrix products, arithmetic and copies ran while one was open for 0% of the time, Pallas kernels for 14%

profile of v2, /device:TPU:1, one launch (start us, length us, event | category | flops | bytes accessed | tf_op | source)
XLA Modules:
  0.0 78.0 jit_solution(13292612207128418715)
XLA Ops:
  0.6 0.0 copy-start.6
  0.6 0.0 copy-start.7
  0.7 0.0 copy-start.8
  0.7 1.3 %pad_maximum_fusion.1.own.keys = bf16[2,128,1536]{2,1,0:T(8,128)(2,1)S(1)} fusion(bf16[1,128,1536]{2,1,0:T(8,128)(2,1)} %bitcast.16, bf16[1,128,1536]{2,1,0:T(8,128)(2,1)} %bitcast.17), kind=kLoop, calls=%fused_computation.1 | loop fusion | flops 393216 | bytes 1572864 | tf_op jit(solution)/shard_map/stack | solution.py:235
  1.9 2.1 %collective-permute-start.2 = (bf16[2,128,1536]{2,1,0:T(8,128)(2,1)S(1)}, bf16[2,128,1536]{2,1,0:T(8,128)(2,1)}, u32[]{:S(2)}, u32[]{:S(2)}) collective-permute-start(bf16[2,128,1536]{2,1,0:T(8,128)(2,1)S(1)} %pad_maximum_fusion.1.own.keys), channel_id=1, source_target_pairs={{0,4},{4,0},{8,12},{12,8},{16,20},{20,16},{24,28},{28,24},{1,5},{5... | collective-permute-start | bytes 2359304 | tf_op jit(solution)/shard_map/ppermute | solution.py:218
  4.0 1.3 %collective-permute-start.3 = (bf16[2,128,1536]{2,1,0:T(8,128)(2,1)S(1)}, bf16[2,128,1536]{2,1,0:T(8,128)(2,1)}, u32[]{:S(2)}, u32[]{:S(2)}) collective-permute-start(bf16[2,128,1536]{2,1,0:T(8,128)(2,1)S(1)} %pad_maximum_fusion.1.own.keys), channel_id=1, source_target_pairs={{4,12},{8,0},{12,20},{16,8},{20,28},{24,16},{5,13},{9,1},{13,21},{... | collective-permute-start | bytes 2359304 | tf_op jit(solution)/shard_map/ppermute | solution.py:218
  5.3 1.0 %collective-permute-start = (bf16[2,128,1536]{2,1,0:T(8,128)(2,1)S(1)}, bf16[2,128,1536]{2,1,0:T(8,128)(2,1)S(1)}, u32[]{:S(2)}, u32[]{:S(2)}) collective-permute-start(bf16[2,128,1536]{2,1,0:T(8,128)(2,1)S(1)} %pad_maximum_fusion.1.own.keys), channel_id=1, source_target_pairs={{0,1},{1,0},{2,3},{3,2},{4,5},{5,4},{6,7},{7,6},{8,9},{9,8},{10,11... | collective-permute-start | bytes 2359304 | tf_op jit(solution)/shard_map/ppermute | solution.py:237
  6.3 3.0 %collective-permute-start.1 = (bf16[2,128,1536]{2,1,0:T(8,128)(2,1)S(1)}, bf16[2,128,1536]{2,1,0:T(8,128)(2,1)S(1)}, u32[]{:S(2)}, u32[]{:S(2)}) collective-permute-start(bf16[2,128,1536]{2,1,0:T(8,128)(2,1)S(1)} %pad_maximum_fusion.1.own.keys), channel_id=1, source_target_pairs={{1,2},{2,1},{5,6},{6,5},{9,10},{10,9},{13,14},{14,13},{17,18},{18,... | collective-permute-start | bytes 2359304 | tf_op jit(solution)/shard_map/ppermute | solution.py:238
  9.4 4.3 %collective-permute-start.4 = (bf16[2,128,1536]{2,1,0:T(8,128)(2,1)S(1)}, bf16[2,128,1536]{2,1,0:T(8,128)(2,1)S(1)}, u32[]{:S(2)}, u32[]{:S(2)}) collective-permute-start(bf16[2,128,1536]{2,1,0:T(8,128)(2,1)S(1)} %pad_maximum_fusion.1.own.keys), channel_id=1, source_target_pairs={{0,8},{8,16},{12,4},{16,24},{20,12},{28,20},{1,9},{9,17},{13,5},{1... | collective-permute-start | bytes 2359304 | tf_op jit(solution)/shard_map/ppermute | solution.py:218
  13.7 7.7 %collective-permute-done.2.part = bf16[2,128,1536]{2,1,0:T(8,128)(2,1)} collective-permute-done((bf16[2,128,1536]{2,1,0:T(8,128)(2,1)S(1)}, bf16[2,128,1536]{2,1,0:T(8,128)(2,1)}, u32[]{:S(2)}, u32[]{:S(2)}) %collective-permute-start.2) | collective-permute-done | bytes 786464 | tf_op jit(solution)/shard_map/ppermute | solution.py:218
  21.4 1.6 %collective-permute-start.5 = (bf16[2,128,1536]{2,1,0:T(8,128)(2,1)}, bf16[2,128,1536]{2,1,0:T(8,128)(2,1)}, u32[]{:S(2)}, u32[]{:S(2)}) collective-permute-start(bf16[2,128,1536]{2,1,0:T(8,128)(2,1)} %collective-permute-done.2.part), channel_id=1, source_target_pairs={{0,8},{8,16},{12,4},{16,24},{20,12},{28,20},{2,10},{10,18},{14,6},... | collective-permute-start | bytes 2359304 | tf_op jit(solution)/shard_map/ppermute | solution.py:228
  23.0 1.2 %collective-permute-done.3.a = bf16[2,128,1536]{2,1,0:T(8,128)(2,1)} collective-permute-done((bf16[2,128,1536]{2,1,0:T(8,128)(2,1)S(1)}, bf16[2,128,1536]{2,1,0:T(8,128)(2,1)}, u32[]{:S(2)}, u32[]{:S(2)}) %collective-permute-start.3) | collective-permute-done | bytes 786464 | tf_op jit(solution)/shard_map/ppermute | solution.py:218
  24.1 1.9 %collective-permute-start.6 = (bf16[2,128,1536]{2,1,0:T(8,128)(2,1)}, bf16[2,128,1536]{2,1,0:T(8,128)(2,1)}, u32[]{:S(2)}, u32[]{:S(2)}) collective-permute-start(bf16[2,128,1536]{2,1,0:T(8,128)(2,1)} %collective-permute-done.3.a), channel_id=1, source_target_pairs={{1,5},{5,1},{9,13},{13,9},{17,21},{21,17},{25,29},{29,25},{3,7},{7... | collective-permute-start | bytes 2359304 | tf_op jit(solution)/shard_map/ppermute | solution.py:229
  26.0 0.0 copy-done.6
  26.0 0.0 copy-done.7
  26.0 0.1 pad_maximum_fusion.mine
  26.1 0.0 collective-permute-done
  26.1 0.0 copy-start
  26.1 0.9 %copy-done = bf16[2,128,1536]{2,1,0:T(8,128)(2,1)} copy-done((bf16[2,128,1536]{2,1,0:T(8,128)(2,1)}, bf16[2,128,1536]{2,1,0:T(8,128)(2,1)S(1)}, u32[]{:S(2)}) %copy-start) | copy-done | bytes 786456
  27.0 1.3 %collective-permute-start.8 = (bf16[2,128,1536]{2,1,0:T(8,128)(2,1)S(1)}, bf16[2,128,1536]{2,1,0:T(8,128)(2,1)S(1)}, u32[]{:S(2)}, u32[]{:S(2)}) collective-permute-start(bf16[2,128,1536]{2,1,0:T(8,128)(2,1)S(1)} %pad_maximum_fusion.mine), channel_id=1, source_target_pairs={{4,12},{8,0},{12,20},{16,8},{20,28},{24,16},{5,13},{9,1},{13,21},{... | collective-permute-start | bytes 2359304 | tf_op jit(solution)/shard_map/ppermute | solution.py:218
  28.3 0.0 collective-permute-done.1
  28.3 0.0 copy-start.2
  28.3 0.9 %copy-done.2 = bf16[2,128,1536]{2,1,0:T(8,128)(2,1)} copy-done((bf16[2,128,1536]{2,1,0:T(8,128)(2,1)}, bf16[2,128,1536]{2,1,0:T(8,128)(2,1)S(1)}, u32[]{:S(2)}) %copy-start.2) | copy-done | bytes 786456
  29.2 3.4 %collective-permute-start.7 = (bf16[2,128,1536]{2,1,0:T(8,128)(2,1)S(1)}, bf16[2,128,1536]{2,1,0:T(8,128)(2,1)}, u32[]{:S(2)}, u32[]{:S(2)}) collective-permute-start(bf16[2,128,1536]{2,1,0:T(8,128)(2,1)S(1)} %pad_maximum_fusion.mine), channel_id=1, source_target_pairs={{0,4},{4,0},{8,12},{12,8},{16,20},{20,16},{24,28},{28,24},{1,5},{5... | collective-permute-start | bytes 2359304 | tf_op jit(solution)/shard_map/ppermute | solution.py:218
  32.6 0.0 collective-permute-done.4.b
  32.6 0.0 copy-start.4
  32.6 0.9 %copy-done.4 = bf16[2,128,1536]{2,1,0:T(8,128)(2,1)} copy-done((bf16[2,128,1536]{2,1,0:T(8,128)(2,1)}, bf16[2,128,1536]{2,1,0:T(8,128)(2,1)S(1)}, u32[]{:S(2)}) %copy-start.4) | copy-done | bytes 786456
  33.5 3.2 %collective-permute-start.13 = (bf16[2,128,1536]{2,1,0:T(8,128)(2,1)S(1)}, bf16[2,128,1536]{2,1,0:T(8,128)(2,1)S(1)}, u32[]{:S(2)}, u32[]{:S(2)}) collective-permute-start(bf16[2,128,1536]{2,1,0:T(8,128)(2,1)S(1)} %pad_maximum_fusion.mine), channel_id=1, source_target_pairs={{0,8},{8,16},{12,4},{16,24},{20,12},{28,20},{1,9},{9,17},{13,5},{1... | collective-permute-start | bytes 2359304 | tf_op jit(solution)/shard_map/ppermute | solution.py:218
  36.7 0.0 copy-done.8
  36.7 0.1 copy.8.picks
  36.8 0.0 collective-permute-done.5.outer_even
  36.8 2.7 %collective-permute-done.6.outer_odd = bf16[2,128,1536]{2,1,0:T(8,128)(2,1)} collective-permute-done((bf16[2,128,1536]{2,1,0:T(8,128)(2,1)}, bf16[2,128,1536]{2,1,0:T(8,128)(2,1)}, u32[]{:S(2)}, u32[]{:S(2)}) %collective-permute-start.6) | collective-permute-done | bytes 786464 | tf_op jit(solution)/shard_map/ppermute | solution.py:229
  39.5 0.0 copy-start.1
  39.5 1.1 %copy-done.1 = bf16[2,128,1536]{2,1,0:T(8,128)(2,1)S(1)} copy-done((bf16[2,128,1536]{2,1,0:T(8,128)(2,1)S(1)}, bf16[2,128,1536]{2,1,0:T(8,128)(2,1)}, u32[]{:S(2)}) %copy-start.1) | copy-done | bytes 786456
  40.7 0.0 copy-start.3
  40.7 1.1 %copy-done.3 = bf16[2,128,1536]{2,1,0:T(8,128)(2,1)S(1)} copy-done((bf16[2,128,1536]{2,1,0:T(8,128)(2,1)S(1)}, bf16[2,128,1536]{2,1,0:T(8,128)(2,1)}, u32[]{:S(2)}) %copy-start.3) | copy-done | bytes 786456
  41.8 0.0 copy-start.5
  41.8 1.1 %copy-done.5 = bf16[2,128,1536]{2,1,0:T(8,128)(2,1)S(1)} copy-done((bf16[2,128,1536]{2,1,0:T(8,128)(2,1)S(1)}, bf16[2,128,1536]{2,1,0:T(8,128)(2,1)}, u32[]{:S(2)}) %copy-start.5) | copy-done | bytes 786456
  42.9 8.2 %query_side.1 = (bf16[128,1536]{1,0:T(8,128)(2,1)}, f32[2,128,1536]{2,1,0:T(8,128)S(1)}, bf16[2,64,1536]{2,1,0:T(8,128)(2,1)S(1)}, bf16[2,64,1536]{2,1,0:T(8,128)(2,1)S(1)}, f32[5,12,128]{2,1,0:T(8,128)S(1)}) custom-call(bf16[2,128,1536]{2,1,0:T(8,128)(2,1)S(1)} %pad_maximum_fusion.mine, bf16[2,128,1536]{2,1,0:T(8,128)(2,1)S(1)} %pad_maximum_fusion.1.own.keys, ...), custom_call_target="tpu_custom_call" | custom-call | flops 1107296256 | bytes 8388608 | tf_op jit(solution)/shard_map/query_side/pallas_call | solution.py:250
  51.1 0.0 collective-permute-start.9
  51.1 0.0 collective-permute-done.8.a
  51.1 3.4 %collective-permute-start.15 = (bf16[2,128,1536]{2,1,0:T(8,128)(2,1)S(1)}, bf16[2,128,1536]{2,1,0:T(8,128)(2,1)S(1)}, u32[]{:S(2)}, u32[]{:S(2)}) collective-permute-start(bf16[2,128,1536]{2,1,0:T(8,128)(2,1)S(1)} %collective-permute-done.8.a), channel_id=1, source_target_pairs={{1,5},{5,1},{9,13},{13,9},{17,21},{21,17},{25,29},{29,25},{3,7},{7... | collective-permute-start | bytes 2359304 | tf_op jit(solution)/shard_map/ppermute | solution.py:229
  54.5 0.0 collective-permute-done.7.part
  54.5 0.0 collective-permute-done.9.of_part
  54.5 0.7 collective-permute-start.14
  55.2 3.9 %collective-permute-start.11 = (bf16[2,64,1536]{2,1,0:T(8,128)(2,1)S(1)}, bf16[2,64,1536]{2,1,0:T(8,128)(2,1)S(1)}, u32[]{:S(2)}, u32[]{:S(2)}) collective-permute-start(bf16[2,64,1536]{2,1,0:T(8,128)(2,1)S(1)} %get-tuple-element.18), channel_id=1, source_target_pairs={{0,1},{1,0},{2,3},{3,2},{4,5},{5,4},{6,7},{7,6},{8,9},{9,8},{10,11... | collective-permute-start | bytes 1179656 | tf_op jit(solution)/shard_map/ppermute | solution.py:273
  59.1 2.9 %collective-permute-start.12 = (bf16[2,64,1536]{2,1,0:T(8,128)(2,1)S(1)}, bf16[2,64,1536]{2,1,0:T(8,128)(2,1)S(1)}, u32[]{:S(2)}, u32[]{:S(2)}) collective-permute-start(bf16[2,64,1536]{2,1,0:T(8,128)(2,1)S(1)} %get-tuple-element.19), channel_id=1, source_target_pairs={{1,2},{2,1},{5,6},{6,5},{9,10},{10,9},{13,14},{14,13},{17,18},{18,... | collective-permute-start | bytes 1179656 | tf_op jit(solution)/shard_map/ppermute | solution.py:274
  62.1 0.0 collective-permute-done.13.b
  62.1 1.3 %collective-permute-start.10 = (f32[5,12,128]{2,1,0:T(8,128)S(1)}, f32[5,12,128]{2,1,0:T(8,128)S(1)}, u32[]{:S(2)}, u32[]{:S(2)}) collective-permute-start(f32[5,12,128]{2,1,0:T(8,128)S(1)} %get-tuple-element.17), channel_id=1, source_target_pairs={{4,12},{8,0},{12,20},{16,8},{20,28},{24,16},{5,13},{9,1},{13,21},{... | collective-permute-start | bytes 92168 | tf_op jit(solution)/shard_map/ppermute | solution.py:218
  63.4 5.2 %collective-permute-done.10.of_a = f32[5,12,128]{2,1,0:T(8,128)S(1)} collective-permute-done((f32[5,12,128]{2,1,0:T(8,128)S(1)}, f32[5,12,128]{2,1,0:T(8,128)S(1)}, u32[]{:S(2)}, u32[]{:S(2)}) %collective-permute-start.10) | collective-permute-done | bytes 30752 | tf_op jit(solution)/shard_map/ppermute | solution.py:218
  68.6 4.1 %collective-permute-start.16 = (f32[2,5,12,128]{3,2,1,0:T(8,128)S(1)}, f32[2,5,12,128]{3,2,1,0:T(8,128)S(1)}, u32[]{:S(2)}, u32[]{:S(2)}) collective-permute-start(f32[2,5,12,128]{3,2,1,0:T(8,128)S(1)} %pad_maximum_fusion.2), channel_id=1, source_target_pairs={{0,8},{8,16},{12,4},{16,24},{20,12},{28,20},{1,9},{9,17},{13,5},{1... | collective-permute-start | bytes 184328 | tf_op jit(solution)/shard_map/ppermute | solution.py:218
  72.8 2.7 %key_side.1.sums_in = f32[2,128,1536]{2,1,0:T(8,128)S(1)} custom-call(bf16[2,128,1536]{2,1,0:T(8,128)(2,1)S(1)} %pad_maximum_fusion.1.own.keys, f32[2,128,1536]{2,1,0:T(8,128)S(1)} %get-tuple-element.15.own_grads, bf16[2,128,1536]{2,1,0:T(8,128)(2,1)} %collective-permute-done.7.part, bf16[2,128,1536]{2,1,0:T(8,128)(2,1)S(1)} %collective-permute-done.8.a, ...), custom_call_target="tpu_custom_call" | custom-call | flops 402653184 | bytes 8388608 | tf_op jit(solution)/shard_map/key_side/pallas_call | solution.py:277
  75.5 0.0 collective-permute-done.16.of_b
  75.5 0.0 collective-permute-done.11.face_1_grads
  75.5 0.0 collective-permute-done.12.face_2_grads
  75.5 0.0 collective-permute-done.15.outer_odd
  75.5 0.0 collective-permute-done.14.outer_even
  75.6 2.5 %last_side.1 = (bf16[128,1536]{1,0:T(8,128)(2,1)}, bf16[128,1536]{1,0:T(8,128)(2,1)}) custom-call(bf16[2,128,1536]{2,1,0:T(8,128)(2,1)S(1)} %pad_maximum_fusion.1.own.keys, f32[2,128,1536]{2,1,0:T(8,128)S(1)} %key_side.1.sums_in, bf16[2,64,1536]{2,1,0:T(8,128)(2,1)S(1)} %collective-permute-done.11.face_1_grads, ...), custom_call_target="tpu_custom_call" | custom-call | flops 402653184 | bytes 8388608 | tf_op jit(solution)/shard_map/last_side/pallas_call | solution.py:287
  (1 shorter events, 0.0 us)
Async XLA Ops:
  0.6 25.4 %copy-start.6 = (bf16[1,2,64,1536]{3,2,1,0:T(8,128)(2,1)S(1)}, bf16[1,2,64,1536]{3,2,1,0:T(8,128)(2,1)}, u32[]{:S(2)}) copy-start(bf16[1,2,64,1536]{3,2,1,0:T(8,128)(2,1)} %param.8) | copy-start | bytes 1179652
  0.6 25.4 %copy-start.7 = (bf16[1,2,64,1536]{3,2,1,0:T(8,128)(2,1)S(1)}, bf16[1,2,64,1536]{3,2,1,0:T(8,128)(2,1)}, u32[]{:S(2)}) copy-start(bf16[1,2,64,1536]{3,2,1,0:T(8,128)(2,1)} %param.5) | copy-start | bytes 1179652
  0.7 36.1 %copy-start.8 = (s32[1,1,12,2]{2,3,1,0:T(2,128)S(1)}, s32[1,1,12,2]{2,3,1,0:T(2,128)}, u32[]{:S(2)}) copy-start(s32[1,1,12,2]{2,3,1,0:T(2,128)} %param.9) | copy-start | bytes 292
  1.9 19.5 %collective-permute-start.2 = (bf16[2,128,1536]{2,1,0:T(8,128)(2,1)S(1)}, bf16[2,128,1536]{2,1,0:T(8,128)(2,1)}, u32[]{:S(2)}, u32[]{:S(2)}) collective-permute-start(bf16[2,128,1536]{2,1,0:T(8,128)(2,1)S(1)} %pad_maximum_fusion.1.own.keys), channel_id=1, source_target_pairs={{0,4},{4,0},{8,12},{12,8},{16,20},{20,16},{24,28},{28,24},{1,5},{5... | collective-permute-start | bytes 2359304 | tf_op jit(solution)/shard_map/ppermute | solution.py:218
  4.0 20.1 %collective-permute-start.3 = (bf16[2,128,1536]{2,1,0:T(8,128)(2,1)S(1)}, bf16[2,128,1536]{2,1,0:T(8,128)(2,1)}, u32[]{:S(2)}, u32[]{:S(2)}) collective-permute-start(bf16[2,128,1536]{2,1,0:T(8,128)(2,1)S(1)} %pad_maximum_fusion.1.own.keys), channel_id=1, source_target_pairs={{4,12},{8,0},{12,20},{16,8},{20,28},{24,16},{5,13},{9,1},{13,21},{... | collective-permute-start | bytes 2359304 | tf_op jit(solution)/shard_map/ppermute | solution.py:218
  5.3 20.8 %collective-permute-start = (bf16[2,128,1536]{2,1,0:T(8,128)(2,1)S(1)}, bf16[2,128,1536]{2,1,0:T(8,128)(2,1)S(1)}, u32[]{:S(2)}, u32[]{:S(2)}) collective-permute-start(bf16[2,128,1536]{2,1,0:T(8,128)(2,1)S(1)} %pad_maximum_fusion.1.own.keys), channel_id=1, source_target_pairs={{0,1},{1,0},{2,3},{3,2},{4,5},{5,4},{6,7},{7,6},{8,9},{9,8},{10,11... | collective-permute-start | bytes 2359304 | tf_op jit(solution)/shard_map/ppermute | solution.py:237
  6.3 22.0 %collective-permute-start.1 = (bf16[2,128,1536]{2,1,0:T(8,128)(2,1)S(1)}, bf16[2,128,1536]{2,1,0:T(8,128)(2,1)S(1)}, u32[]{:S(2)}, u32[]{:S(2)}) collective-permute-start(bf16[2,128,1536]{2,1,0:T(8,128)(2,1)S(1)} %pad_maximum_fusion.1.own.keys), channel_id=1, source_target_pairs={{1,2},{2,1},{5,6},{6,5},{9,10},{10,9},{13,14},{14,13},{17,18},{18,... | collective-permute-start | bytes 2359304 | tf_op jit(solution)/shard_map/ppermute | solution.py:238
  9.4 23.3 %collective-permute-start.4 = (bf16[2,128,1536]{2,1,0:T(8,128)(2,1)S(1)}, bf16[2,128,1536]{2,1,0:T(8,128)(2,1)S(1)}, u32[]{:S(2)}, u32[]{:S(2)}) collective-permute-start(bf16[2,128,1536]{2,1,0:T(8,128)(2,1)S(1)} %pad_maximum_fusion.1.own.keys), channel_id=1, source_target_pairs={{0,8},{8,16},{12,4},{16,24},{20,12},{28,20},{1,9},{9,17},{13,5},{1... | collective-permute-start | bytes 2359304 | tf_op jit(solution)/shard_map/ppermute | solution.py:218
  21.4 15.4 %collective-permute-start.5 = (bf16[2,128,1536]{2,1,0:T(8,128)(2,1)}, bf16[2,128,1536]{2,1,0:T(8,128)(2,1)}, u32[]{:S(2)}, u32[]{:S(2)}) collective-permute-start(bf16[2,128,1536]{2,1,0:T(8,128)(2,1)} %collective-permute-done.2.part), channel_id=1, source_target_pairs={{0,8},{8,16},{12,4},{16,24},{20,12},{28,20},{2,10},{10,18},{14,6},... | collective-permute-start | bytes 2359304 | tf_op jit(solution)/shard_map/ppermute | solution.py:228
  24.1 15.4 %collective-permute-start.6 = (bf16[2,128,1536]{2,1,0:T(8,128)(2,1)}, bf16[2,128,1536]{2,1,0:T(8,128)(2,1)}, u32[]{:S(2)}, u32[]{:S(2)}) collective-permute-start(bf16[2,128,1536]{2,1,0:T(8,128)(2,1)} %collective-permute-done.3.a), channel_id=1, source_target_pairs={{1,5},{5,1},{9,13},{13,9},{17,21},{21,17},{25,29},{29,25},{3,7},{7... | collective-permute-start | bytes 2359304 | tf_op jit(solution)/shard_map/ppermute | solution.py:229
  26.1 0.9 %copy-start = (bf16[2,128,1536]{2,1,0:T(8,128)(2,1)}, bf16[2,128,1536]{2,1,0:T(8,128)(2,1)S(1)}, u32[]{:S(2)}) copy-start(bf16[2,128,1536]{2,1,0:T(8,128)(2,1)S(1)} %collective-permute-done) | copy-start | bytes 2359300
  27.0 24.1 %collective-permute-start.8 = (bf16[2,128,1536]{2,1,0:T(8,128)(2,1)S(1)}, bf16[2,128,1536]{2,1,0:T(8,128)(2,1)S(1)}, u32[]{:S(2)}, u32[]{:S(2)}) collective-permute-start(bf16[2,128,1536]{2,1,0:T(8,128)(2,1)S(1)} %pad_maximum_fusion.mine), channel_id=1, source_target_pairs={{4,12},{8,0},{12,20},{16,8},{20,28},{24,16},{5,13},{9,1},{13,21},{... | collective-permute-start | bytes 2359304 | tf_op jit(solution)/shard_map/ppermute | solution.py:218
  28.3 0.9 %copy-start.2 = (bf16[2,128,1536]{2,1,0:T(8,128)(2,1)}, bf16[2,128,1536]{2,1,0:T(8,128)(2,1)S(1)}, u32[]{:S(2)}) copy-start(bf16[2,128,1536]{2,1,0:T(8,128)(2,1)S(1)} %collective-permute-done.1) | copy-start | bytes 2359300
  29.2 25.3 %collective-permute-start.7 = (bf16[2,128,1536]{2,1,0:T(8,128)(2,1)S(1)}, bf16[2,128,1536]{2,1,0:T(8,128)(2,1)}, u32[]{:S(2)}, u32[]{:S(2)}) collective-permute-start(bf16[2,128,1536]{2,1,0:T(8,128)(2,1)S(1)} %pad_maximum_fusion.mine), channel_id=1, source_target_pairs={{0,4},{4,0},{8,12},{12,8},{16,20},{20,16},{24,28},{28,24},{1,5},{5... | collective-permute-start | bytes 2359304 | tf_op jit(solution)/shard_map/ppermute | solution.py:218
  32.6 0.9 %copy-start.4 = (bf16[2,128,1536]{2,1,0:T(8,128)(2,1)}, bf16[2,128,1536]{2,1,0:T(8,128)(2,1)S(1)}, u32[]{:S(2)}) copy-start(bf16[2,128,1536]{2,1,0:T(8,128)(2,1)S(1)} %collective-permute-done.4.b) | copy-start | bytes 2359300
  33.5 28.5 %collective-permute-start.13 = (bf16[2,128,1536]{2,1,0:T(8,128)(2,1)S(1)}, bf16[2,128,1536]{2,1,0:T(8,128)(2,1)S(1)}, u32[]{:S(2)}, u32[]{:S(2)}) collective-permute-start(bf16[2,128,1536]{2,1,0:T(8,128)(2,1)S(1)} %pad_maximum_fusion.mine), channel_id=1, source_target_pairs={{0,8},{8,16},{12,4},{16,24},{20,12},{28,20},{1,9},{9,17},{13,5},{1... | collective-permute-start | bytes 2359304 | tf_op jit(solution)/shard_map/ppermute | solution.py:218
  39.5 1.1 %copy-start.1 = (bf16[2,128,1536]{2,1,0:T(8,128)(2,1)S(1)}, bf16[2,128,1536]{2,1,0:T(8,128)(2,1)}, u32[]{:S(2)}) copy-start(bf16[2,128,1536]{2,1,0:T(8,128)(2,1)} %copy-done) | copy-start | bytes 2359300
  40.7 1.1 %copy-start.3 = (bf16[2,128,1536]{2,1,0:T(8,128)(2,1)S(1)}, bf16[2,128,1536]{2,1,0:T(8,128)(2,1)}, u32[]{:S(2)}) copy-start(bf16[2,128,1536]{2,1,0:T(8,128)(2,1)} %copy-done.2) | copy-start | bytes 2359300
  41.8 1.1 %copy-start.5 = (bf16[2,128,1536]{2,1,0:T(8,128)(2,1)S(1)}, bf16[2,128,1536]{2,1,0:T(8,128)(2,1)}, u32[]{:S(2)}) copy-start(bf16[2,128,1536]{2,1,0:T(8,128)(2,1)} %copy-done.4) | copy-start | bytes 2359300
  51.1 3.4 %collective-permute-start.9 = (f32[5,12,128]{2,1,0:T(8,128)S(1)}, f32[5,12,128]{2,1,0:T(8,128)S(1)}, u32[]{:S(2)}, u32[]{:S(2)}) collective-permute-start(f32[5,12,128]{2,1,0:T(8,128)S(1)} %get-tuple-element.17), channel_id=1, source_target_pairs={{0,4},{4,0},{8,12},{12,8},{16,20},{20,16},{24,28},{28,24},{1,5},{5... | collective-permute-start | bytes 92168 | tf_op jit(solution)/shard_map/ppermute | solution.py:218
  51.1 24.4 %collective-permute-start.15 = (bf16[2,128,1536]{2,1,0:T(8,128)(2,1)S(1)}, bf16[2,128,1536]{2,1,0:T(8,128)(2,1)S(1)}, u32[]{:S(2)}, u32[]{:S(2)}) collective-permute-start(bf16[2,128,1536]{2,1,0:T(8,128)(2,1)S(1)} %collective-permute-done.8.a), channel_id=1, source_target_pairs={{1,5},{5,1},{9,13},{13,9},{17,21},{21,17},{25,29},{29,25},{3,7},{7... | collective-permute-start | bytes 2359304 | tf_op jit(solution)/shard_map/ppermute | solution.py:229
  54.5 21.0 %collective-permute-start.14 = (bf16[2,128,1536]{2,1,0:T(8,128)(2,1)}, bf16[2,128,1536]{2,1,0:T(8,128)(2,1)S(1)}, u32[]{:S(2)}, u32[]{:S(2)}) collective-permute-start(bf16[2,128,1536]{2,1,0:T(8,128)(2,1)} %collective-permute-done.7.part), channel_id=1, source_target_pairs={{0,8},{8,16},{12,4},{16,24},{20,12},{28,20},{2,10},{10,18},{14,6},... | collective-permute-start | bytes 2359304 | tf_op jit(solution)/shard_map/ppermute | solution.py:228
  55.2 20.3 %collective-permute-start.11 = (bf16[2,64,1536]{2,1,0:T(8,128)(2,1)S(1)}, bf16[2,64,1536]{2,1,0:T(8,128)(2,1)S(1)}, u32[]{:S(2)}, u32[]{:S(2)}) collective-permute-start(bf16[2,64,1536]{2,1,0:T(8,128)(2,1)S(1)} %get-tuple-element.18), channel_id=1, source_target_pairs={{0,1},{1,0},{2,3},{3,2},{4,5},{5,4},{6,7},{7,6},{8,9},{9,8},{10,11... | collective-permute-start | bytes 1179656 | tf_op jit(solution)/shard_map/ppermute | solution.py:273
  59.1 16.4 %collective-permute-start.12 = (bf16[2,64,1536]{2,1,0:T(8,128)(2,1)S(1)}, bf16[2,64,1536]{2,1,0:T(8,128)(2,1)S(1)}, u32[]{:S(2)}, u32[]{:S(2)}) collective-permute-start(bf16[2,64,1536]{2,1,0:T(8,128)(2,1)S(1)} %get-tuple-element.19), channel_id=1, source_target_pairs={{1,2},{2,1},{5,6},{6,5},{9,10},{10,9},{13,14},{14,13},{17,18},{18,... | collective-permute-start | bytes 1179656 | tf_op jit(solution)/shard_map/ppermute | solution.py:274
  62.1 6.5 %collective-permute-start.10 = (f32[5,12,128]{2,1,0:T(8,128)S(1)}, f32[5,12,128]{2,1,0:T(8,128)S(1)}, u32[]{:S(2)}, u32[]{:S(2)}) collective-permute-start(f32[5,12,128]{2,1,0:T(8,128)S(1)} %get-tuple-element.17), channel_id=1, source_target_pairs={{4,12},{8,0},{12,20},{16,8},{20,28},{24,16},{5,13},{9,1},{13,21},{... | collective-permute-start | bytes 92168 | tf_op jit(solution)/shard_map/ppermute | solution.py:218
  68.6 6.9 %collective-permute-start.16 = (f32[2,5,12,128]{3,2,1,0:T(8,128)S(1)}, f32[2,5,12,128]{3,2,1,0:T(8,128)S(1)}, u32[]{:S(2)}, u32[]{:S(2)}) collective-permute-start(f32[2,5,12,128]{3,2,1,0:T(8,128)S(1)} %pad_maximum_fusion.2), channel_id=1, source_target_pairs={{0,8},{8,16},{12,4},{16,24},{20,12},{28,20},{1,9},{9,17},{13,5},{1... | collective-permute-start | bytes 184328 | tf_op jit(solution)/shard_map/ppermute | solution.py:218

commit v3 on v1

v3 whole, which is shorter than its diff:
```python
import functools

import jax
import jax.numpy as jnp
from jax import lax
from jax.experimental import pallas as pl
from jax.experimental.pallas import tpu as pltpu
from jax.sharding import PartitionSpec as P

HEAD_DIM = 128
REACH = 2
SCALE = HEAD_DIM**-0.5
LOG2E = 1.4426950408889634
FAR_AWAY = 3e38
VMEM_BYTES = 12 * 1024 * 1024
NT = (((1,), (1,)), ((), ()))
NN = (((1,), (0,)), ((), ()))
TN = (((0,), (0,)), ((), ()))


def dot(left, right, dims):
    return lax.dot_general(left, right, dims, preferred_element_type=jnp.float32)


def corners(first, second):
    zero = jnp.zeros_like(first)
    top = jnp.concatenate([first, zero], axis=1)
    return jnp.concatenate([top, jnp.concatenate([zero, second], axis=1)], axis=0)


def columns(e):
    return pl.ds(e * HEAD_DIM, HEAD_DIM)


def routes(size):
    def keep(move):
        return [(i, move(i)) for i in range(size) if 0 <= move(i) < size]

    partner = keep(lambda i: i ^ 1)
    route_a = keep(lambda i: i - 2 if i % 2 == 0 else i + 2)
    route_b = keep(lambda i: i + 2 if i % 2 == 0 else i - 2)
    outer = keep(lambda i: i - 1 if i % 2 == 0 else i + 1)
    return partner, route_a, route_b, outer


def after(value, *done):
    return lax.optimization_barrier((value, *done))[0]


def in_hbm(block):
    return pltpu.with_memory_space_constraint(block, pltpu.HBM)


def pair_kernel(key, value, query, grad, key_value, query_grad, sems):
    parts = sems.shape[1]
    rows = key.shape[0] // parts
    copies = []
    for i, (source, out) in enumerate(
        ((key, key_value.at[0]), (value, key_value.at[1]), (query, query_grad.at[0]), (grad, query_grad.at[1]))
    ):
        for part in range(parts):
            at = pl.ds(part * rows, rows)
            copies.append(pltpu.make_async_copy(source.at[at], out.at[at], sems.at[i, part]))
    for copy in copies:
        copy.start()
    for copy in copies:
        copy.wait()


def paired(*blocks):
    rows, width = blocks[0].shape
    parts = 4 if rows % 64 == 0 else 1
    return pl.pallas_call(
        pair_kernel,
        out_shape=(jax.ShapeDtypeStruct((2, rows, width), blocks[0].dtype),) * 2,
        in_specs=[pl.BlockSpec(memory_space=pltpu.HBM)] * 4,
        out_specs=[pl.BlockSpec(memory_space=pltpu.VMEM)] * 2,
        scratch_shapes=[pltpu.SemaphoreType.DMA((4, parts))],
        compiler_params=pltpu.CompilerParams(vmem_limit_bytes=VMEM_BYTES),
        cost_estimate=pl.CostEstimate(flops=0, bytes_accessed=16 * rows * width, transcendentals=0),
        name="pairs",
    )(*map(in_hbm, blocks))


class Stream:
    def __init__(self, sources, buffers, sems):
        heads = buffers[0].shape[2] // HEAD_DIM
        self.chunks = sems.shape[0]
        self.step = heads // self.chunks
        self.sources, self.buffers, self.sems = sources, buffers, sems
        for chunk in range(self.chunks):
            for i in range(len(sources)):
                self.copy(chunk, i).start()

    def copy(self, chunk, i):
        cols = pl.ds(chunk * self.step * HEAD_DIM, self.step * HEAD_DIM)
        return pltpu.make_async_copy(
            self.sources[i].at[:, :, cols], self.buffers[i].at[:, :, cols], self.sems.at[chunk, i]
        )

    def ready(self, e):
        if e % self.step == 0:
            for i in range(len(self.sources)):
                self.copy(e // self.step, i).wait()


def stream_sems(heads, count):
    return pltpu.SemaphoreType.DMA((4 if heads % 4 == 0 else 1, count))


def query_kernel(
    n_tm, n_height, mine, own, face_1, face_2, part, a, b, outer, picks,
    grad_query, own_grads, face_1_grads, face_2_grads, stats,
    scratch, graded, face_1_vmem, face_2_vmem, far_vmem, sems,
):
    heads, n_picks = mine.shape[2] // HEAD_DIM, picks.shape[1]
    at, line = lax.axis_index("tm"), lax.axis_index("height")
    odd, line_odd = lax.rem(at, 2), lax.rem(line, 2)
    sources = (face_1.at[:, line_odd], face_2.at[:, 1 - line_odd], part, a, b, outer)
    buffers = (face_1_vmem, face_2_vmem, *(far_vmem.at[i] for i in range(2 * REACH)))
    stream = Stream(sources, buffers, sems)
    query, grad = mine.at[0], mine.at[1]
    face_1_ok = (line_odd == 1) | (line + 1 < n_height)
    face_2_ok = jnp.where(line_odd == 1, line + 1 < n_height, line > 0)
    slot_at = (2 - odd, 3 - 3 * odd, 3 * odd, 1 + odd)
    rows = [own.shape[1], face_1_vmem.shape[1], face_2_vmem.shape[1]] + [own.shape[1]] * n_picks
    spans = [pl.ds(sum(rows[:i]), count) for i, count in enumerate(rows)]
    left, right = pl.ds(0, HEAD_DIM), pl.ds(HEAD_DIM, HEAD_DIM)

    def chosen(e, p):
        slot = picks[e, p]
        target = at + slot - jnp.where(slot < REACH, REACH, REACH - 1)
        ok = (target >= 0) & (target < n_tm)
        for before in range(p):
            ok &= picks[e, before] != slot
        return ok

    def place(e, p):
        return sum(jnp.where(picks[e, p] == slot, i, 0) for i, slot in enumerate(slot_at))

    def blocks(e, which):
        cols = columns(e)
        far = [far_vmem[place(e, p), which, :, cols] for p in range(n_picks)]
        return [own[which, :, cols], face_1_vmem[which, :, cols], face_2_vmem[which, :, cols], *far]

    def products(e):
        stream.ready(e)
        both = corners(query[:, columns(e)], grad[:, columns(e)])
        for key, value, span in zip(blocks(e, 0), blocks(e, 1), spans):
            scratch[e % 2, span, :] = dot(jnp.concatenate([key, value], axis=1), both, NT)

    def softmax(e):
        present = [None, face_1_ok, face_2_ok] + [chosen(e, p) for p in range(n_picks)]
        score = [scratch.at[e % 2, span, left] for span in spans]
        grad_weight = [scratch.at[e % 2, span, right] for span in spans]
        tops = [jnp.max(s[...], axis=0, keepdims=True) for s in score]
        tops = [t if ok is None else jnp.where(ok, t, -jnp.inf) for t, ok in zip(tops, present)]
        top = functools.reduce(jnp.maximum, tops) * (SCALE * LOG2E)
        expo = [
            jnp.exp2(s[...] * (SCALE * LOG2E) - (top if ok is None else jnp.where(ok, top, FAR_AWAY)))
            for s, ok in zip(score, present)
        ]
        total = sum(jnp.sum(x, axis=0, keepdims=True) for x in expo)
        inverse = 1.0 / total
        delta = sum(jnp.sum(x * w[...], axis=0, keepdims=True) for x, w in zip(expo, grad_weight))
        delta, level = delta * inverse, top + jnp.log2(total)
        stats[0, e : e + 1, :] = delta
        for i, slot in enumerate(slot_at):
            ok = [present[3 + p] & (picks[e, p] == slot) for p in range(n_picks)]
            stats[1 + i, e : e + 1, :] = jnp.where(functools.reduce(jnp.logical_or, ok), level, FAR_AWAY)
        for i, (x, w, span) in enumerate(zip(expo, grad_weight, spans)):
            weights = x * inverse
            graded[e % 2, span, left] = (weights * (w[...] - delta) * SCALE).astype(jnp.bfloat16)
            if i < 3:
                graded[e % 2, span, right] = weights.astype(jnp.bfloat16)

    def gradients(e):
        cols = columns(e)
        dq = dot(graded[e % 2, :, left], jnp.concatenate(blocks(e, 0), axis=0), TN)
        grad_query[:, cols] = dq.astype(grad_query.dtype)
        both = corners(query[:, cols], grad[:, cols])
        for out, span in zip((own_grads, face_1_grads, face_2_grads), spans):
            grads = dot(graded[e % 2, span, :], both, NN)
            out[0, :, cols] = grads[:, :HEAD_DIM].astype(out.dtype)
            out[1, :, cols] = grads[:, HEAD_DIM:].astype(out.dtype)

    for step in range(heads + 2):
        if step < heads:
            products(step)
        if 0 <= step - 1 < heads:
            softmax(step - 1)
        if 0 <= step - 2:
            gradients(step - 2)


def key_kernel(
    keys, own_grads, face_1_grads, face_2_grads, part, a, b, outer, of_part, of_a, of_b,
    grad_key, grad_value, scratch,
):
    heads, face = keys.shape[2] // HEAD_DIM, face_1_grads.shape[1]
    last_first = lax.rem(lax.axis_index("height"), 2) == 0
    others = ((part, of_part.at[0], 1), (a, of_a, 3), (b, of_b, 2), (outer, of_part.at[1], 4))

    def products(e):
        cols = columns(e)
        pair = jnp.concatenate([keys[0, :, cols], keys[1, :, cols]], axis=1)
        for i, (block, _, _) in enumerate(others):
            scratch[e % 2, i] = dot(pair, corners(block[0, :, cols], block[1, :, cols]), NT)

    def finish(e):
        cols = columns(e)
        sums = jnp.concatenate([own_grads[0, :, cols], own_grads[1, :, cols]], axis=1)
        for i, (block, stats, slot) in enumerate(others):
            score, grad_weights = scratch[e % 2, i, :, :HEAD_DIM], scratch[e % 2, i, :, HEAD_DIM:]
            weights = jnp.exp2(score * (SCALE * LOG2E) - stats[slot, e : e + 1, :])
            dscore = weights * (grad_weights - stats[0, e : e + 1, :]) * SCALE
            both = jnp.concatenate([dscore.astype(jnp.bfloat16), weights.astype(jnp.bfloat16)], axis=1)
            sums += dot(both, corners(block[0, :, cols], block[1, :, cols]), NN)
        for at, out in ((0, grad_key), (1, grad_value)):
            one = face_1_grads[at, :, cols].astype(jnp.float32)
            two = face_2_grads[at, :, cols].astype(jnp.float32)
            first, last = jnp.where(last_first, two, one), jnp.where(last_first, one, two)
            part_sum = sums[:, at * HEAD_DIM : (at + 1) * HEAD_DIM]
            out[:face, cols] = (part_sum[:face] + first).astype(out.dtype)
            out[face:, cols] = (part_sum[face:] + last).astype(out.dtype)

    products(0)
    for e in range(heads):
        if e + 1 < heads:
            products(e + 1)
        finish(e)


def per_device(query_tok, key_tok, value_tok, grad_out, far_picks):
    frames_dev, rows_dev, columns, width = query_tok.shape
    tile, face = frames_dev * rows_dev * columns, frames_dev * columns
    heads, n_picks = width // HEAD_DIM, far_picks.shape[3]
    n_tm, n_height = lax.axis_size("tm"), lax.axis_size("height")
    query, key = query_tok.reshape(tile, width), key_tok.reshape(tile, width)
    value, grad = value_tok.reshape(tile, width), grad_out.reshape(tile, width)
    partner, route_a, route_b, outer = routes(n_tm)
    relayed = n_tm % 2 == 0
    pairs_1 = [(i, i ^ 1) for i in range(n_height) if i ^ 1 < n_height]
    pairs_2 = [(i, i - 1 if i % 2 == 0 else i + 1) for i in range(n_height)]
    pairs_2 = [(i, j) for i, j in pairs_2 if 0 <= j < n_height]

    def move(block, route):
        return lax.ppermute(block, "tm", route)

    key_value, query_grad = paired(key, value, query, grad)
    kv_part, kv_b = move(key_value, partner), move(key_value, route_b)
    kv_a = move(after(key_value, kv_part), route_a)
    face_1 = lax.ppermute(key_value, "height", pairs_1)
    face_2 = lax.ppermute(key_value, "height", pairs_2)
    qg_part = move(after(query_grad, kv_part), partner)
    qg_a = move(query_grad, route_a)
    kv_outer = move(after(kv_part, face_1, face_2), route_b) if relayed else move(key_value, outer)
    qg_b = move(after(query_grad, kv_b), route_b)
    qg_outer = move(qg_a, partner) if relayed else move(query_grad, outer)

    f32, bf16 = jnp.float32, jnp.bfloat16
    vmem, hbm = pl.BlockSpec(memory_space=pltpu.VMEM), pl.BlockSpec(memory_space=pltpu.HBM)
    block = 2 * tile * tile * HEAD_DIM * heads
    params = pltpu.CompilerParams(vmem_limit_bytes=VMEM_BYTES)
    by_row = (2, rows_dev, face, width)
    grad_query, own_grads, face_1_grads, face_2_grads, stats = pl.pallas_call(
        functools.partial(query_kernel, n_tm, n_height),
        out_shape=(
            jax.ShapeDtypeStruct((tile, width), bf16),
            jax.ShapeDtypeStruct((2, tile, width), f32),
            jax.ShapeDtypeStruct((2, face, width), bf16),
            jax.ShapeDtypeStruct((2, face, width), bf16),
            jax.ShapeDtypeStruct((1 + 2 * REACH, heads, tile), f32),
        ),
        in_specs=[vmem] * 2 + [hbm] * 6 + [pl.BlockSpec(memory_space=pltpu.SMEM)],
        out_specs=[vmem] * 5,
        scratch_shapes=[
            pltpu.VMEM((2, tile * (1 + n_picks) + 2 * face, 2 * HEAD_DIM), f32),
            pltpu.VMEM((2, tile * (1 + n_picks) + 2 * face, 2 * HEAD_DIM), bf16),
            *[pltpu.VMEM((2, face, width), bf16)] * 2,
            pltpu.VMEM((2 * REACH, 2, tile, width), bf16),
            stream_sems(heads, 2 + 2 * REACH),
        ],
        compiler_params=params,
        cost_estimate=pl.CostEstimate(flops=200 * block, bytes_accessed=4 << 20, transcendentals=0),
        name="query_side",
    )(query_grad, key_value, in_hbm(face_1.reshape(by_row)), in_hbm(face_2.reshape(by_row)),
      in_hbm(kv_part), in_hbm(kv_a), in_hbm(kv_b), in_hbm(kv_outer),
      far_picks.reshape(heads, n_picks))

    of_a, of_b = move(stats, route_a), move(stats, route_b)
    of_part = move(jnp.stack([stats, of_a]), partner)
    if not relayed:
        of_part = jnp.stack([of_part[0], move(stats, outer)])
    back_1 = lax.ppermute(face_1_grads, "height", pairs_1)
    back_2 = lax.ppermute(face_2_grads, "height", pairs_2)

    grad_key, grad_value = pl.pallas_call(
        key_kernel,
        out_shape=(jax.ShapeDtypeStruct((tile, width), bf16),) * 2,
        in_specs=[vmem] * 11,
        out_specs=[vmem] * 2,
        scratch_shapes=[pltpu.VMEM((2, 2 * REACH, tile, 2 * HEAD_DIM), f32)],
        compiler_params=params,
        cost_estimate=pl.CostEstimate(flops=100 * block, bytes_accessed=4 << 20, transcendentals=0),
        name="key_side",
    )(key_value, own_grads, back_1, back_2, qg_part, qg_a, qg_b, qg_outer, of_part, of_a, of_b)
    return tuple(x.reshape(query_tok.shape) for x in (grad_query, grad_key, grad_value))


def solution(mesh):
    spec = P("tm", "height", None, None)
    return jax.shard_map(
        per_device, mesh=mesh, in_specs=(spec,) * 5, out_specs=(spec,) * 3, check_vma=False
    )
```

time: 95 us -> 74.9 us (0.79)
  the two profiles are of different devices: /device:TPU:22 before, /device:TPU:1 now
where the time goes in v3:
time: 74.9 us; the launch traced here: 74.5 us
  waiting for transfers between devices  31.2 us (42%)
  starting transfers between devices  29.6 us (40%)
  Pallas kernels  12.8 us (17%)
  between operations  0.8 us (1%)
    ppermute x11, waiting for transfers between devices, move(): return lax.ppermute(block, 'tm', route)  29.3 us
    ppermute x11, starting transfers between devices, move(): return lax.ppermute(block, 'tm', route)  21 us
    pallas_call x1, Pallas kernels, per_device(): pl.pallas_call(functools.partial(query_kernel, n_tm, n_height), out_shape...  7.46 us
    ppermute x1, starting transfers between devices, per_device(): back_2 = lax.ppermute(face_2_grads, 'height', pairs_2)  3.85 us
    pallas_call x1, Pallas kernels, per_device(): pl.pallas_call(key_kernel, out_shape=(jax.ShapeDtypeStruct((tile, width),...  3.77 us
    ppermute x1, starting transfers between devices, per_device(): face_2 = lax.ppermute(key_value, 'height', pairs_2)  3.02 us
    ppermute x1, waiting for transfers between devices, per_device(): back_2 = lax.ppermute(face_2_grads, 'height', pairs_2)  1.91 us
    pallas_call x1, Pallas kernels, paired(): pl.pallas_call(pair_kernel, out_shape=(jax.ShapeDtypeStruct((2, rows, wid...  1.6 us
  transfers between devices with their start and end apart: 15, of which 7 were waited for; matrix products, arithmetic and copies ran while one was open for 0% of the time, Pallas kernels for 10%

profile of v3, /device:TPU:1, one launch (start us, length us, event | category | flops | bytes accessed | tf_op | source)
XLA Modules:
  0.0 74.5 jit_solution(5459512077082034935)
XLA Ops:
  0.6 0.0 copy-start
  0.6 1.6 %pairs.1 = (bf16[2,128,1536]{2,1,0:T(8,128)(2,1)S(1)}, bf16[2,128,1536]{2,1,0:T(8,128)(2,1)S(1)}) custom-call(bf16[128,1536]{1,0:T(8,128)(2,1)} %bitcast.14, bf16[128,1536]{1,0:T(8,128)(2,1)} %bitcast.15, bf16[128,1536]{1,0:T(8,128)(2,1)} %bitcast.16, bf16[128,1536]{1,0:T(8,128)(2,1)} %bitcast.17), custom_call_target="tpu_custom_call" | custom-call | bytes 3145728 | tf_op jit(solution)/shard_map/pairs/pallas_call | solution.py:73
  2.2 2.1 %collective-permute-start.2 = (bf16[2,128,1536]{2,1,0:T(8,128)(2,1)S(1)}, bf16[2,128,1536]{2,1,0:T(8,128)(2,1)S(1)}, u32[]{:S(2)}, u32[]{:S(2)}) collective-permute-start(bf16[2,128,1536]{2,1,0:T(8,128)(2,1)S(1)} %get-tuple-element.18.own.keys), channel_id=1, source_target_pairs={{0,4},{4,0},{8,12},{12,8},{16,20},{20,16},{24,28},{28,24},{1,5},{5... | collective-permute-start | bytes 2359304 | tf_op jit(solution)/shard_map/ppermute | solution.py:248
  4.4 1.0 %collective-permute-start = (bf16[2,128,1536]{2,1,0:T(8,128)(2,1)S(1)}, bf16[2,128,1536]{2,1,0:T(8,128)(2,1)S(1)}, u32[]{:S(2)}, u32[]{:S(2)}) collective-permute-start(bf16[2,128,1536]{2,1,0:T(8,128)(2,1)S(1)} %get-tuple-element.18.own.keys), channel_id=1, source_target_pairs={{0,1},{1,0},{2,3},{3,2},{4,5},{5,4},{6,7},{7,6},{8,9},{9,8},{10,11... | collective-permute-start | bytes 2359304 | tf_op jit(solution)/shard_map/ppermute | solution.py:253
  5.3 3.0 %collective-permute-start.1 = (bf16[2,128,1536]{2,1,0:T(8,128)(2,1)S(1)}, bf16[2,128,1536]{2,1,0:T(8,128)(2,1)S(1)}, u32[]{:S(2)}, u32[]{:S(2)}) collective-permute-start(bf16[2,128,1536]{2,1,0:T(8,128)(2,1)S(1)} %get-tuple-element.18.own.keys), channel_id=1, source_target_pairs={{1,2},{2,1},{5,6},{6,5},{9,10},{10,9},{13,14},{14,13},{17,18},{18,... | collective-permute-start | bytes 2359304 | tf_op jit(solution)/shard_map/ppermute | solution.py:254
  8.3 4.1 %collective-permute-start.4 = (bf16[2,128,1536]{2,1,0:T(8,128)(2,1)S(1)}, bf16[2,128,1536]{2,1,0:T(8,128)(2,1)}, u32[]{:S(2)}, u32[]{:S(2)}) collective-permute-start(bf16[2,128,1536]{2,1,0:T(8,128)(2,1)S(1)} %get-tuple-element.18.own.keys), channel_id=1, source_target_pairs={{0,8},{8,16},{12,4},{16,24},{20,12},{28,20},{1,9},{9,17},{13,5},{1... | collective-permute-start | bytes 2359304 | tf_op jit(solution)/shard_map/ppermute | solution.py:248
  12.4 1.3 %collective-permute-start.9 = (bf16[2,128,1536]{2,1,0:T(8,128)(2,1)S(1)}, bf16[2,128,1536]{2,1,0:T(8,128)(2,1)S(1)}, u32[]{:S(2)}, u32[]{:S(2)}) collective-permute-start(bf16[2,128,1536]{2,1,0:T(8,128)(2,1)S(1)} %get-tuple-element.25.mine), channel_id=1, source_target_pairs={{4,12},{8,0},{12,20},{16,8},{20,28},{24,16},{5,13},{9,1},{13,21},{... | collective-permute-start | bytes 2359304 | tf_op jit(solution)/shard_map/ppermute | solution.py:248
  13.7 7.9 %collective-permute-done.2.part = bf16[2,128,1536]{2,1,0:T(8,128)(2,1)S(1)} collective-permute-done((bf16[2,128,1536]{2,1,0:T(8,128)(2,1)S(1)}, bf16[2,128,1536]{2,1,0:T(8,128)(2,1)S(1)}, u32[]{:S(2)}, u32[]{:S(2)}) %collective-permute-start.2) | collective-permute-done | bytes 786464 | tf_op jit(solution)/shard_map/ppermute | solution.py:248
  21.6 0.0 copy-start.1
  21.6 0.0 collective-permute-done
  21.6 0.0 copy-start.2
  21.6 0.0 collective-permute-done.1
  21.6 0.0 copy-start.3
  21.6 4.1 %collective-permute-start.5 = (bf16[2,128,1536]{2,1,0:T(8,128)(2,1)S(1)}, bf16[2,128,1536]{2,1,0:T(8,128)(2,1)}, u32[]{:S(2)}, u32[]{:S(2)}) collective-permute-start(bf16[2,128,1536]{2,1,0:T(8,128)(2,1)S(1)} %collective-permute-done.2.part), channel_id=1, source_target_pairs={{0,8},{8,16},{12,4},{16,24},{20,12},{28,20},{1,9},{9,17},{13,5},{1... | collective-permute-start | bytes 2359304 | tf_op jit(solution)/shard_map/ppermute | solution.py:248
  25.8 1.3 %collective-permute-start.3 = (bf16[2,128,1536]{2,1,0:T(8,128)(2,1)S(1)}, bf16[2,128,1536]{2,1,0:T(8,128)(2,1)}, u32[]{:S(2)}, u32[]{:S(2)}) collective-permute-start(bf16[2,128,1536]{2,1,0:T(8,128)(2,1)S(1)} %get-tuple-element.18.own.keys), channel_id=1, source_target_pairs={{4,12},{8,0},{12,20},{16,8},{20,28},{24,16},{5,13},{9,1},{13,21},{... | collective-permute-start | bytes 2359304 | tf_op jit(solution)/shard_map/ppermute | solution.py:248
  27.1 0.0 copy-done.2
  27.1 0.0 copy-done.3
  27.1 0.0 copy-done
  27.1 0.1 copy.8.picks
  27.2 2.0 %collective-permute-start.8 = (bf16[2,128,1536]{2,1,0:T(8,128)(2,1)S(1)}, bf16[2,128,1536]{2,1,0:T(8,128)(2,1)S(1)}, u32[]{:S(2)}, u32[]{:S(2)}) collective-permute-start(bf16[2,128,1536]{2,1,0:T(8,128)(2,1)S(1)} %get-tuple-element.25.mine), channel_id=1, source_target_pairs={{0,4},{4,0},{8,12},{12,8},{16,20},{20,16},{24,28},{28,24},{1,5},{5... | collective-permute-start | bytes 2359304 | tf_op jit(solution)/shard_map/ppermute | solution.py:248
  29.2 0.0 collective-permute-done.4.b
  29.2 2.4 %collective-permute-start.10 = (bf16[2,128,1536]{2,1,0:T(8,128)(2,1)S(1)}, bf16[2,128,1536]{2,1,0:T(8,128)(2,1)S(1)}, u32[]{:S(2)}, u32[]{:S(2)}) collective-permute-start(bf16[2,128,1536]{2,1,0:T(8,128)(2,1)S(1)} %get-tuple-element.25.mine), channel_id=1, source_target_pairs={{0,8},{8,16},{12,4},{16,24},{20,12},{28,20},{1,9},{9,17},{13,5},{1... | collective-permute-start | bytes 2359304 | tf_op jit(solution)/shard_map/ppermute | solution.py:248
  31.6 0.4 collective-permute-done.9.a
  32.0 0.0 collective-permute-start.11
  32.0 11.6 %collective-permute-done.5.outer = bf16[2,128,1536]{2,1,0:T(8,128)(2,1)} collective-permute-done((bf16[2,128,1536]{2,1,0:T(8,128)(2,1)S(1)}, bf16[2,128,1536]{2,1,0:T(8,128)(2,1)}, u32[]{:S(2)}, u32[]{:S(2)}) %collective-permute-start.5) | collective-permute-done | bytes 786464 | tf_op jit(solution)/shard_map/ppermute | solution.py:248
  43.6 5.4 %collective-permute-done.3.a = bf16[2,128,1536]{2,1,0:T(8,128)(2,1)} collective-permute-done((bf16[2,128,1536]{2,1,0:T(8,128)(2,1)S(1)}, bf16[2,128,1536]{2,1,0:T(8,128)(2,1)}, u32[]{:S(2)}, u32[]{:S(2)}) %collective-permute-start.3) | collective-permute-done | bytes 786464 | tf_op jit(solution)/shard_map/ppermute | solution.py:248
  48.9 0.0 copy-done.1
  48.9 7.5 %query_side.1 = (bf16[128,1536]{1,0:T(8,128)(2,1)}, f32[2,128,1536]{2,1,0:T(8,128)S(1)}, bf16[2,64,1536]{2,1,0:T(8,128)(2,1)S(1)}, bf16[2,64,1536]{2,1,0:T(8,128)(2,1)S(1)}, f32[5,12,128]{2,1,0:T(8,128)S(1)}) custom-call(bf16[2,128,1536]{2,1,0:T(8,128)(2,1)S(1)} %get-tuple-element.25.mine, bf16[2,128,1536]{2,1,0:T(8,128)(2,1)S(1)} %get-tuple-element.18.own.keys, ...), custom_call_target="tpu_custom_call" | custom-call | flops 10066329600 | bytes 4194304 | tf_op jit(solution)/shard_map/query_side/pallas_call | solution.py:266
  56.4 1.3 %collective-permute-start.12 = (f32[5,12,128]{2,1,0:T(8,128)S(1)}, f32[5,12,128]{2,1,0:T(8,128)S(1)}, u32[]{:S(2)}, u32[]{:S(2)}) collective-permute-start(f32[5,12,128]{2,1,0:T(8,128)S(1)} %get-tuple-element.26), channel_id=1, source_target_pairs={{4,12},{8,0},{12,20},{16,8},{20,28},{24,16},{5,13},{9,1},{13,21},{... | collective-permute-start | bytes 92168 | tf_op jit(solution)/shard_map/ppermute | solution.py:248
  57.7 0.8 %collective-permute-start.6 = (bf16[2,64,1536]{2,1,0:T(8,128)(2,1)S(1)}, bf16[2,64,1536]{2,1,0:T(8,128)(2,1)S(1)}, u32[]{:S(2)}, u32[]{:S(2)}) collective-permute-start(bf16[2,64,1536]{2,1,0:T(8,128)(2,1)S(1)} %get-tuple-element.22), channel_id=1, source_target_pairs={{0,1},{1,0},{2,3},{3,2},{4,5},{5,4},{6,7},{7,6},{8,9},{9,8},{10,11... | collective-permute-start | bytes 1179656 | tf_op jit(solution)/shard_map/ppermute | solution.py:295
  58.5 3.0 %collective-permute-done.12.of_a = f32[5,12,128]{2,1,0:T(8,128)S(1)} collective-permute-done((f32[5,12,128]{2,1,0:T(8,128)S(1)}, f32[5,12,128]{2,1,0:T(8,128)S(1)}, u32[]{:S(2)}, u32[]{:S(2)}) %collective-permute-start.12) | collective-permute-done | bytes 30752 | tf_op jit(solution)/shard_map/ppermute | solution.py:248
  61.4 3.9 %collective-permute-start.7 = (bf16[2,64,1536]{2,1,0:T(8,128)(2,1)S(1)}, bf16[2,64,1536]{2,1,0:T(8,128)(2,1)S(1)}, u32[]{:S(2)}, u32[]{:S(2)}) collective-permute-start(bf16[2,64,1536]{2,1,0:T(8,128)(2,1)S(1)} %get-tuple-element.23), channel_id=1, source_target_pairs={{1,2},{2,1},{5,6},{6,5},{9,10},{10,9},{13,14},{14,13},{17,18},{18,... | collective-permute-start | bytes 1179656 | tf_op jit(solution)/shard_map/ppermute | solution.py:296
  65.3 0.0 collective-permute-done.8.part
  65.3 0.1 collective-permute-start.13
  65.4 0.0 collective-permute-done.10.b
  65.4 2.3 %collective-permute-start.14 = (f32[5,12,128]{2,1,0:T(8,128)S(1)}, f32[5,12,128]{2,1,0:T(8,128)S(1)}, u32[]{:S(2)}, u32[]{:S(2)}) collective-permute-start(f32[5,12,128]{2,1,0:T(8,128)S(1)} %get-tuple-element.26), channel_id=1, source_target_pairs={{0,8},{8,16},{12,4},{16,24},{20,12},{28,20},{1,9},{9,17},{13,5},{1... | collective-permute-start | bytes 92168 | tf_op jit(solution)/shard_map/ppermute | solution.py:248
  67.8 0.0 collective-permute-done.11.outer
  67.8 1.1 %collective-permute-done.14.of_b = f32[5,12,128]{2,1,0:T(8,128)S(1)} collective-permute-done((f32[5,12,128]{2,1,0:T(8,128)S(1)}, f32[5,12,128]{2,1,0:T(8,128)S(1)}, u32[]{:S(2)}, u32[]{:S(2)}) %collective-permute-start.14) | collective-permute-done | bytes 30752 | tf_op jit(solution)/shard_map/ppermute | solution.py:248
  68.8 0.0 collective-permute-done.13.of_part
  68.8 0.0 collective-permute-done.6.face_1_grads
  68.8 1.9 %collective-permute-done.7.face_2_grads = bf16[2,64,1536]{2,1,0:T(8,128)(2,1)S(1)} collective-permute-done((bf16[2,64,1536]{2,1,0:T(8,128)(2,1)S(1)}, bf16[2,64,1536]{2,1,0:T(8,128)(2,1)S(1)}, u32[]{:S(2)}, u32[]{:S(2)}) %collective-permute-start.7) | collective-permute-done | bytes 393248 | tf_op jit(solution)/shard_map/ppermute | solution.py:296
  70.8 3.8 %key_side.1 = (bf16[128,1536]{1,0:T(8,128)(2,1)}, bf16[128,1536]{1,0:T(8,128)(2,1)}) custom-call(bf16[2,128,1536]{2,1,0:T(8,128)(2,1)S(1)} %get-tuple-element.18.own.keys, f32[2,128,1536]{2,1,0:T(8,128)S(1)} %get-tuple-element.21.own_grads, bf16[2,64,1536]{2,1,0:T(8,128)(2,1)S(1)} %collective-permute-done.6.face_1_grads, ...), custom_call_target="tpu_custom_call" | custom-call | flops 5033164800 | bytes 4194304 | tf_op jit(solution)/shard_map/key_side/pallas_call | solution.py:298
  (1 shorter events, 0.0 us)
Async XLA Ops:
  0.6 26.5 %copy-start = (s32[1,1,12,2]{2,3,1,0:T(2,128)S(1)}, s32[1,1,12,2]{2,3,1,0:T(2,128)}, u32[]{:S(2)}) copy-start(s32[1,1,12,2]{2,3,1,0:T(2,128)} %param.9) | copy-start | bytes 292
  2.2 19.4 %collective-permute-start.2 = (bf16[2,128,1536]{2,1,0:T(8,128)(2,1)S(1)}, bf16[2,128,1536]{2,1,0:T(8,128)(2,1)S(1)}, u32[]{:S(2)}, u32[]{:S(2)}) collective-permute-start(bf16[2,128,1536]{2,1,0:T(8,128)(2,1)S(1)} %get-tuple-element.18.own.keys), channel_id=1, source_target_pairs={{0,4},{4,0},{8,12},{12,8},{16,20},{20,16},{24,28},{28,24},{1,5},{5... | collective-permute-start | bytes 2359304 | tf_op jit(solution)/shard_map/ppermute | solution.py:248
  4.4 17.3 %collective-permute-start = (bf16[2,128,1536]{2,1,0:T(8,128)(2,1)S(1)}, bf16[2,128,1536]{2,1,0:T(8,128)(2,1)S(1)}, u32[]{:S(2)}, u32[]{:S(2)}) collective-permute-start(bf16[2,128,1536]{2,1,0:T(8,128)(2,1)S(1)} %get-tuple-element.18.own.keys), channel_id=1, source_target_pairs={{0,1},{1,0},{2,3},{3,2},{4,5},{5,4},{6,7},{7,6},{8,9},{9,8},{10,11... | collective-permute-start | bytes 2359304 | tf_op jit(solution)/shard_map/ppermute | solution.py:253
  5.3 16.3 %collective-permute-start.1 = (bf16[2,128,1536]{2,1,0:T(8,128)(2,1)S(1)}, bf16[2,128,1536]{2,1,0:T(8,128)(2,1)S(1)}, u32[]{:S(2)}, u32[]{:S(2)}) collective-permute-start(bf16[2,128,1536]{2,1,0:T(8,128)(2,1)S(1)} %get-tuple-element.18.own.keys), channel_id=1, source_target_pairs={{1,2},{2,1},{5,6},{6,5},{9,10},{10,9},{13,14},{14,13},{17,18},{18,... | collective-permute-start | bytes 2359304 | tf_op jit(solution)/shard_map/ppermute | solution.py:254
  8.3 20.8 %collective-permute-start.4 = (bf16[2,128,1536]{2,1,0:T(8,128)(2,1)S(1)}, bf16[2,128,1536]{2,1,0:T(8,128)(2,1)}, u32[]{:S(2)}, u32[]{:S(2)}) collective-permute-start(bf16[2,128,1536]{2,1,0:T(8,128)(2,1)S(1)} %get-tuple-element.18.own.keys), channel_id=1, source_target_pairs={{0,8},{8,16},{12,4},{16,24},{20,12},{28,20},{1,9},{9,17},{13,5},{1... | collective-permute-start | bytes 2359304 | tf_op jit(solution)/shard_map/ppermute | solution.py:248
  12.4 19.6 %collective-permute-start.9 = (bf16[2,128,1536]{2,1,0:T(8,128)(2,1)S(1)}, bf16[2,128,1536]{2,1,0:T(8,128)(2,1)S(1)}, u32[]{:S(2)}, u32[]{:S(2)}) collective-permute-start(bf16[2,128,1536]{2,1,0:T(8,128)(2,1)S(1)} %get-tuple-element.25.mine), channel_id=1, source_target_pairs={{4,12},{8,0},{12,20},{16,8},{20,28},{24,16},{5,13},{9,1},{13,21},{... | collective-permute-start | bytes 2359304 | tf_op jit(solution)/shard_map/ppermute | solution.py:248
  21.6 27.3 %copy-start.1 = (bf16[2,128,1536]{2,1,0:T(8,128)(2,1)}, bf16[2,128,1536]{2,1,0:T(8,128)(2,1)S(1)}, u32[]{:S(2)}) copy-start(bf16[2,128,1536]{2,1,0:T(8,128)(2,1)S(1)} %collective-permute-done.2.part) | copy-start | bytes 2359300
  21.6 5.4 %copy-start.2 = (bf16[2,128,1536]{2,1,0:T(8,128)(2,1)}, bf16[2,128,1536]{2,1,0:T(8,128)(2,1)S(1)}, u32[]{:S(2)}) copy-start(bf16[2,128,1536]{2,1,0:T(8,128)(2,1)S(1)} %collective-permute-done) | copy-start | bytes 2359300
  21.6 5.4 %copy-start.3 = (bf16[2,128,1536]{2,1,0:T(8,128)(2,1)}, bf16[2,128,1536]{2,1,0:T(8,128)(2,1)S(1)}, u32[]{:S(2)}) copy-start(bf16[2,128,1536]{2,1,0:T(8,128)(2,1)S(1)} %collective-permute-done.1) | copy-start | bytes 2359300
  21.6 21.9 %collective-permute-start.5 = (bf16[2,128,1536]{2,1,0:T(8,128)(2,1)S(1)}, bf16[2,128,1536]{2,1,0:T(8,128)(2,1)}, u32[]{:S(2)}, u32[]{:S(2)}) collective-permute-start(bf16[2,128,1536]{2,1,0:T(8,128)(2,1)S(1)} %collective-permute-done.2.part), channel_id=1, source_target_pairs={{0,8},{8,16},{12,4},{16,24},{20,12},{28,20},{1,9},{9,17},{13,5},{1... | collective-permute-start | bytes 2359304 | tf_op jit(solution)/shard_map/ppermute | solution.py:248
  25.8 23.2 %collective-permute-start.3 = (bf16[2,128,1536]{2,1,0:T(8,128)(2,1)S(1)}, bf16[2,128,1536]{2,1,0:T(8,128)(2,1)}, u32[]{:S(2)}, u32[]{:S(2)}) collective-permute-start(bf16[2,128,1536]{2,1,0:T(8,128)(2,1)S(1)} %get-tuple-element.18.own.keys), channel_id=1, source_target_pairs={{4,12},{8,0},{12,20},{16,8},{20,28},{24,16},{5,13},{9,1},{13,21},{... | collective-permute-start | bytes 2359304 | tf_op jit(solution)/shard_map/ppermute | solution.py:248
  27.2 38.1 %collective-permute-start.8 = (bf16[2,128,1536]{2,1,0:T(8,128)(2,1)S(1)}, bf16[2,128,1536]{2,1,0:T(8,128)(2,1)S(1)}, u32[]{:S(2)}, u32[]{:S(2)}) collective-permute-start(bf16[2,128,1536]{2,1,0:T(8,128)(2,1)S(1)} %get-tuple-element.25.mine), channel_id=1, source_target_pairs={{0,4},{4,0},{8,12},{12,8},{16,20},{20,16},{24,28},{28,24},{1,5},{5... | collective-permute-start | bytes 2359304 | tf_op jit(solution)/shard_map/ppermute | solution.py:248
  29.2 36.2 %collective-permute-start.10 = (bf16[2,128,1536]{2,1,0:T(8,128)(2,1)S(1)}, bf16[2,128,1536]{2,1,0:T(8,128)(2,1)S(1)}, u32[]{:S(2)}, u32[]{:S(2)}) collective-permute-start(bf16[2,128,1536]{2,1,0:T(8,128)(2,1)S(1)} %get-tuple-element.25.mine), channel_id=1, source_target_pairs={{0,8},{8,16},{12,4},{16,24},{20,12},{28,20},{1,9},{9,17},{13,5},{1... | collective-permute-start | bytes 2359304 | tf_op jit(solution)/shard_map/ppermute | solution.py:248
  32.0 35.8 %collective-permute-start.11 = (bf16[2,128,1536]{2,1,0:T(8,128)(2,1)S(1)}, bf16[2,128,1536]{2,1,0:T(8,128)(2,1)S(1)}, u32[]{:S(2)}, u32[]{:S(2)}) collective-permute-start(bf16[2,128,1536]{2,1,0:T(8,128)(2,1)S(1)} %collective-permute-done.9.a), channel_id=1, source_target_pairs={{0,4},{4,0},{8,12},{12,8},{16,20},{20,16},{24,28},{28,24},{1,5},{5... | collective-permute-start | bytes 2359304 | tf_op jit(solution)/shard_map/ppermute | solution.py:248
  56.4 5.0 %collective-permute-start.12 = (f32[5,12,128]{2,1,0:T(8,128)S(1)}, f32[5,12,128]{2,1,0:T(8,128)S(1)}, u32[]{:S(2)}, u32[]{:S(2)}) collective-permute-start(f32[5,12,128]{2,1,0:T(8,128)S(1)} %get-tuple-element.26), channel_id=1, source_target_pairs={{4,12},{8,0},{12,20},{16,8},{20,28},{24,16},{5,13},{9,1},{13,21},{... | collective-permute-start | bytes 92168 | tf_op jit(solution)/shard_map/ppermute | solution.py:248
  57.7 11.1 %collective-permute-start.6 = (bf16[2,64,1536]{2,1,0:T(8,128)(2,1)S(1)}, bf16[2,64,1536]{2,1,0:T(8,128)(2,1)S(1)}, u32[]{:S(2)}, u32[]{:S(2)}) collective-permute-start(bf16[2,64,1536]{2,1,0:T(8,128)(2,1)S(1)} %get-tuple-element.22), channel_id=1, source_target_pairs={{0,1},{1,0},{2,3},{3,2},{4,5},{5,4},{6,7},{7,6},{8,9},{9,8},{10,11... | collective-permute-start | bytes 1179656 | tf_op jit(solution)/shard_map/ppermute | solution.py:295
  61.4 9.3 %collective-permute-start.7 = (bf16[2,64,1536]{2,1,0:T(8,128)(2,1)S(1)}, bf16[2,64,1536]{2,1,0:T(8,128)(2,1)S(1)}, u32[]{:S(2)}, u32[]{:S(2)}) collective-permute-start(bf16[2,64,1536]{2,1,0:T(8,128)(2,1)S(1)} %get-tuple-element.23), channel_id=1, source_target_pairs={{1,2},{2,1},{5,6},{6,5},{9,10},{10,9},{13,14},{14,13},{17,18},{18,... | collective-permute-start | bytes 1179656 | tf_op jit(solution)/shard_map/ppermute | solution.py:296
  65.3 3.5 %collective-permute-start.13 = (f32[2,5,12,128]{3,2,1,0:T(8,128)S(1)}, f32[2,5,12,128]{3,2,1,0:T(8,128)S(1)}, u32[]{:S(2)}, u32[]{:S(2)}) collective-permute-start(f32[2,5,12,128]{3,2,1,0:T(8,128)S(1)} %pad_maximum_fusion), channel_id=1, source_target_pairs={{0,4},{4,0},{8,12},{12,8},{16,20},{20,16},{24,28},{28,24},{1,5},{5... | collective-permute-start | bytes 184328 | tf_op jit(solution)/shard_map/ppermute | solution.py:248
  65.4 3.4 %collective-permute-start.14 = (f32[5,12,128]{2,1,0:T(8,128)S(1)}, f32[5,12,128]{2,1,0:T(8,128)S(1)}, u32[]{:S(2)}, u32[]{:S(2)}) collective-permute-start(f32[5,12,128]{2,1,0:T(8,128)S(1)} %get-tuple-element.26), channel_id=1, source_target_pairs={{0,8},{8,16},{12,4},{16,24},{20,12},{28,20},{1,9},{9,17},{13,5},{1... | collective-permute-start | bytes 92168 | tf_op jit(solution)/shard_map/ppermute | solution.py:248

commit v4 on v3

--- a/solution.py
+++ b/solution.py
@@ -85,27 +85,31 @@
 class Stream:
     def __init__(self, sources, buffers, sems):
         heads = buffers[0].shape[2] // HEAD_DIM
-        self.chunks = sems.shape[0]
-        self.step = heads // self.chunks
+        self.starts = stream_starts(heads)
+        self.ends = self.starts[1:] + [heads]
         self.sources, self.buffers, self.sems = sources, buffers, sems
-        for chunk in range(self.chunks):
+        for chunk in range(len(self.starts)):
             for i in range(len(sources)):
                 self.copy(chunk, i).start()
 
     def copy(self, chunk, i):
-        cols = pl.ds(chunk * self.step * HEAD_DIM, self.step * HEAD_DIM)
+        cols = pl.ds(self.starts[chunk] * HEAD_DIM, (self.ends[chunk] - self.starts[chunk]) * HEAD_DIM)
         return pltpu.make_async_copy(
             self.sources[i].at[:, :, cols], self.buffers[i].at[:, :, cols], self.sems.at[chunk, i]
         )
 
     def ready(self, e):
-        if e % self.step == 0:
+        if e in self.starts:
             for i in range(len(self.sources)):
-                self.copy(e // self.step, i).wait()
+                self.copy(self.starts.index(e), i).wait()
+
+
+def stream_starts(heads):
+    return [at for at in (0, 1, 3, 7) if at < heads]
 
 
 def stream_sems(heads, count):
-    return pltpu.SemaphoreType.DMA((4 if heads % 4 == 0 else 1, count))
+    return pltpu.SemaphoreType.DMA((len(stream_starts(heads)), count))
 
 
 def query_kernel(
@@ -251,11 +255,11 @@
     kv_part, kv_b = move(key_value, partner), move(key_value, route_b)
     kv_a = move(after(key_value, kv_part), route_a)
     face_1 = lax.ppermute(key_value, "height", pairs_1)
-    face_2 = lax.ppermute(key_value, "height", pairs_2)
     qg_part = move(after(query_grad, kv_part), partner)
     qg_a = move(query_grad, route_a)
-    kv_outer = move(after(kv_part, face_1, face_2), route_b) if relayed else move(key_value, outer)
+    kv_outer = move(after(kv_part, face_1), route_b) if relayed else move(key_value, outer)
     qg_b = move(after(query_grad, kv_b), route_b)
+    face_2 = lax.ppermute(after(key_value, qg_a), "height", pairs_2)
     qg_outer = move(qg_a, partner) if relayed else move(query_grad, outer)
 
     f32, bf16 = jnp.float32, jnp.bfloat16

time: 74.9 us -> 74.4 us (level)
  waiting for transfers between devices: 31.2 us -> 21.3 us
  starting transfers between devices: 29.6 us -> 39.2 us
    ppermute x11, waiting for transfers between devices: 29.3 us -> 20.4 us  [move(): return lax.ppermute(block, 'tm', route)]
    ppermute x11, starting transfers between devices: 21 us -> 25.3 us  [move(): return lax.ppermute(block, 'tm', route)]
    ppermute x1, starting transfers between devices: 3.85 us -> 5.96 us  [per_device(): back_2 = lax.ppermute(face_2_grads, 'height', pairs_2)]
    ppermute x1, starting transfers between devices: 3.02 us -> 4.76 us  [per_device(): face_2 = lax.ppermute(after(key_value, qg_a), 'height', pairs_2)]
    ppermute x1, starting transfers between devices: 0.78 us -> 2.15 us  [per_device(): back_1 = lax.ppermute(face_1_grads, 'height', pairs_1)]
    ppermute x1, waiting for transfers between devices: 1.91 us -> 0.9 us  [per_device(): back_2 = lax.ppermute(face_2_grads, 'height', pairs_2)]
where the time goes in v4:
time: 74.4 us; the launch traced here: 74 us
  starting transfers between devices  39.2 us (53%)
  waiting for transfers between devices  21.3 us (29%)
  Pallas kernels  12.6 us (17%)
  between operations  0.78 us (1%)
    ppermute x11, starting transfers between devices, move(): return lax.ppermute(block, 'tm', route)  25.3 us
    ppermute x11, waiting for transfers between devices, move(): return lax.ppermute(block, 'tm', route)  20.4 us
    pallas_call x1, Pallas kernels, per_device(): pl.pallas_call(functools.partial(query_kernel, n_tm, n_height), out_shape...  7.25 us
    ppermute x1, starting transfers between devices, per_device(): back_2 = lax.ppermute(face_2_grads, 'height', pairs_2)  5.96 us
    ppermute x1, starting transfers between devices, per_device(): face_2 = lax.ppermute(after(key_value, qg_a), 'height', pairs_2)  4.76 us
    pallas_call x1, Pallas kernels, per_device(): pl.pallas_call(key_kernel, out_shape=(jax.ShapeDtypeStruct((tile, width),...  3.76 us
    ppermute x1, starting transfers between devices, per_device(): back_1 = lax.ppermute(face_1_grads, 'height', pairs_1)  2.15 us
    pallas_call x1, Pallas kernels, paired(): pl.pallas_call(pair_kernel, out_shape=(jax.ShapeDtypeStruct((2, rows, wid...  1.6 us
  transfers between devices with their start and end apart: 15, of which 7 were waited for; matrix products, arithmetic and copies ran while one was open for 0% of the time, Pallas kernels for 10%

profile of v4, /device:TPU:1, one launch (start us, length us, event | category | flops | bytes accessed | tf_op | source)
XLA Modules:
  0.0 74.0 jit_solution(4169151823913379445)
XLA Ops:
  0.6 0.0 copy-start
  0.6 1.6 %pairs.1 = (bf16[2,128,1536]{2,1,0:T(8,128)(2,1)S(1)}, bf16[2,128,1536]{2,1,0:T(8,128)(2,1)S(1)}) custom-call(bf16[128,1536]{1,0:T(8,128)(2,1)} %bitcast.14, bf16[128,1536]{1,0:T(8,128)(2,1)} %bitcast.15, bf16[128,1536]{1,0:T(8,128)(2,1)} %bitcast.16, bf16[128,1536]{1,0:T(8,128)(2,1)} %bitcast.17), custom_call_target="tpu_custom_call" | custom-call | bytes 3145728 | tf_op jit(solution)/shard_map/pairs/pallas_call | solution.py:73
  2.2 2.1 %collective-permute-start.3 = (bf16[2,128,1536]{2,1,0:T(8,128)(2,1)S(1)}, bf16[2,128,1536]{2,1,0:T(8,128)(2,1)S(1)}, u32[]{:S(2)}, u32[]{:S(2)}) collective-permute-start(bf16[2,128,1536]{2,1,0:T(8,128)(2,1)S(1)} %get-tuple-element.20.own.keys), channel_id=1, source_target_pairs={{0,4},{4,0},{8,12},{12,8},{16,20},{20,16},{24,28},{28,24},{1,5},{5... | collective-permute-start | bytes 2359304 | tf_op jit(solution)/shard_map/ppermute | solution.py:252
  4.4 1.0 %collective-permute-start = (bf16[2,128,1536]{2,1,0:T(8,128)(2,1)S(1)}, bf16[2,128,1536]{2,1,0:T(8,128)(2,1)S(1)}, u32[]{:S(2)}, u32[]{:S(2)}) collective-permute-start(bf16[2,128,1536]{2,1,0:T(8,128)(2,1)S(1)} %get-tuple-element.20.own.keys), channel_id=1, source_target_pairs={{0,1},{1,0},{2,3},{3,2},{4,5},{5,4},{6,7},{7,6},{8,9},{9,8},{10,11... | collective-permute-start | bytes 2359304 | tf_op jit(solution)/shard_map/ppermute | solution.py:257
  5.3 1.3 %collective-permute-start.1 = (bf16[2,128,1536]{2,1,0:T(8,128)(2,1)S(1)}, bf16[2,128,1536]{2,1,0:T(8,128)(2,1)S(1)}, u32[]{:S(2)}, u32[]{:S(2)}) collective-permute-start(bf16[2,128,1536]{2,1,0:T(8,128)(2,1)S(1)} %get-tuple-element.27.mine), channel_id=1, source_target_pairs={{4,12},{8,0},{12,20},{16,8},{20,28},{24,16},{5,13},{9,1},{13,21},{... | collective-permute-start | bytes 2359304 | tf_op jit(solution)/shard_map/ppermute | solution.py:252
  6.6 4.9 %collective-permute-start.5 = (bf16[2,128,1536]{2,1,0:T(8,128)(2,1)S(1)}, bf16[2,128,1536]{2,1,0:T(8,128)(2,1)}, u32[]{:S(2)}, u32[]{:S(2)}) collective-permute-start(bf16[2,128,1536]{2,1,0:T(8,128)(2,1)S(1)} %get-tuple-element.20.own.keys), channel_id=1, source_target_pairs={{0,8},{8,16},{12,4},{16,24},{20,12},{28,20},{1,9},{9,17},{13,5},{1... | collective-permute-start | bytes 2359304 | tf_op jit(solution)/shard_map/ppermute | solution.py:252
  11.5 10.1 %collective-permute-done.3.part = bf16[2,128,1536]{2,1,0:T(8,128)(2,1)S(1)} collective-permute-done((bf16[2,128,1536]{2,1,0:T(8,128)(2,1)S(1)}, bf16[2,128,1536]{2,1,0:T(8,128)(2,1)S(1)}, u32[]{:S(2)}, u32[]{:S(2)}) %collective-permute-start.3) | collective-permute-done | bytes 786464 | tf_op jit(solution)/shard_map/ppermute | solution.py:252
  21.6 0.0 copy-start.1
  21.6 0.0 collective-permute-done
  21.6 0.0 copy-start.2
  21.6 4.1 %collective-permute-start.6 = (bf16[2,128,1536]{2,1,0:T(8,128)(2,1)S(1)}, bf16[2,128,1536]{2,1,0:T(8,128)(2,1)}, u32[]{:S(2)}, u32[]{:S(2)}) collective-permute-start(bf16[2,128,1536]{2,1,0:T(8,128)(2,1)S(1)} %collective-permute-done.3.part), channel_id=1, source_target_pairs={{0,8},{8,16},{12,4},{16,24},{20,12},{28,20},{1,9},{9,17},{13,5},{1... | collective-permute-start | bytes 2359304 | tf_op jit(solution)/shard_map/ppermute | solution.py:252
  25.8 1.3 %collective-permute-start.4 = (bf16[2,128,1536]{2,1,0:T(8,128)(2,1)S(1)}, bf16[2,128,1536]{2,1,0:T(8,128)(2,1)}, u32[]{:S(2)}, u32[]{:S(2)}) collective-permute-start(bf16[2,128,1536]{2,1,0:T(8,128)(2,1)S(1)} %get-tuple-element.20.own.keys), channel_id=1, source_target_pairs={{4,12},{8,0},{12,20},{16,8},{20,28},{24,16},{5,13},{9,1},{13,21},{... | collective-permute-start | bytes 2359304 | tf_op jit(solution)/shard_map/ppermute | solution.py:252
  27.0 0.0 collective-permute-done.1.a
  27.1 4.8 %collective-permute-start.2 = (bf16[2,128,1536]{2,1,0:T(8,128)(2,1)S(1)}, bf16[2,128,1536]{2,1,0:T(8,128)(2,1)}, u32[]{:S(2)}, u32[]{:S(2)}) collective-permute-start(bf16[2,128,1536]{2,1,0:T(8,128)(2,1)S(1)} %get-tuple-element.20.own.keys), channel_id=1, source_target_pairs={{1,2},{2,1},{5,6},{6,5},{9,10},{10,9},{13,14},{14,13},{17,18},{18,... | collective-permute-start | bytes 2359304 | tf_op jit(solution)/shard_map/ppermute | solution.py:262
  31.8 0.0 copy-done.2
  31.8 0.0 copy-done
  31.8 0.1 copy.8.picks
  31.9 2.3 %collective-permute-start.9 = (bf16[2,128,1536]{2,1,0:T(8,128)(2,1)S(1)}, bf16[2,128,1536]{2,1,0:T(8,128)(2,1)S(1)}, u32[]{:S(2)}, u32[]{:S(2)}) collective-permute-start(bf16[2,128,1536]{2,1,0:T(8,128)(2,1)S(1)} %get-tuple-element.27.mine), channel_id=1, source_target_pairs={{0,4},{4,0},{8,12},{12,8},{16,20},{20,16},{24,28},{28,24},{1,5},{5... | collective-permute-start | bytes 2359304 | tf_op jit(solution)/shard_map/ppermute | solution.py:252
  34.2 0.0 collective-permute-done.5.b
  34.2 2.4 %collective-permute-start.10 = (bf16[2,128,1536]{2,1,0:T(8,128)(2,1)S(1)}, bf16[2,128,1536]{2,1,0:T(8,128)(2,1)S(1)}, u32[]{:S(2)}, u32[]{:S(2)}) collective-permute-start(bf16[2,128,1536]{2,1,0:T(8,128)(2,1)S(1)} %get-tuple-element.27.mine), channel_id=1, source_target_pairs={{0,8},{8,16},{12,4},{16,24},{20,12},{28,20},{1,9},{9,17},{13,5},{1... | collective-permute-start | bytes 2359304 | tf_op jit(solution)/shard_map/ppermute | solution.py:252
  36.6 7.5 %collective-permute-done.6.outer = bf16[2,128,1536]{2,1,0:T(8,128)(2,1)} collective-permute-done((bf16[2,128,1536]{2,1,0:T(8,128)(2,1)S(1)}, bf16[2,128,1536]{2,1,0:T(8,128)(2,1)}, u32[]{:S(2)}, u32[]{:S(2)}) %collective-permute-start.6) | collective-permute-done | bytes 786464 | tf_op jit(solution)/shard_map/ppermute | solution.py:252
  44.1 2.4 %collective-permute-start.11 = (bf16[2,128,1536]{2,1,0:T(8,128)(2,1)S(1)}, bf16[2,128,1536]{2,1,0:T(8,128)(2,1)S(1)}, u32[]{:S(2)}, u32[]{:S(2)}) collective-permute-start(bf16[2,128,1536]{2,1,0:T(8,128)(2,1)S(1)} %collective-permute-done.1.a), channel_id=1, source_target_pairs={{0,4},{4,0},{8,12},{12,8},{16,20},{20,16},{24,28},{28,24},{1,5},{5... | collective-permute-start | bytes 2359304 | tf_op jit(solution)/shard_map/ppermute | solution.py:252
  46.5 0.0 collective-permute-done.4.a
  46.5 0.0 collective-permute-done.2
  46.5 0.0 copy-done.1
  46.5 7.2 %query_side.1 = (bf16[128,1536]{1,0:T(8,128)(2,1)}, f32[2,128,1536]{2,1,0:T(8,128)S(1)}, bf16[2,64,1536]{2,1,0:T(8,128)(2,1)S(1)}, bf16[2,64,1536]{2,1,0:T(8,128)(2,1)S(1)}, f32[5,12,128]{2,1,0:T(8,128)S(1)}) custom-call(bf16[2,128,1536]{2,1,0:T(8,128)(2,1)S(1)} %get-tuple-element.27.mine, bf16[2,128,1536]{2,1,0:T(8,128)(2,1)S(1)} %get-tuple-element.20.own.keys, ...), custom_call_target="tpu_custom_call" | custom-call | flops 10066329600 | bytes 4194304 | tf_op jit(solution)/shard_map/query_side/pallas_call | solution.py:270
  53.8 1.3 %collective-permute-start.12 = (f32[5,12,128]{2,1,0:T(8,128)S(1)}, f32[5,12,128]{2,1,0:T(8,128)S(1)}, u32[]{:S(2)}, u32[]{:S(2)}) collective-permute-start(f32[5,12,128]{2,1,0:T(8,128)S(1)} %get-tuple-element.28), channel_id=1, source_target_pairs={{4,12},{8,0},{12,20},{16,8},{20,28},{24,16},{5,13},{9,1},{13,21},{... | collective-permute-start | bytes 92168 | tf_op jit(solution)/shard_map/ppermute | solution.py:252
  55.1 2.1 %collective-permute-start.7 = (bf16[2,64,1536]{2,1,0:T(8,128)(2,1)S(1)}, bf16[2,64,1536]{2,1,0:T(8,128)(2,1)S(1)}, u32[]{:S(2)}, u32[]{:S(2)}) collective-permute-start(bf16[2,64,1536]{2,1,0:T(8,128)(2,1)S(1)} %get-tuple-element.24), channel_id=1, source_target_pairs={{0,1},{1,0},{2,3},{3,2},{4,5},{5,4},{6,7},{7,6},{8,9},{9,8},{10,11... | collective-permute-start | bytes 1179656 | tf_op jit(solution)/shard_map/ppermute | solution.py:299
  57.2 1.6 %collective-permute-done.12.of_a = f32[5,12,128]{2,1,0:T(8,128)S(1)} collective-permute-done((f32[5,12,128]{2,1,0:T(8,128)S(1)}, f32[5,12,128]{2,1,0:T(8,128)S(1)}, u32[]{:S(2)}, u32[]{:S(2)}) %collective-permute-start.12) | collective-permute-done | bytes 30752 | tf_op jit(solution)/shard_map/ppermute | solution.py:252
  58.8 6.0 %collective-permute-start.8 = (bf16[2,64,1536]{2,1,0:T(8,128)(2,1)S(1)}, bf16[2,64,1536]{2,1,0:T(8,128)(2,1)S(1)}, u32[]{:S(2)}, u32[]{:S(2)}) collective-permute-start(bf16[2,64,1536]{2,1,0:T(8,128)(2,1)S(1)} %get-tuple-element.25), channel_id=1, source_target_pairs={{1,2},{2,1},{5,6},{6,5},{9,10},{10,9},{13,14},{14,13},{17,18},{18,... | collective-permute-start | bytes 1179656 | tf_op jit(solution)/shard_map/ppermute | solution.py:300
  64.8 0.0 collective-permute-done.9.part
  64.8 0.1 collective-permute-start.13
  64.9 0.0 collective-permute-done.10.b
  64.9 3.2 %collective-permute-start.14 = (f32[5,12,128]{2,1,0:T(8,128)S(1)}, f32[5,12,128]{2,1,0:T(8,128)S(1)}, u32[]{:S(2)}, u32[]{:S(2)}) collective-permute-start(f32[5,12,128]{2,1,0:T(8,128)S(1)} %get-tuple-element.28), channel_id=1, source_target_pairs={{0,8},{8,16},{12,4},{16,24},{20,12},{28,20},{1,9},{9,17},{13,5},{1... | collective-permute-start | bytes 92168 | tf_op jit(solution)/shard_map/ppermute | solution.py:252
  68.1 0.3 collective-permute-done.11.outer
  68.5 0.7 %collective-permute-done.14.of_b = f32[5,12,128]{2,1,0:T(8,128)S(1)} collective-permute-done((f32[5,12,128]{2,1,0:T(8,128)S(1)}, f32[5,12,128]{2,1,0:T(8,128)S(1)}, u32[]{:S(2)}, u32[]{:S(2)}) %collective-permute-start.14) | collective-permute-done | bytes 30752 | tf_op jit(solution)/shard_map/ppermute | solution.py:252
  69.2 0.1 collective-permute-done.13.of_part
  69.3 0.0 collective-permute-done.7.face_1_grads
  69.3 0.9 %collective-permute-done.8.face_2_grads = bf16[2,64,1536]{2,1,0:T(8,128)(2,1)S(1)} collective-permute-done((bf16[2,64,1536]{2,1,0:T(8,128)(2,1)S(1)}, bf16[2,64,1536]{2,1,0:T(8,128)(2,1)S(1)}, u32[]{:S(2)}, u32[]{:S(2)}) %collective-permute-start.8) | collective-permute-done | bytes 393248 | tf_op jit(solution)/shard_map/ppermute | solution.py:300
  70.2 3.8 %key_side.1 = (bf16[128,1536]{1,0:T(8,128)(2,1)}, bf16[128,1536]{1,0:T(8,128)(2,1)}) custom-call(bf16[2,128,1536]{2,1,0:T(8,128)(2,1)S(1)} %get-tuple-element.20.own.keys, f32[2,128,1536]{2,1,0:T(8,128)S(1)} %get-tuple-element.23.own_grads, bf16[2,64,1536]{2,1,0:T(8,128)(2,1)S(1)} %collective-permute-done.7.face_1_grads, ...), custom_call_target="tpu_custom_call" | custom-call | flops 5033164800 | bytes 4194304 | tf_op jit(solution)/shard_map/key_side/pallas_call | solution.py:302
  (1 shorter events, 0.0 us)
Async XLA Ops:
  0.6 31.2 %copy-start = (s32[1,1,12,2]{2,3,1,0:T(2,128)S(1)}, s32[1,1,12,2]{2,3,1,0:T(2,128)}, u32[]{:S(2)}) copy-start(s32[1,1,12,2]{2,3,1,0:T(2,128)} %param.9) | copy-start | bytes 292
  2.2 19.4 %collective-permute-start.3 = (bf16[2,128,1536]{2,1,0:T(8,128)(2,1)S(1)}, bf16[2,128,1536]{2,1,0:T(8,128)(2,1)S(1)}, u32[]{:S(2)}, u32[]{:S(2)}) collective-permute-start(bf16[2,128,1536]{2,1,0:T(8,128)(2,1)S(1)} %get-tuple-element.20.own.keys), channel_id=1, source_target_pairs={{0,4},{4,0},{8,12},{12,8},{16,20},{20,16},{24,28},{28,24},{1,5},{5... | collective-permute-start | bytes 2359304 | tf_op jit(solution)/shard_map/ppermute | solution.py:252
  4.4 17.3 %collective-permute-start = (bf16[2,128,1536]{2,1,0:T(8,128)(2,1)S(1)}, bf16[2,128,1536]{2,1,0:T(8,128)(2,1)S(1)}, u32[]{:S(2)}, u32[]{:S(2)}) collective-permute-start(bf16[2,128,1536]{2,1,0:T(8,128)(2,1)S(1)} %get-tuple-element.20.own.keys), channel_id=1, source_target_pairs={{0,1},{1,0},{2,3},{3,2},{4,5},{5,4},{6,7},{7,6},{8,9},{9,8},{10,11... | collective-permute-start | bytes 2359304 | tf_op jit(solution)/shard_map/ppermute | solution.py:257
  5.3 21.7 %collective-permute-start.1 = (bf16[2,128,1536]{2,1,0:T(8,128)(2,1)S(1)}, bf16[2,128,1536]{2,1,0:T(8,128)(2,1)S(1)}, u32[]{:S(2)}, u32[]{:S(2)}) collective-permute-start(bf16[2,128,1536]{2,1,0:T(8,128)(2,1)S(1)} %get-tuple-element.27.mine), channel_id=1, source_target_pairs={{4,12},{8,0},{12,20},{16,8},{20,28},{24,16},{5,13},{9,1},{13,21},{... | collective-permute-start | bytes 2359304 | tf_op jit(solution)/shard_map/ppermute | solution.py:252
  6.6 27.6 %collective-permute-start.5 = (bf16[2,128,1536]{2,1,0:T(8,128)(2,1)S(1)}, bf16[2,128,1536]{2,1,0:T(8,128)(2,1)}, u32[]{:S(2)}, u32[]{:S(2)}) collective-permute-start(bf16[2,128,1536]{2,1,0:T(8,128)(2,1)S(1)} %get-tuple-element.20.own.keys), channel_id=1, source_target_pairs={{0,8},{8,16},{12,4},{16,24},{20,12},{28,20},{1,9},{9,17},{13,5},{1... | collective-permute-start | bytes 2359304 | tf_op jit(solution)/shard_map/ppermute | solution.py:252
  21.6 24.9 %copy-start.1 = (bf16[2,128,1536]{2,1,0:T(8,128)(2,1)}, bf16[2,128,1536]{2,1,0:T(8,128)(2,1)S(1)}, u32[]{:S(2)}) copy-start(bf16[2,128,1536]{2,1,0:T(8,128)(2,1)S(1)} %collective-permute-done.3.part) | copy-start | bytes 2359300
  21.6 10.2 %copy-start.2 = (bf16[2,128,1536]{2,1,0:T(8,128)(2,1)}, bf16[2,128,1536]{2,1,0:T(8,128)(2,1)S(1)}, u32[]{:S(2)}) copy-start(bf16[2,128,1536]{2,1,0:T(8,128)(2,1)S(1)} %collective-permute-done) | copy-start | bytes 2359300
  21.6 22.5 %collective-permute-start.6 = (bf16[2,128,1536]{2,1,0:T(8,128)(2,1)S(1)}, bf16[2,128,1536]{2,1,0:T(8,128)(2,1)}, u32[]{:S(2)}, u32[]{:S(2)}) collective-permute-start(bf16[2,128,1536]{2,1,0:T(8,128)(2,1)S(1)} %collective-permute-done.3.part), channel_id=1, source_target_pairs={{0,8},{8,16},{12,4},{16,24},{20,12},{28,20},{1,9},{9,17},{13,5},{1... | collective-permute-start | bytes 2359304 | tf_op jit(solution)/shard_map/ppermute | solution.py:252
  25.8 20.8 %collective-permute-start.4 = (bf16[2,128,1536]{2,1,0:T(8,128)(2,1)S(1)}, bf16[2,128,1536]{2,1,0:T(8,128)(2,1)}, u32[]{:S(2)}, u32[]{:S(2)}) collective-permute-start(bf16[2,128,1536]{2,1,0:T(8,128)(2,1)S(1)} %get-tuple-element.20.own.keys), channel_id=1, source_target_pairs={{4,12},{8,0},{12,20},{16,8},{20,28},{24,16},{5,13},{9,1},{13,21},{... | collective-permute-start | bytes 2359304 | tf_op jit(solution)/shard_map/ppermute | solution.py:252
  27.1 19.5 %collective-permute-start.2 = (bf16[2,128,1536]{2,1,0:T(8,128)(2,1)S(1)}, bf16[2,128,1536]{2,1,0:T(8,128)(2,1)}, u32[]{:S(2)}, u32[]{:S(2)}) collective-permute-start(bf16[2,128,1536]{2,1,0:T(8,128)(2,1)S(1)} %get-tuple-element.20.own.keys), channel_id=1, source_target_pairs={{1,2},{2,1},{5,6},{6,5},{9,10},{10,9},{13,14},{14,13},{17,18},{18,... | collective-permute-start | bytes 2359304 | tf_op jit(solution)/shard_map/ppermute | solution.py:262
  31.9 32.9 %collective-permute-start.9 = (bf16[2,128,1536]{2,1,0:T(8,128)(2,1)S(1)}, bf16[2,128,1536]{2,1,0:T(8,128)(2,1)S(1)}, u32[]{:S(2)}, u32[]{:S(2)}) collective-permute-start(bf16[2,128,1536]{2,1,0:T(8,128)(2,1)S(1)} %get-tuple-element.27.mine), channel_id=1, source_target_pairs={{0,4},{4,0},{8,12},{12,8},{16,20},{20,16},{24,28},{28,24},{1,5},{5... | collective-permute-start | bytes 2359304 | tf_op jit(solution)/shard_map/ppermute | solution.py:252
  34.2 30.7 %collective-permute-start.10 = (bf16[2,128,1536]{2,1,0:T(8,128)(2,1)S(1)}, bf16[2,128,1536]{2,1,0:T(8,128)(2,1)S(1)}, u32[]{:S(2)}, u32[]{:S(2)}) collective-permute-start(bf16[2,128,1536]{2,1,0:T(8,128)(2,1)S(1)} %get-tuple-element.27.mine), channel_id=1, source_target_pairs={{0,8},{8,16},{12,4},{16,24},{20,12},{28,20},{1,9},{9,17},{13,5},{1... | collective-permute-start | bytes 2359304 | tf_op jit(solution)/shard_map/ppermute | solution.py:252
  44.1 24.4 %collective-permute-start.11 = (bf16[2,128,1536]{2,1,0:T(8,128)(2,1)S(1)}, bf16[2,128,1536]{2,1,0:T(8,128)(2,1)S(1)}, u32[]{:S(2)}, u32[]{:S(2)}) collective-permute-start(bf16[2,128,1536]{2,1,0:T(8,128)(2,1)S(1)} %collective-permute-done.1.a), channel_id=1, source_target_pairs={{0,4},{4,0},{8,12},{12,8},{16,20},{20,16},{24,28},{28,24},{1,5},{5... | collective-permute-start | bytes 2359304 | tf_op jit(solution)/shard_map/ppermute | solution.py:252
  53.8 5.0 %collective-permute-start.12 = (f32[5,12,128]{2,1,0:T(8,128)S(1)}, f32[5,12,128]{2,1,0:T(8,128)S(1)}, u32[]{:S(2)}, u32[]{:S(2)}) collective-permute-start(f32[5,12,128]{2,1,0:T(8,128)S(1)} %get-tuple-element.28), channel_id=1, source_target_pairs={{4,12},{8,0},{12,20},{16,8},{20,28},{24,16},{5,13},{9,1},{13,21},{... | collective-permute-start | bytes 92168 | tf_op jit(solution)/shard_map/ppermute | solution.py:252
  55.1 14.3 %collective-permute-start.7 = (bf16[2,64,1536]{2,1,0:T(8,128)(2,1)S(1)}, bf16[2,64,1536]{2,1,0:T(8,128)(2,1)S(1)}, u32[]{:S(2)}, u32[]{:S(2)}) collective-permute-start(bf16[2,64,1536]{2,1,0:T(8,128)(2,1)S(1)} %get-tuple-element.24), channel_id=1, source_target_pairs={{0,1},{1,0},{2,3},{3,2},{4,5},{5,4},{6,7},{7,6},{8,9},{9,8},{10,11... | collective-permute-start | bytes 1179656 | tf_op jit(solution)/shard_map/ppermute | solution.py:299
  58.8 11.4 %collective-permute-start.8 = (bf16[2,64,1536]{2,1,0:T(8,128)(2,1)S(1)}, bf16[2,64,1536]{2,1,0:T(8,128)(2,1)S(1)}, u32[]{:S(2)}, u32[]{:S(2)}) collective-permute-start(bf16[2,64,1536]{2,1,0:T(8,128)(2,1)S(1)} %get-tuple-element.25), channel_id=1, source_target_pairs={{1,2},{2,1},{5,6},{6,5},{9,10},{10,9},{13,14},{14,13},{17,18},{18,... | collective-permute-start | bytes 1179656 | tf_op jit(solution)/shard_map/ppermute | solution.py:300
  64.8 4.5 %collective-permute-start.13 = (f32[2,5,12,128]{3,2,1,0:T(8,128)S(1)}, f32[2,5,12,128]{3,2,1,0:T(8,128)S(1)}, u32[]{:S(2)}, u32[]{:S(2)}) collective-permute-start(f32[2,5,12,128]{3,2,1,0:T(8,128)S(1)} %pad_maximum_fusion), channel_id=1, source_target_pairs={{0,4},{4,0},{8,12},{12,8},{16,20},{20,16},{24,28},{28,24},{1,5},{5... | collective-permute-start | bytes 184328 | tf_op jit(solution)/shard_map/ppermute | solution.py:252
  64.9 4.3 %collective-permute-start.14 = (f32[5,12,128]{2,1,0:T(8,128)S(1)}, f32[5,12,128]{2,1,0:T(8,128)S(1)}, u32[]{:S(2)}, u32[]{:S(2)}) collective-permute-start(f32[5,12,128]{2,1,0:T(8,128)S(1)} %get-tuple-element.28), channel_id=1, source_target_pairs={{0,8},{8,16},{12,4},{16,24},{20,12},{28,20},{1,9},{9,17},{13,5},{1... | collective-permute-start | bytes 92168 | tf_op jit(solution)/shard_map/ppermute | solution.py:252

commit v5 on v4

--- a/solution.py
+++ b/solution.py
@@ -255,12 +255,12 @@
     kv_part, kv_b = move(key_value, partner), move(key_value, route_b)
     kv_a = move(after(key_value, kv_part), route_a)
     face_1 = lax.ppermute(key_value, "height", pairs_1)
-    qg_part = move(after(query_grad, kv_part), partner)
+    qg_part = move(query_grad, partner)
     qg_a = move(query_grad, route_a)
     kv_outer = move(after(kv_part, face_1), route_b) if relayed else move(key_value, outer)
     qg_b = move(after(query_grad, kv_b), route_b)
     face_2 = lax.ppermute(after(key_value, qg_a), "height", pairs_2)
-    qg_outer = move(qg_a, partner) if relayed else move(query_grad, outer)
+    qg_outer = move(after(qg_a, qg_part), partner) if relayed else move(query_grad, outer)
 
     f32, bf16 = jnp.float32, jnp.bfloat16
     vmem, hbm = pl.BlockSpec(memory_space=pltpu.VMEM), pl.BlockSpec(memory_space=pltpu.HBM)

time: 74.4 us -> 72.9 us (0.980)
  waiting for transfers between devices: 21.3 us -> 20.2 us
  starting transfers between devices: 39.2 us -> 38.2 us
    ppermute x1, starting transfers between devices: 5.96 us -> 3.05 us  [per_device(): back_2 = lax.ppermute(face_2_grads, 'height', pairs_2)]
    ppermute x1, starting transfers between devices: 2.15 us -> 3.7 us  [per_device(): back_1 = lax.ppermute(face_1_grads, 'height', pairs_1)]
    ppermute x1, starting transfers between devices: 4.76 us -> 6.01 us  [per_device(): face_2 = lax.ppermute(after(key_value, qg_a), 'height', pairs_2)]
    ppermute x1, waiting for transfers between devices: 0.9 us -> 0.01 us  [per_device(): back_2 = lax.ppermute(face_2_grads, 'height', pairs_2)]
    ppermute x11, starting transfers between devices: 25.3 us -> 24.5 us  [move(): return lax.ppermute(block, 'tm', route)]
  transfers between devices with their start and end apart: 15 -> 15, of which waited for: 7 -> 5; matrix products, arithmetic and copies ran while one was open for 0% -> 0% of each run, Pallas kernels for 10% -> 10%
where the time goes in v5:
time: 72.9 us; the launch traced here: 71.8 us
  starting transfers between devices  38.2 us (52%)
  waiting for transfers between devices  20.2 us (28%)
  Pallas kernels  12.6 us (17%)
  between operations  0.76 us (1%)
    ppermute x11, starting transfers between devices, move(): return lax.ppermute(block, 'tm', route)  24.5 us
    ppermute x11, waiting for transfers between devices, move(): return lax.ppermute(block, 'tm', route)  20.2 us
    pallas_call x1, Pallas kernels, per_device(): pl.pallas_call(functools.partial(query_kernel, n_tm, n_height), out_shape...  7.23 us
    ppermute x1, starting transfers between devices, per_device(): face_2 = lax.ppermute(after(key_value, qg_a), 'height', pairs_2)  6.01 us
    pallas_call x1, Pallas kernels, per_device(): pl.pallas_call(key_kernel, out_shape=(jax.ShapeDtypeStruct((tile, width),...  3.76 us
    ppermute x1, starting transfers between devices, per_device(): back_1 = lax.ppermute(face_1_grads, 'height', pairs_1)  3.7 us
    ppermute x1, starting transfers between devices, per_device(): back_2 = lax.ppermute(face_2_grads, 'height', pairs_2)  3.05 us
    pallas_call x1, Pallas kernels, paired(): pl.pallas_call(pair_kernel, out_shape=(jax.ShapeDtypeStruct((2, rows, wid...  1.6 us
  transfers between devices with their start and end apart: 15, of which 5 were waited for; matrix products, arithmetic and copies ran while one was open for 0% of the time, Pallas kernels for 10%

profile of v5, /device:TPU:1, one launch (start us, length us, event | category | flops | bytes accessed | tf_op | source)
XLA Modules:
  0.0 71.8 jit_solution(2184976270136347260)
XLA Ops:
  0.6 0.0 copy-start
  0.6 1.6 %pairs.1 = (bf16[2,128,1536]{2,1,0:T(8,128)(2,1)S(1)}, bf16[2,128,1536]{2,1,0:T(8,128)(2,1)S(1)}) custom-call(bf16[128,1536]{1,0:T(8,128)(2,1)} %bitcast.14, bf16[128,1536]{1,0:T(8,128)(2,1)} %bitcast.15, bf16[128,1536]{1,0:T(8,128)(2,1)} %bitcast.16, bf16[128,1536]{1,0:T(8,128)(2,1)} %bitcast.17), custom_call_target="tpu_custom_call" | custom-call | bytes 3145728 | tf_op jit(solution)/shard_map/pairs/pallas_call | solution.py:73
  2.2 2.1 %collective-permute-start.3 = (bf16[2,128,1536]{2,1,0:T(8,128)(2,1)S(1)}, bf16[2,128,1536]{2,1,0:T(8,128)(2,1)}, u32[]{:S(2)}, u32[]{:S(2)}) collective-permute-start(bf16[2,128,1536]{2,1,0:T(8,128)(2,1)S(1)} %get-tuple-element.20.own.keys), channel_id=1, source_target_pairs={{0,4},{4,0},{8,12},{12,8},{16,20},{20,16},{24,28},{28,24},{1,5},{5... | collective-permute-start | bytes 2359304 | tf_op jit(solution)/shard_map/ppermute | solution.py:252
  4.4 1.0 %collective-permute-start = (bf16[2,128,1536]{2,1,0:T(8,128)(2,1)S(1)}, bf16[2,128,1536]{2,1,0:T(8,128)(2,1)S(1)}, u32[]{:S(2)}, u32[]{:S(2)}) collective-permute-start(bf16[2,128,1536]{2,1,0:T(8,128)(2,1)S(1)} %get-tuple-element.20.own.keys), channel_id=1, source_target_pairs={{0,1},{1,0},{2,3},{3,2},{4,5},{5,4},{6,7},{7,6},{8,9},{9,8},{10,11... | collective-permute-start | bytes 2359304 | tf_op jit(solution)/shard_map/ppermute | solution.py:257
  5.3 1.3 %collective-permute-start.1 = (bf16[2,128,1536]{2,1,0:T(8,128)(2,1)S(1)}, bf16[2,128,1536]{2,1,0:T(8,128)(2,1)S(1)}, u32[]{:S(2)}, u32[]{:S(2)}) collective-permute-start(bf16[2,128,1536]{2,1,0:T(8,128)(2,1)S(1)} %get-tuple-element.26.mine), channel_id=1, source_target_pairs={{4,12},{8,0},{12,20},{16,8},{20,28},{24,16},{5,13},{9,1},{13,21},{... | collective-permute-start | bytes 2359304 | tf_op jit(solution)/shard_map/ppermute | solution.py:252
  6.6 4.9 %collective-permute-start.5 = (bf16[2,128,1536]{2,1,0:T(8,128)(2,1)S(1)}, bf16[2,128,1536]{2,1,0:T(8,128)(2,1)}, u32[]{:S(2)}, u32[]{:S(2)}) collective-permute-start(bf16[2,128,1536]{2,1,0:T(8,128)(2,1)S(1)} %get-tuple-element.20.own.keys), channel_id=1, source_target_pairs={{0,8},{8,16},{12,4},{16,24},{20,12},{28,20},{1,9},{9,17},{13,5},{1... | collective-permute-start | bytes 2359304 | tf_op jit(solution)/shard_map/ppermute | solution.py:252
  11.5 0.0 collective-permute-start.9
  11.5 10.2 %collective-permute-done.3.part = bf16[2,128,1536]{2,1,0:T(8,128)(2,1)} collective-permute-done((bf16[2,128,1536]{2,1,0:T(8,128)(2,1)S(1)}, bf16[2,128,1536]{2,1,0:T(8,128)(2,1)}, u32[]{:S(2)}, u32[]{:S(2)}) %collective-permute-start.3) | collective-permute-done | bytes 786464 | tf_op jit(solution)/shard_map/ppermute | solution.py:252
  21.7 0.0 collective-permute-done
  21.7 0.0 copy-start.1
  21.7 4.0 %collective-permute-start.6 = (bf16[2,128,1536]{2,1,0:T(8,128)(2,1)}, bf16[2,128,1536]{2,1,0:T(8,128)(2,1)}, u32[]{:S(2)}, u32[]{:S(2)}) collective-permute-start(bf16[2,128,1536]{2,1,0:T(8,128)(2,1)} %collective-permute-done.3.part), channel_id=1, source_target_pairs={{0,8},{8,16},{12,4},{16,24},{20,12},{28,20},{1,9},{9,17},{13,5},{1... | collective-permute-start | bytes 2359304 | tf_op jit(solution)/shard_map/ppermute | solution.py:252
  25.7 1.3 %collective-permute-start.4 = (bf16[2,128,1536]{2,1,0:T(8,128)(2,1)S(1)}, bf16[2,128,1536]{2,1,0:T(8,128)(2,1)}, u32[]{:S(2)}, u32[]{:S(2)}) collective-permute-start(bf16[2,128,1536]{2,1,0:T(8,128)(2,1)S(1)} %get-tuple-element.20.own.keys), channel_id=1, source_target_pairs={{4,12},{8,0},{12,20},{16,8},{20,28},{24,16},{5,13},{9,1},{13,21},{... | collective-permute-start | bytes 2359304 | tf_op jit(solution)/shard_map/ppermute | solution.py:252
  27.0 0.0 collective-permute-done.1.a
  27.0 6.0 %collective-permute-start.2 = (bf16[2,128,1536]{2,1,0:T(8,128)(2,1)S(1)}, bf16[2,128,1536]{2,1,0:T(8,128)(2,1)}, u32[]{:S(2)}, u32[]{:S(2)}) collective-permute-start(bf16[2,128,1536]{2,1,0:T(8,128)(2,1)S(1)} %get-tuple-element.20.own.keys), channel_id=1, source_target_pairs={{1,2},{2,1},{5,6},{6,5},{9,10},{10,9},{13,14},{14,13},{17,18},{18,... | collective-permute-start | bytes 2359304 | tf_op jit(solution)/shard_map/ppermute | solution.py:262
  33.1 0.0 copy-done.1
  33.1 0.0 copy-done
  33.1 0.1 copy.8.picks
  33.2 0.0 collective-permute-done.5.b
  33.2 4.3 %collective-permute-start.10 = (bf16[2,128,1536]{2,1,0:T(8,128)(2,1)S(1)}, bf16[2,128,1536]{2,1,0:T(8,128)(2,1)S(1)}, u32[]{:S(2)}, u32[]{:S(2)}) collective-permute-start(bf16[2,128,1536]{2,1,0:T(8,128)(2,1)S(1)} %get-tuple-element.26.mine), channel_id=1, source_target_pairs={{0,8},{8,16},{12,4},{16,24},{20,12},{28,20},{1,9},{9,17},{13,5},{1... | collective-permute-start | bytes 2359304 | tf_op jit(solution)/shard_map/ppermute | solution.py:252
  37.5 1.1 %collective-permute-done.9.part = bf16[2,128,1536]{2,1,0:T(8,128)(2,1)S(1)} collective-permute-done((bf16[2,128,1536]{2,1,0:T(8,128)(2,1)S(1)}, bf16[2,128,1536]{2,1,0:T(8,128)(2,1)S(1)}, u32[]{:S(2)}, u32[]{:S(2)}) %collective-permute-start.9) | collective-permute-done | bytes 786464 | tf_op jit(solution)/shard_map/ppermute | solution.py:252
  38.6 1.1 %collective-permute-start.11 = (bf16[2,128,1536]{2,1,0:T(8,128)(2,1)S(1)}, bf16[2,128,1536]{2,1,0:T(8,128)(2,1)S(1)}, u32[]{:S(2)}, u32[]{:S(2)}) collective-permute-start(bf16[2,128,1536]{2,1,0:T(8,128)(2,1)S(1)} %collective-permute-done.1.a), channel_id=1, source_target_pairs={{0,4},{4,0},{8,12},{12,8},{16,20},{20,16},{24,28},{28,24},{1,5},{5... | collective-permute-start | bytes 2359304 | tf_op jit(solution)/shard_map/ppermute | solution.py:252
  39.7 4.3 %collective-permute-done.6.outer = bf16[2,128,1536]{2,1,0:T(8,128)(2,1)} collective-permute-done((bf16[2,128,1536]{2,1,0:T(8,128)(2,1)}, bf16[2,128,1536]{2,1,0:T(8,128)(2,1)}, u32[]{:S(2)}, u32[]{:S(2)}) %collective-permute-start.6) | collective-permute-done | bytes 786464 | tf_op jit(solution)/shard_map/ppermute | solution.py:252
  44.0 0.0 collective-permute-done.4.a
  44.0 0.0 collective-permute-done.2
  44.0 7.2 %query_side.1 = (bf16[128,1536]{1,0:T(8,128)(2,1)}, f32[2,128,1536]{2,1,0:T(8,128)S(1)}, bf16[2,64,1536]{2,1,0:T(8,128)(2,1)S(1)}, bf16[2,64,1536]{2,1,0:T(8,128)(2,1)S(1)}, f32[5,12,128]{2,1,0:T(8,128)S(1)}) custom-call(bf16[2,128,1536]{2,1,0:T(8,128)(2,1)S(1)} %get-tuple-element.26.mine, bf16[2,128,1536]{2,1,0:T(8,128)(2,1)S(1)} %get-tuple-element.20.own.keys, ...), custom_call_target="tpu_custom_call" | custom-call | flops 10066329600 | bytes 4194304 | tf_op jit(solution)/shard_map/query_side/pallas_call | solution.py:270
  51.3 3.7 %collective-permute-start.7 = (bf16[2,64,1536]{2,1,0:T(8,128)(2,1)S(1)}, bf16[2,64,1536]{2,1,0:T(8,128)(2,1)S(1)}, u32[]{:S(2)}, u32[]{:S(2)}) collective-permute-start(bf16[2,64,1536]{2,1,0:T(8,128)(2,1)S(1)} %get-tuple-element.24), channel_id=1, source_target_pairs={{0,1},{1,0},{2,3},{3,2},{4,5},{5,4},{6,7},{7,6},{8,9},{9,8},{10,11... | collective-permute-start | bytes 1179656 | tf_op jit(solution)/shard_map/ppermute | solution.py:299
  55.0 3.0 %collective-permute-start.8 = (bf16[2,64,1536]{2,1,0:T(8,128)(2,1)S(1)}, bf16[2,64,1536]{2,1,0:T(8,128)(2,1)S(1)}, u32[]{:S(2)}, u32[]{:S(2)}) collective-permute-start(bf16[2,64,1536]{2,1,0:T(8,128)(2,1)S(1)} %get-tuple-element.25), channel_id=1, source_target_pairs={{1,2},{2,1},{5,6},{6,5},{9,10},{10,9},{13,14},{14,13},{17,18},{18,... | collective-permute-start | bytes 1179656 | tf_op jit(solution)/shard_map/ppermute | solution.py:300
  58.0 1.3 %collective-permute-start.12 = (f32[5,12,128]{2,1,0:T(8,128)S(1)}, f32[5,12,128]{2,1,0:T(8,128)S(1)}, u32[]{:S(2)}, u32[]{:S(2)}) collective-permute-start(f32[5,12,128]{2,1,0:T(8,128)S(1)} %get-tuple-element.28), channel_id=1, source_target_pairs={{4,12},{8,0},{12,20},{16,8},{20,28},{24,16},{5,13},{9,1},{13,21},{... | collective-permute-start | bytes 92168 | tf_op jit(solution)/shard_map/ppermute | solution.py:252
  59.3 3.4 %collective-permute-done.12.of_a = f32[5,12,128]{2,1,0:T(8,128)S(1)} collective-permute-done((f32[5,12,128]{2,1,0:T(8,128)S(1)}, f32[5,12,128]{2,1,0:T(8,128)S(1)}, u32[]{:S(2)}, u32[]{:S(2)}) %collective-permute-start.12) | collective-permute-done | bytes 30752 | tf_op jit(solution)/shard_map/ppermute | solution.py:252
  62.8 0.1 collective-permute-start.13
  62.9 0.0 collective-permute-done.10.b
  62.9 4.0 %collective-permute-start.14 = (f32[5,12,128]{2,1,0:T(8,128)S(1)}, f32[5,12,128]{2,1,0:T(8,128)S(1)}, u32[]{:S(2)}, u32[]{:S(2)}) collective-permute-start(f32[5,12,128]{2,1,0:T(8,128)S(1)} %get-tuple-element.28), channel_id=1, source_target_pairs={{0,8},{8,16},{12,4},{16,24},{20,12},{28,20},{1,9},{9,17},{13,5},{1... | collective-permute-start | bytes 92168 | tf_op jit(solution)/shard_map/ppermute | solution.py:252
  67.0 0.0 collective-permute-done.11.outer
  67.0 1.1 %collective-permute-done.14.of_b = f32[5,12,128]{2,1,0:T(8,128)S(1)} collective-permute-done((f32[5,12,128]{2,1,0:T(8,128)S(1)}, f32[5,12,128]{2,1,0:T(8,128)S(1)}, u32[]{:S(2)}, u32[]{:S(2)}) %collective-permute-start.14) | collective-permute-done | bytes 30752 | tf_op jit(solution)/shard_map/ppermute | solution.py:252
  68.0 0.0 collective-permute-done.13.of_part
  68.0 0.0 collective-permute-done.7.face_1_grads
  68.0 0.0 collective-permute-done.8.face_2_grads
  68.1 3.8 %key_side.1 = (bf16[128,1536]{1,0:T(8,128)(2,1)}, bf16[128,1536]{1,0:T(8,128)(2,1)}) custom-call(bf16[2,128,1536]{2,1,0:T(8,128)(2,1)S(1)} %get-tuple-element.20.own.keys, f32[2,128,1536]{2,1,0:T(8,128)S(1)} %get-tuple-element.23.own_grads, bf16[2,64,1536]{2,1,0:T(8,128)(2,1)S(1)} %collective-permute-done.7.face_1_grads, ...), custom_call_target="tpu_custom_call" | custom-call | flops 5033164800 | bytes 4194304 | tf_op jit(solution)/shard_map/key_side/pallas_call | solution.py:302
  (1 shorter events, 0.0 us)
Async XLA Ops:
  0.6 32.4 %copy-start = (s32[1,1,12,2]{2,3,1,0:T(2,128)S(1)}, s32[1,1,12,2]{2,3,1,0:T(2,128)}, u32[]{:S(2)}) copy-start(s32[1,1,12,2]{2,3,1,0:T(2,128)} %param.9) | copy-start | bytes 292
  2.2 19.5 %collective-permute-start.3 = (bf16[2,128,1536]{2,1,0:T(8,128)(2,1)S(1)}, bf16[2,128,1536]{2,1,0:T(8,128)(2,1)}, u32[]{:S(2)}, u32[]{:S(2)}) collective-permute-start(bf16[2,128,1536]{2,1,0:T(8,128)(2,1)S(1)} %get-tuple-element.20.own.keys), channel_id=1, source_target_pairs={{0,4},{4,0},{8,12},{12,8},{16,20},{20,16},{24,28},{28,24},{1,5},{5... | collective-permute-start | bytes 2359304 | tf_op jit(solution)/shard_map/ppermute | solution.py:252
  4.4 17.4 %collective-permute-start = (bf16[2,128,1536]{2,1,0:T(8,128)(2,1)S(1)}, bf16[2,128,1536]{2,1,0:T(8,128)(2,1)S(1)}, u32[]{:S(2)}, u32[]{:S(2)}) collective-permute-start(bf16[2,128,1536]{2,1,0:T(8,128)(2,1)S(1)} %get-tuple-element.20.own.keys), channel_id=1, source_target_pairs={{0,1},{1,0},{2,3},{3,2},{4,5},{5,4},{6,7},{7,6},{8,9},{9,8},{10,11... | collective-permute-start | bytes 2359304 | tf_op jit(solution)/shard_map/ppermute | solution.py:257
  5.3 21.7 %collective-permute-start.1 = (bf16[2,128,1536]{2,1,0:T(8,128)(2,1)S(1)}, bf16[2,128,1536]{2,1,0:T(8,128)(2,1)S(1)}, u32[]{:S(2)}, u32[]{:S(2)}) collective-permute-start(bf16[2,128,1536]{2,1,0:T(8,128)(2,1)S(1)} %get-tuple-element.26.mine), channel_id=1, source_target_pairs={{4,12},{8,0},{12,20},{16,8},{20,28},{24,16},{5,13},{9,1},{13,21},{... | collective-permute-start | bytes 2359304 | tf_op jit(solution)/shard_map/ppermute | solution.py:252
  6.6 26.6 %collective-permute-start.5 = (bf16[2,128,1536]{2,1,0:T(8,128)(2,1)S(1)}, bf16[2,128,1536]{2,1,0:T(8,128)(2,1)}, u32[]{:S(2)}, u32[]{:S(2)}) collective-permute-start(bf16[2,128,1536]{2,1,0:T(8,128)(2,1)S(1)} %get-tuple-element.20.own.keys), channel_id=1, source_target_pairs={{0,8},{8,16},{12,4},{16,24},{20,12},{28,20},{1,9},{9,17},{13,5},{1... | collective-permute-start | bytes 2359304 | tf_op jit(solution)/shard_map/ppermute | solution.py:252
  11.5 27.1 %collective-permute-start.9 = (bf16[2,128,1536]{2,1,0:T(8,128)(2,1)S(1)}, bf16[2,128,1536]{2,1,0:T(8,128)(2,1)S(1)}, u32[]{:S(2)}, u32[]{:S(2)}) collective-permute-start(bf16[2,128,1536]{2,1,0:T(8,128)(2,1)S(1)} %get-tuple-element.26.mine), channel_id=1, source_target_pairs={{0,4},{4,0},{8,12},{12,8},{16,20},{20,16},{24,28},{28,24},{1,5},{5... | collective-permute-start | bytes 2359304 | tf_op jit(solution)/shard_map/ppermute | solution.py:252
  21.7 11.3 %copy-start.1 = (bf16[2,128,1536]{2,1,0:T(8,128)(2,1)}, bf16[2,128,1536]{2,1,0:T(8,128)(2,1)S(1)}, u32[]{:S(2)}) copy-start(bf16[2,128,1536]{2,1,0:T(8,128)(2,1)S(1)} %collective-permute-done) | copy-start | bytes 2359300
  21.7 22.3 %collective-permute-start.6 = (bf16[2,128,1536]{2,1,0:T(8,128)(2,1)}, bf16[2,128,1536]{2,1,0:T(8,128)(2,1)}, u32[]{:S(2)}, u32[]{:S(2)}) collective-permute-start(bf16[2,128,1536]{2,1,0:T(8,128)(2,1)} %collective-permute-done.3.part), channel_id=1, source_target_pairs={{0,8},{8,16},{12,4},{16,24},{20,12},{28,20},{1,9},{9,17},{13,5},{1... | collective-permute-start | bytes 2359304 | tf_op jit(solution)/shard_map/ppermute | solution.py:252
  25.7 18.3 %collective-permute-start.4 = (bf16[2,128,1536]{2,1,0:T(8,128)(2,1)S(1)}, bf16[2,128,1536]{2,1,0:T(8,128)(2,1)}, u32[]{:S(2)}, u32[]{:S(2)}) collective-permute-start(bf16[2,128,1536]{2,1,0:T(8,128)(2,1)S(1)} %get-tuple-element.20.own.keys), channel_id=1, source_target_pairs={{4,12},{8,0},{12,20},{16,8},{20,28},{24,16},{5,13},{9,1},{13,21},{... | collective-permute-start | bytes 2359304 | tf_op jit(solution)/shard_map/ppermute | solution.py:252
  27.0 17.0 %collective-permute-start.2 = (bf16[2,128,1536]{2,1,0:T(8,128)(2,1)S(1)}, bf16[2,128,1536]{2,1,0:T(8,128)(2,1)}, u32[]{:S(2)}, u32[]{:S(2)}) collective-permute-start(bf16[2,128,1536]{2,1,0:T(8,128)(2,1)S(1)} %get-tuple-element.20.own.keys), channel_id=1, source_target_pairs={{1,2},{2,1},{5,6},{6,5},{9,10},{10,9},{13,14},{14,13},{17,18},{18,... | collective-permute-start | bytes 2359304 | tf_op jit(solution)/shard_map/ppermute | solution.py:262
  33.2 29.8 %collective-permute-start.10 = (bf16[2,128,1536]{2,1,0:T(8,128)(2,1)S(1)}, bf16[2,128,1536]{2,1,0:T(8,128)(2,1)S(1)}, u32[]{:S(2)}, u32[]{:S(2)}) collective-permute-start(bf16[2,128,1536]{2,1,0:T(8,128)(2,1)S(1)} %get-tuple-element.26.mine), channel_id=1, source_target_pairs={{0,8},{8,16},{12,4},{16,24},{20,12},{28,20},{1,9},{9,17},{13,5},{1... | collective-permute-start | bytes 2359304 | tf_op jit(solution)/shard_map/ppermute | solution.py:252
  38.6 28.4 %collective-permute-start.11 = (bf16[2,128,1536]{2,1,0:T(8,128)(2,1)S(1)}, bf16[2,128,1536]{2,1,0:T(8,128)(2,1)S(1)}, u32[]{:S(2)}, u32[]{:S(2)}) collective-permute-start(bf16[2,128,1536]{2,1,0:T(8,128)(2,1)S(1)} %collective-permute-done.1.a), channel_id=1, source_target_pairs={{0,4},{4,0},{8,12},{12,8},{16,20},{20,16},{24,28},{28,24},{1,5},{5... | collective-permute-start | bytes 2359304 | tf_op jit(solution)/shard_map/ppermute | solution.py:252
  51.3 16.8 %collective-permute-start.7 = (bf16[2,64,1536]{2,1,0:T(8,128)(2,1)S(1)}, bf16[2,64,1536]{2,1,0:T(8,128)(2,1)S(1)}, u32[]{:S(2)}, u32[]{:S(2)}) collective-permute-start(bf16[2,64,1536]{2,1,0:T(8,128)(2,1)S(1)} %get-tuple-element.24), channel_id=1, source_target_pairs={{0,1},{1,0},{2,3},{3,2},{4,5},{5,4},{6,7},{7,6},{8,9},{9,8},{10,11... | collective-permute-start | bytes 1179656 | tf_op jit(solution)/shard_map/ppermute | solution.py:299
  55.0 13.1 %collective-permute-start.8 = (bf16[2,64,1536]{2,1,0:T(8,128)(2,1)S(1)}, bf16[2,64,1536]{2,1,0:T(8,128)(2,1)S(1)}, u32[]{:S(2)}, u32[]{:S(2)}) collective-permute-start(bf16[2,64,1536]{2,1,0:T(8,128)(2,1)S(1)} %get-tuple-element.25), channel_id=1, source_target_pairs={{1,2},{2,1},{5,6},{6,5},{9,10},{10,9},{13,14},{14,13},{17,18},{18,... | collective-permute-start | bytes 1179656 | tf_op jit(solution)/shard_map/ppermute | solution.py:300
  58.0 4.7 %collective-permute-start.12 = (f32[5,12,128]{2,1,0:T(8,128)S(1)}, f32[5,12,128]{2,1,0:T(8,128)S(1)}, u32[]{:S(2)}, u32[]{:S(2)}) collective-permute-start(f32[5,12,128]{2,1,0:T(8,128)S(1)} %get-tuple-element.28), channel_id=1, source_target_pairs={{4,12},{8,0},{12,20},{16,8},{20,28},{24,16},{5,13},{9,1},{13,21},{... | collective-permute-start | bytes 92168 | tf_op jit(solution)/shard_map/ppermute | solution.py:252
  62.8 5.2 %collective-permute-start.13 = (f32[2,5,12,128]{3,2,1,0:T(8,128)S(1)}, f32[2,5,12,128]{3,2,1,0:T(8,128)S(1)}, u32[]{:S(2)}, u32[]{:S(2)}) collective-permute-start(f32[2,5,12,128]{3,2,1,0:T(8,128)S(1)} %pad_maximum_fusion), channel_id=1, source_target_pairs={{0,4},{4,0},{8,12},{12,8},{16,20},{20,16},{24,28},{28,24},{1,5},{5... | collective-permute-start | bytes 184328 | tf_op jit(solution)/shard_map/ppermute | solution.py:252
  62.9 5.1 %collective-permute-start.14 = (f32[5,12,128]{2,1,0:T(8,128)S(1)}, f32[5,12,128]{2,1,0:T(8,128)S(1)}, u32[]{:S(2)}, u32[]{:S(2)}) collective-permute-start(f32[5,12,128]{2,1,0:T(8,128)S(1)} %get-tuple-element.28), channel_id=1, source_target_pairs={{0,8},{8,16},{12,4},{16,24},{20,12},{28,20},{1,9},{9,17},{13,5},{1... | collective-permute-start | bytes 92168 | tf_op jit(solution)/shard_map/ppermute | solution.py:252

commit v6 on v5

--- a/solution.py
+++ b/solution.py
@@ -197,13 +197,8 @@
             gradients(step - 2)
 
 
-def key_kernel(
-    keys, own_grads, face_1_grads, face_2_grads, part, a, b, outer, of_part, of_a, of_b,
-    grad_key, grad_value, scratch,
-):
-    heads, face = keys.shape[2] // HEAD_DIM, face_1_grads.shape[1]
-    last_first = lax.rem(lax.axis_index("height"), 2) == 0
-    others = ((part, of_part.at[0], 1), (a, of_a, 3), (b, of_b, 2), (outer, of_part.at[1], 4))
+def far_grads(keys, others, sums, store, scratch):
+    heads = keys.shape[2] // HEAD_DIM
 
     def products(e):
         cols = columns(e)
@@ -213,26 +208,47 @@
 
     def finish(e):
         cols = columns(e)
-        sums = jnp.concatenate([own_grads[0, :, cols], own_grads[1, :, cols]], axis=1)
+        total = jnp.concatenate([sums[0, :, cols], sums[1, :, cols]], axis=1)
         for i, (block, stats, slot) in enumerate(others):
             score, grad_weights = scratch[e % 2, i, :, :HEAD_DIM], scratch[e % 2, i, :, HEAD_DIM:]
             weights = jnp.exp2(score * (SCALE * LOG2E) - stats[slot, e : e + 1, :])
             dscore = weights * (grad_weights - stats[0, e : e + 1, :]) * SCALE
             both = jnp.concatenate([dscore.astype(jnp.bfloat16), weights.astype(jnp.bfloat16)], axis=1)
-            sums += dot(both, corners(block[0, :, cols], block[1, :, cols]), NN)
-        for at, out in ((0, grad_key), (1, grad_value)):
-            one = face_1_grads[at, :, cols].astype(jnp.float32)
-            two = face_2_grads[at, :, cols].astype(jnp.float32)
-            first, last = jnp.where(last_first, two, one), jnp.where(last_first, one, two)
-            part_sum = sums[:, at * HEAD_DIM : (at + 1) * HEAD_DIM]
-            out[:face, cols] = (part_sum[:face] + first).astype(out.dtype)
-            out[face:, cols] = (part_sum[face:] + last).astype(out.dtype)
+            total += dot(both, corners(block[0, :, cols], block[1, :, cols]), NN)
+        store(cols, total)
 
     products(0)
     for e in range(heads):
         if e + 1 < heads:
             products(e + 1)
         finish(e)
+
+
+def key_kernel(
+    keys, own_grads, face_1_grads, face_2_grads, part, b, outer, of_part, of_b, sums_out, scratch
+):
+    face = face_1_grads.shape[1]
+    last_first = lax.rem(lax.axis_index("height"), 2) == 0
+
+    def store(cols, total):
+        for at in range(2):
+            one = face_1_grads[at, :, cols].astype(jnp.float32)
+            two = face_2_grads[at, :, cols].astype(jnp.float32)
+            first, last = jnp.where(last_first, two, one), jnp.where(last_first, one, two)
+            part_sum = total[:, at * HEAD_DIM : (at + 1) * HEAD_DIM]
+            sums_out[at, :face, cols] = part_sum[:face] + first
+            sums_out[at, face:, cols] = part_sum[face:] + last
+
+    others = ((part, of_part, 1), (b, of_b.at[0], 2), (outer, of_b.at[1], 4))
+    far_grads(keys, others, own_grads, store, scratch)
+
+
+def last_kernel(keys, sums, a, of_a, grad_key, grad_value, scratch):
+    def store(cols, total):
+        grad_key[:, cols] = total[:, :HEAD_DIM].astype(grad_key.dtype)
+        grad_value[:, cols] = total[:, HEAD_DIM:].astype(grad_value.dtype)
+
+    far_grads(keys, ((a, of_a, 3),), sums, store, scratch)
 
 
 def per_device(query_tok, key_tok, value_tok, grad_out, far_picks):
@@ -292,23 +308,33 @@
       in_hbm(kv_part), in_hbm(kv_a), in_hbm(kv_b), in_hbm(kv_outer),
       far_picks.reshape(heads, n_picks))
 
-    of_a, of_b = move(stats, route_a), move(stats, route_b)
-    of_part = move(jnp.stack([stats, of_a]), partner)
+    of_part, of_a = move(stats, partner), move(stats, route_a)
+    of_b = move(jnp.stack([stats, of_part]), route_b)
     if not relayed:
-        of_part = jnp.stack([of_part[0], move(stats, outer)])
+        of_b = jnp.stack([of_b[0], move(stats, outer)])
     back_1 = lax.ppermute(face_1_grads, "height", pairs_1)
     back_2 = lax.ppermute(face_2_grads, "height", pairs_2)
 
+    sums = pl.pallas_call(
+        key_kernel,
+        out_shape=jax.ShapeDtypeStruct((2, tile, width), f32),
+        in_specs=[vmem] * 9,
+        out_specs=vmem,
+        scratch_shapes=[pltpu.VMEM((2, 3, tile, 2 * HEAD_DIM), f32)],
+        compiler_params=params,
+        cost_estimate=pl.CostEstimate(flops=80 * block, bytes_accessed=4 << 20, transcendentals=0),
+        name="key_side",
+    )(key_value, own_grads, back_1, back_2, qg_part, qg_b, qg_outer, of_part, of_b)
     grad_key, grad_value = pl.pallas_call(
-        key_kernel,
+        last_kernel,
         out_shape=(jax.ShapeDtypeStruct((tile, width), bf16),) * 2,
-        in_specs=[vmem] * 11,
+        in_specs=[vmem] * 4,
         out_specs=[vmem] * 2,
-        scratch_shapes=[pltpu.VMEM((2, 2 * REACH, tile, 2 * HEAD_DIM), f32)],
+        scratch_shapes=[pltpu.VMEM((2, 1, tile, 2 * HEAD_DIM), f32)],
         compiler_params=params,
-        cost_estimate=pl.CostEstimate(flops=100 * block, bytes_accessed=4 << 20, transcendentals=0),
-        name="key_side",
-    )(key_value, own_grads, back_1, back_2, qg_part, qg_a, qg_b, qg_outer, of_part, of_a, of_b)
+        cost_estimate=pl.CostEstimate(flops=30 * block, bytes_accessed=4 << 20, transcendentals=0),
+        name="last_side",
+    )(key_value, sums, qg_a, of_a)
     return tuple(x.reshape(query_tok.shape) for x in (grad_query, grad_key, grad_value))
 
 

time: 72.9 us -> 71.5 us (0.981)
  waiting for transfers between devices: 20.2 us -> 19 us
  Pallas kernels: 12.6 us -> 13.4 us
    ppermute x11, waiting for transfers between devices: 20.2 us -> 19 us  [move(): return lax.ppermute(block, 'tm', route)]
    pallas_call x1 -> x2, Pallas kernels: 3.76 us -> 4.54 us  [the longest x1 2.29 us: per_device(): pl.pallas_call(last_kernel, out_shape=(jax.ShapeDtypeStruct((tile, width)...]
  transfers between devices with their start and end apart: 15 -> 15, of which waited for: 5 -> 6; matrix products, arithmetic and copies ran while one was open for 0% -> 0% of each run, Pallas kernels for 10% -> 13%
where the time goes in v6:
time: 71.5 us; the launch traced here: 70.9 us
  starting transfers between devices  37.6 us (53%)
  waiting for transfers between devices  19 us (27%)
  Pallas kernels  13.4 us (19%)
  between operations  0.77 us (1%)
    ppermute x11, starting transfers between devices, move(): return lax.ppermute(block, 'tm', route)  23.9 us
    ppermute x11, waiting for transfers between devices, move(): return lax.ppermute(block, 'tm', route)  19 us
    pallas_call x1, Pallas kernels, per_device(): pl.pallas_call(functools.partial(query_kernel, n_tm, n_height), out_shape...  7.23 us
    ppermute x1, starting transfers between devices, per_device(): face_2 = lax.ppermute(after(key_value, qg_a), 'height', pairs_2)  6.01 us
    ppermute x1, starting transfers between devices, per_device(): back_1 = lax.ppermute(face_1_grads, 'height', pairs_1)  3.7 us
    ppermute x1, starting transfers between devices, per_device(): back_2 = lax.ppermute(face_2_grads, 'height', pairs_2)  3.05 us
    pallas_call x1, Pallas kernels, per_device(): pl.pallas_call(last_kernel, out_shape=(jax.ShapeDtypeStruct((tile, width)...  2.29 us
    pallas_call x1, Pallas kernels, per_device(): pl.pallas_call(key_kernel, out_shape=jax.ShapeDtypeStruct((2, tile, width...  2.25 us
  transfers between devices with their start and end apart: 15, of which 6 were waited for; matrix products, arithmetic and copies ran while one was open for 0% of the time, Pallas kernels for 13%

profile of v6, /device:TPU:1, one launch (start us, length us, event | category | flops | bytes accessed | tf_op | source)
XLA Modules:
  0.0 70.9 jit_solution(16659576724732187569)
XLA Ops:
  0.6 0.0 copy-start
  0.6 1.6 %pairs.1 = (bf16[2,128,1536]{2,1,0:T(8,128)(2,1)S(1)}, bf16[2,128,1536]{2,1,0:T(8,128)(2,1)S(1)}) custom-call(bf16[128,1536]{1,0:T(8,128)(2,1)} %bitcast.14, bf16[128,1536]{1,0:T(8,128)(2,1)} %bitcast.15, bf16[128,1536]{1,0:T(8,128)(2,1)} %bitcast.16, bf16[128,1536]{1,0:T(8,128)(2,1)} %bitcast.17), custom_call_target="tpu_custom_call" | custom-call | bytes 3145728 | tf_op jit(solution)/shard_map/pairs/pallas_call | solution.py:73
  2.2 2.1 %collective-permute-start.3 = (bf16[2,128,1536]{2,1,0:T(8,128)(2,1)S(1)}, bf16[2,128,1536]{2,1,0:T(8,128)(2,1)}, u32[]{:S(2)}, u32[]{:S(2)}) collective-permute-start(bf16[2,128,1536]{2,1,0:T(8,128)(2,1)S(1)} %get-tuple-element.20.own.keys), channel_id=1, source_target_pairs={{0,4},{4,0},{8,12},{12,8},{16,20},{20,16},{24,28},{28,24},{1,5},{5... | collective-permute-start | bytes 2359304 | tf_op jit(solution)/shard_map/ppermute | solution.py:268
  4.4 1.0 %collective-permute-start = (bf16[2,128,1536]{2,1,0:T(8,128)(2,1)S(1)}, bf16[2,128,1536]{2,1,0:T(8,128)(2,1)S(1)}, u32[]{:S(2)}, u32[]{:S(2)}) collective-permute-start(bf16[2,128,1536]{2,1,0:T(8,128)(2,1)S(1)} %get-tuple-element.20.own.keys), channel_id=1, source_target_pairs={{0,1},{1,0},{2,3},{3,2},{4,5},{5,4},{6,7},{7,6},{8,9},{9,8},{10,11... | collective-permute-start | bytes 2359304 | tf_op jit(solution)/shard_map/ppermute | solution.py:273
  5.3 1.3 %collective-permute-start.1 = (bf16[2,128,1536]{2,1,0:T(8,128)(2,1)S(1)}, bf16[2,128,1536]{2,1,0:T(8,128)(2,1)S(1)}, u32[]{:S(2)}, u32[]{:S(2)}) collective-permute-start(bf16[2,128,1536]{2,1,0:T(8,128)(2,1)S(1)} %get-tuple-element.26.mine), channel_id=1, source_target_pairs={{4,12},{8,0},{12,20},{16,8},{20,28},{24,16},{5,13},{9,1},{13,21},{... | collective-permute-start | bytes 2359304 | tf_op jit(solution)/shard_map/ppermute | solution.py:268
  6.6 4.9 %collective-permute-start.5 = (bf16[2,128,1536]{2,1,0:T(8,128)(2,1)S(1)}, bf16[2,128,1536]{2,1,0:T(8,128)(2,1)}, u32[]{:S(2)}, u32[]{:S(2)}) collective-permute-start(bf16[2,128,1536]{2,1,0:T(8,128)(2,1)S(1)} %get-tuple-element.20.own.keys), channel_id=1, source_target_pairs={{0,8},{8,16},{12,4},{16,24},{20,12},{28,20},{1,9},{9,17},{13,5},{1... | collective-permute-start | bytes 2359304 | tf_op jit(solution)/shard_map/ppermute | solution.py:268
  11.5 0.0 collective-permute-start.9
  11.5 10.2 %collective-permute-done.3.part = bf16[2,128,1536]{2,1,0:T(8,128)(2,1)} collective-permute-done((bf16[2,128,1536]{2,1,0:T(8,128)(2,1)S(1)}, bf16[2,128,1536]{2,1,0:T(8,128)(2,1)}, u32[]{:S(2)}, u32[]{:S(2)}) %collective-permute-start.3) | collective-permute-done | bytes 786464 | tf_op jit(solution)/shard_map/ppermute | solution.py:268
  21.7 0.0 collective-permute-done
  21.7 0.0 copy-start.1
  21.7 4.0 %collective-permute-start.6 = (bf16[2,128,1536]{2,1,0:T(8,128)(2,1)}, bf16[2,128,1536]{2,1,0:T(8,128)(2,1)}, u32[]{:S(2)}, u32[]{:S(2)}) collective-permute-start(bf16[2,128,1536]{2,1,0:T(8,128)(2,1)} %collective-permute-done.3.part), channel_id=1, source_target_pairs={{0,8},{8,16},{12,4},{16,24},{20,12},{28,20},{1,9},{9,17},{13,5},{1... | collective-permute-start | bytes 2359304 | tf_op jit(solution)/shard_map/ppermute | solution.py:268
  25.7 1.3 %collective-permute-start.4 = (bf16[2,128,1536]{2,1,0:T(8,128)(2,1)S(1)}, bf16[2,128,1536]{2,1,0:T(8,128)(2,1)}, u32[]{:S(2)}, u32[]{:S(2)}) collective-permute-start(bf16[2,128,1536]{2,1,0:T(8,128)(2,1)S(1)} %get-tuple-element.20.own.keys), channel_id=1, source_target_pairs={{4,12},{8,0},{12,20},{16,8},{20,28},{24,16},{5,13},{9,1},{13,21},{... | collective-permute-start | bytes 2359304 | tf_op jit(solution)/shard_map/ppermute | solution.py:268
  27.0 0.0 collective-permute-done.1.a
  27.0 6.0 %collective-permute-start.2 = (bf16[2,128,1536]{2,1,0:T(8,128)(2,1)S(1)}, bf16[2,128,1536]{2,1,0:T(8,128)(2,1)}, u32[]{:S(2)}, u32[]{:S(2)}) collective-permute-start(bf16[2,128,1536]{2,1,0:T(8,128)(2,1)S(1)} %get-tuple-element.20.own.keys), channel_id=1, source_target_pairs={{1,2},{2,1},{5,6},{6,5},{9,10},{10,9},{13,14},{14,13},{17,18},{18,... | collective-permute-start | bytes 2359304 | tf_op jit(solution)/shard_map/ppermute | solution.py:278
  33.1 0.0 copy-done.1
  33.1 0.0 copy-done
  33.1 0.1 copy.8.picks
  33.2 0.0 collective-permute-done.5.b
  33.2 4.3 %collective-permute-start.10 = (bf16[2,128,1536]{2,1,0:T(8,128)(2,1)S(1)}, bf16[2,128,1536]{2,1,0:T(8,128)(2,1)S(1)}, u32[]{:S(2)}, u32[]{:S(2)}) collective-permute-start(bf16[2,128,1536]{2,1,0:T(8,128)(2,1)S(1)} %get-tuple-element.26.mine), channel_id=1, source_target_pairs={{0,8},{8,16},{12,4},{16,24},{20,12},{28,20},{1,9},{9,17},{13,5},{1... | collective-permute-start | bytes 2359304 | tf_op jit(solution)/shard_map/ppermute | solution.py:268
  37.5 1.1 %collective-permute-done.9.part = bf16[2,128,1536]{2,1,0:T(8,128)(2,1)S(1)} collective-permute-done((bf16[2,128,1536]{2,1,0:T(8,128)(2,1)S(1)}, bf16[2,128,1536]{2,1,0:T(8,128)(2,1)S(1)}, u32[]{:S(2)}, u32[]{:S(2)}) %collective-permute-start.9) | collective-permute-done | bytes 786464 | tf_op jit(solution)/shard_map/ppermute | solution.py:268
  38.6 1.1 %collective-permute-start.11 = (bf16[2,128,1536]{2,1,0:T(8,128)(2,1)S(1)}, bf16[2,128,1536]{2,1,0:T(8,128)(2,1)S(1)}, u32[]{:S(2)}, u32[]{:S(2)}) collective-permute-start(bf16[2,128,1536]{2,1,0:T(8,128)(2,1)S(1)} %collective-permute-done.1.a), channel_id=1, source_target_pairs={{0,4},{4,0},{8,12},{12,8},{16,20},{20,16},{24,28},{28,24},{1,5},{5... | collective-permute-start | bytes 2359304 | tf_op jit(solution)/shard_map/ppermute | solution.py:268
  39.7 4.3 %collective-permute-done.6.outer = bf16[2,128,1536]{2,1,0:T(8,128)(2,1)} collective-permute-done((bf16[2,128,1536]{2,1,0:T(8,128)(2,1)}, bf16[2,128,1536]{2,1,0:T(8,128)(2,1)}, u32[]{:S(2)}, u32[]{:S(2)}) %collective-permute-start.6) | collective-permute-done | bytes 786464 | tf_op jit(solution)/shard_map/ppermute | solution.py:268
  44.0 0.0 collective-permute-done.4.a
  44.0 0.0 collective-permute-done.2
  44.0 7.2 %query_side.1 = (bf16[128,1536]{1,0:T(8,128)(2,1)}, f32[2,128,1536]{2,1,0:T(8,128)S(1)}, bf16[2,64,1536]{2,1,0:T(8,128)(2,1)S(1)}, bf16[2,64,1536]{2,1,0:T(8,128)(2,1)S(1)}, f32[5,12,128]{2,1,0:T(8,128)S(1)}) custom-call(bf16[2,128,1536]{2,1,0:T(8,128)(2,1)S(1)} %get-tuple-element.26.mine, bf16[2,128,1536]{2,1,0:T(8,128)(2,1)S(1)} %get-tuple-element.20.own.keys, ...), custom_call_target="tpu_custom_call" | custom-call | flops 10066329600 | bytes 4194304 | tf_op jit(solution)/shard_map/query_side/pallas_call | solution.py:286
  51.3 3.7 %collective-permute-start.7 = (bf16[2,64,1536]{2,1,0:T(8,128)(2,1)S(1)}, bf16[2,64,1536]{2,1,0:T(8,128)(2,1)S(1)}, u32[]{:S(2)}, u32[]{:S(2)}) collective-permute-start(bf16[2,64,1536]{2,1,0:T(8,128)(2,1)S(1)} %get-tuple-element.24), channel_id=1, source_target_pairs={{0,1},{1,0},{2,3},{3,2},{4,5},{5,4},{6,7},{7,6},{8,9},{9,8},{10,11... | collective-permute-start | bytes 1179656 | tf_op jit(solution)/shard_map/ppermute | solution.py:315
  55.0 3.0 %collective-permute-start.8 = (bf16[2,64,1536]{2,1,0:T(8,128)(2,1)S(1)}, bf16[2,64,1536]{2,1,0:T(8,128)(2,1)S(1)}, u32[]{:S(2)}, u32[]{:S(2)}) collective-permute-start(bf16[2,64,1536]{2,1,0:T(8,128)(2,1)S(1)} %get-tuple-element.25), channel_id=1, source_target_pairs={{1,2},{2,1},{5,6},{6,5},{9,10},{10,9},{13,14},{14,13},{17,18},{18,... | collective-permute-start | bytes 1179656 | tf_op jit(solution)/shard_map/ppermute | solution.py:316
  58.0 0.7 %collective-permute-start.12 = (f32[5,12,128]{2,1,0:T(8,128)S(1)}, f32[5,12,128]{2,1,0:T(8,128)S(1)}, u32[]{:S(2)}, u32[]{:S(2)}) collective-permute-start(f32[5,12,128]{2,1,0:T(8,128)S(1)} %get-tuple-element.28), channel_id=1, source_target_pairs={{0,4},{4,0},{8,12},{12,8},{16,20},{20,16},{24,28},{28,24},{1,5},{5... | collective-permute-start | bytes 92168 | tf_op jit(solution)/shard_map/ppermute | solution.py:268
  58.8 2.2 %collective-permute-done.12.of_part = f32[5,12,128]{2,1,0:T(8,128)S(1)} collective-permute-done((f32[5,12,128]{2,1,0:T(8,128)S(1)}, f32[5,12,128]{2,1,0:T(8,128)S(1)}, u32[]{:S(2)}, u32[]{:S(2)}) %collective-permute-start.12) | collective-permute-done | bytes 30752 | tf_op jit(solution)/shard_map/ppermute | solution.py:268
  61.0 2.9 %collective-permute-start.13 = (f32[2,5,12,128]{3,2,1,0:T(8,128)S(1)}, f32[2,5,12,128]{3,2,1,0:T(8,128)S(1)}, u32[]{:S(2)}, u32[]{:S(2)}) collective-permute-start(f32[2,5,12,128]{3,2,1,0:T(8,128)S(1)} %pad_maximum_fusion), channel_id=1, source_target_pairs={{0,8},{8,16},{12,4},{16,24},{20,12},{28,20},{1,9},{9,17},{13,5},{1... | collective-permute-start | bytes 184328 | tf_op jit(solution)/shard_map/ppermute | solution.py:268
  63.8 0.0 collective-permute-done.10.b
  63.9 1.3 %collective-permute-start.14 = (f32[5,12,128]{2,1,0:T(8,128)S(1)}, f32[5,12,128]{2,1,0:T(8,128)S(1)}, u32[]{:S(2)}, u32[]{:S(2)}) collective-permute-start(f32[5,12,128]{2,1,0:T(8,128)S(1)} %get-tuple-element.28), channel_id=1, source_target_pairs={{4,12},{8,0},{12,20},{16,8},{20,28},{24,16},{5,13},{9,1},{13,21},{... | collective-permute-start | bytes 92168 | tf_op jit(solution)/shard_map/ppermute | solution.py:268
  65.2 0.0 collective-permute-done.11.outer
  65.2 0.1 collective-permute-done.13.of_b
  65.3 0.0 collective-permute-done.7.face_1_grads
  65.3 0.0 collective-permute-done.8.face_2_grads
  65.3 2.2 %key_side.1.sums = f32[2,128,1536]{2,1,0:T(8,128)S(1)} custom-call(bf16[2,128,1536]{2,1,0:T(8,128)(2,1)S(1)} %get-tuple-element.20.own.keys, f32[2,128,1536]{2,1,0:T(8,128)S(1)} %get-tuple-element.23.own_grads, bf16[2,64,1536]{2,1,0:T(8,128)(2,1)S(1)} %collective-permute-done.7.face_1_grads, bf16[2,64,1536]{2,1,0:T(8,128)(2,1)S(1)} %collective-permute-done.8.face_2_grads, ...), custom_call_target="tpu_custom_call" | custom-call | flops 4026531840 | bytes 4194304 | tf_op jit(solution)/shard_map/key_side/pallas_call | solution.py:318
  67.6 1.0 %collective-permute-done.14.of_a = f32[5,12,128]{2,1,0:T(8,128)S(1)} collective-permute-done((f32[5,12,128]{2,1,0:T(8,128)S(1)}, f32[5,12,128]{2,1,0:T(8,128)S(1)}, u32[]{:S(2)}, u32[]{:S(2)}) %collective-permute-start.14) | collective-permute-done | bytes 30752 | tf_op jit(solution)/shard_map/ppermute | solution.py:268
  68.6 2.3 %last_side.1 = (bf16[128,1536]{1,0:T(8,128)(2,1)}, bf16[128,1536]{1,0:T(8,128)(2,1)}) custom-call(bf16[2,128,1536]{2,1,0:T(8,128)(2,1)S(1)} %get-tuple-element.20.own.keys, f32[2,128,1536]{2,1,0:T(8,128)S(1)} %key_side.1.sums, bf16[2,128,1536]{2,1,0:T(8,128)(2,1)S(1)} %collective-permute-done.1.a, f32[5,12,128]{2,1,0:T(8,128)S(1)} %collective-permute-done.14.of_a), custom_call_target="tpu_custom_call" | custom-call | flops 1509949440 | bytes 4194304 | tf_op jit(solution)/shard_map/last_side/pallas_call | solution.py:328
  (1 shorter events, 0.0 us)
Async XLA Ops:
  0.6 32.4 %copy-start = (s32[1,1,12,2]{2,3,1,0:T(2,128)S(1)}, s32[1,1,12,2]{2,3,1,0:T(2,128)}, u32[]{:S(2)}) copy-start(s32[1,1,12,2]{2,3,1,0:T(2,128)} %param.9) | copy-start | bytes 292
  2.2 19.5 %collective-permute-start.3 = (bf16[2,128,1536]{2,1,0:T(8,128)(2,1)S(1)}, bf16[2,128,1536]{2,1,0:T(8,128)(2,1)}, u32[]{:S(2)}, u32[]{:S(2)}) collective-permute-start(bf16[2,128,1536]{2,1,0:T(8,128)(2,1)S(1)} %get-tuple-element.20.own.keys), channel_id=1, source_target_pairs={{0,4},{4,0},{8,12},{12,8},{16,20},{20,16},{24,28},{28,24},{1,5},{5... | collective-permute-start | bytes 2359304 | tf_op jit(solution)/shard_map/ppermute | solution.py:268
  4.4 17.4 %collective-permute-start = (bf16[2,128,1536]{2,1,0:T(8,128)(2,1)S(1)}, bf16[2,128,1536]{2,1,0:T(8,128)(2,1)S(1)}, u32[]{:S(2)}, u32[]{:S(2)}) collective-permute-start(bf16[2,128,1536]{2,1,0:T(8,128)(2,1)S(1)} %get-tuple-element.20.own.keys), channel_id=1, source_target_pairs={{0,1},{1,0},{2,3},{3,2},{4,5},{5,4},{6,7},{7,6},{8,9},{9,8},{10,11... | collective-permute-start | bytes 2359304 | tf_op jit(solution)/shard_map/ppermute | solution.py:273
  5.3 21.7 %collective-permute-start.1 = (bf16[2,128,1536]{2,1,0:T(8,128)(2,1)S(1)}, bf16[2,128,1536]{2,1,0:T(8,128)(2,1)S(1)}, u32[]{:S(2)}, u32[]{:S(2)}) collective-permute-start(bf16[2,128,1536]{2,1,0:T(8,128)(2,1)S(1)} %get-tuple-element.26.mine), channel_id=1, source_target_pairs={{4,12},{8,0},{12,20},{16,8},{20,28},{24,16},{5,13},{9,1},{13,21},{... | collective-permute-start | bytes 2359304 | tf_op jit(solution)/shard_map/ppermute | solution.py:268
  6.6 26.6 %collective-permute-start.5 = (bf16[2,128,1536]{2,1,0:T(8,128)(2,1)S(1)}, bf16[2,128,1536]{2,1,0:T(8,128)(2,1)}, u32[]{:S(2)}, u32[]{:S(2)}) collective-permute-start(bf16[2,128,1536]{2,1,0:T(8,128)(2,1)S(1)} %get-tuple-element.20.own.keys), channel_id=1, source_target_pairs={{0,8},{8,16},{12,4},{16,24},{20,12},{28,20},{1,9},{9,17},{13,5},{1... | collective-permute-start | bytes 2359304 | tf_op jit(solution)/shard_map/ppermute | solution.py:268
  11.5 27.1 %collective-permute-start.9 = (bf16[2,128,1536]{2,1,0:T(8,128)(2,1)S(1)}, bf16[2,128,1536]{2,1,0:T(8,128)(2,1)S(1)}, u32[]{:S(2)}, u32[]{:S(2)}) collective-permute-start(bf16[2,128,1536]{2,1,0:T(8,128)(2,1)S(1)} %get-tuple-element.26.mine), channel_id=1, source_target_pairs={{0,4},{4,0},{8,12},{12,8},{16,20},{20,16},{24,28},{28,24},{1,5},{5... | collective-permute-start | bytes 2359304 | tf_op jit(solution)/shard_map/ppermute | solution.py:268
  21.7 11.3 %copy-start.1 = (bf16[2,128,1536]{2,1,0:T(8,128)(2,1)}, bf16[2,128,1536]{2,1,0:T(8,128)(2,1)S(1)}, u32[]{:S(2)}) copy-start(bf16[2,128,1536]{2,1,0:T(8,128)(2,1)S(1)} %collective-permute-done) | copy-start | bytes 2359300
  21.7 22.3 %collective-permute-start.6 = (bf16[2,128,1536]{2,1,0:T(8,128)(2,1)}, bf16[2,128,1536]{2,1,0:T(8,128)(2,1)}, u32[]{:S(2)}, u32[]{:S(2)}) collective-permute-start(bf16[2,128,1536]{2,1,0:T(8,128)(2,1)} %collective-permute-done.3.part), channel_id=1, source_target_pairs={{0,8},{8,16},{12,4},{16,24},{20,12},{28,20},{1,9},{9,17},{13,5},{1... | collective-permute-start | bytes 2359304 | tf_op jit(solution)/shard_map/ppermute | solution.py:268
  25.7 18.3 %collective-permute-start.4 = (bf16[2,128,1536]{2,1,0:T(8,128)(2,1)S(1)}, bf16[2,128,1536]{2,1,0:T(8,128)(2,1)}, u32[]{:S(2)}, u32[]{:S(2)}) collective-permute-start(bf16[2,128,1536]{2,1,0:T(8,128)(2,1)S(1)} %get-tuple-element.20.own.keys), channel_id=1, source_target_pairs={{4,12},{8,0},{12,20},{16,8},{20,28},{24,16},{5,13},{9,1},{13,21},{... | collective-permute-start | bytes 2359304 | tf_op jit(solution)/shard_map/ppermute | solution.py:268
  27.0 17.0 %collective-permute-start.2 = (bf16[2,128,1536]{2,1,0:T(8,128)(2,1)S(1)}, bf16[2,128,1536]{2,1,0:T(8,128)(2,1)}, u32[]{:S(2)}, u32[]{:S(2)}) collective-permute-start(bf16[2,128,1536]{2,1,0:T(8,128)(2,1)S(1)} %get-tuple-element.20.own.keys), channel_id=1, source_target_pairs={{1,2},{2,1},{5,6},{6,5},{9,10},{10,9},{13,14},{14,13},{17,18},{18,... | collective-permute-start | bytes 2359304 | tf_op jit(solution)/shard_map/ppermute | solution.py:278
  33.2 30.7 %collective-permute-start.10 = (bf16[2,128,1536]{2,1,0:T(8,128)(2,1)S(1)}, bf16[2,128,1536]{2,1,0:T(8,128)(2,1)S(1)}, u32[]{:S(2)}, u32[]{:S(2)}) collective-permute-start(bf16[2,128,1536]{2,1,0:T(8,128)(2,1)S(1)} %get-tuple-element.26.mine), channel_id=1, source_target_pairs={{0,8},{8,16},{12,4},{16,24},{20,12},{28,20},{1,9},{9,17},{13,5},{1... | collective-permute-start | bytes 2359304 | tf_op jit(solution)/shard_map/ppermute | solution.py:268
  38.6 26.6 %collective-permute-start.11 = (bf16[2,128,1536]{2,1,0:T(8,128)(2,1)S(1)}, bf16[2,128,1536]{2,1,0:T(8,128)(2,1)S(1)}, u32[]{:S(2)}, u32[]{:S(2)}) collective-permute-start(bf16[2,128,1536]{2,1,0:T(8,128)(2,1)S(1)} %collective-permute-done.1.a), channel_id=1, source_target_pairs={{0,4},{4,0},{8,12},{12,8},{16,20},{20,16},{24,28},{28,24},{1,5},{5... | collective-permute-start | bytes 2359304 | tf_op jit(solution)/shard_map/ppermute | solution.py:268
  51.3 14.0 %collective-permute-start.7 = (bf16[2,64,1536]{2,1,0:T(8,128)(2,1)S(1)}, bf16[2,64,1536]{2,1,0:T(8,128)(2,1)S(1)}, u32[]{:S(2)}, u32[]{:S(2)}) collective-permute-start(bf16[2,64,1536]{2,1,0:T(8,128)(2,1)S(1)} %get-tuple-element.24), channel_id=1, source_target_pairs={{0,1},{1,0},{2,3},{3,2},{4,5},{5,4},{6,7},{7,6},{8,9},{9,8},{10,11... | collective-permute-start | bytes 1179656 | tf_op jit(solution)/shard_map/ppermute | solution.py:315
  55.0 10.3 %collective-permute-start.8 = (bf16[2,64,1536]{2,1,0:T(8,128)(2,1)S(1)}, bf16[2,64,1536]{2,1,0:T(8,128)(2,1)S(1)}, u32[]{:S(2)}, u32[]{:S(2)}) collective-permute-start(bf16[2,64,1536]{2,1,0:T(8,128)(2,1)S(1)} %get-tuple-element.25), channel_id=1, source_target_pairs={{1,2},{2,1},{5,6},{6,5},{9,10},{10,9},{13,14},{14,13},{17,18},{18,... | collective-permute-start | bytes 1179656 | tf_op jit(solution)/shard_map/ppermute | solution.py:316
  58.0 2.9 %collective-permute-start.12 = (f32[5,12,128]{2,1,0:T(8,128)S(1)}, f32[5,12,128]{2,1,0:T(8,128)S(1)}, u32[]{:S(2)}, u32[]{:S(2)}) collective-permute-start(f32[5,12,128]{2,1,0:T(8,128)S(1)} %get-tuple-element.28), channel_id=1, source_target_pairs={{0,4},{4,0},{8,12},{12,8},{16,20},{20,16},{24,28},{28,24},{1,5},{5... | collective-permute-start | bytes 92168 | tf_op jit(solution)/shard_map/ppermute | solution.py:268
  61.0 4.3 %collective-permute-start.13 = (f32[2,5,12,128]{3,2,1,0:T(8,128)S(1)}, f32[2,5,12,128]{3,2,1,0:T(8,128)S(1)}, u32[]{:S(2)}, u32[]{:S(2)}) collective-permute-start(f32[2,5,12,128]{3,2,1,0:T(8,128)S(1)} %pad_maximum_fusion), channel_id=1, source_target_pairs={{0,8},{8,16},{12,4},{16,24},{20,12},{28,20},{1,9},{9,17},{13,5},{1... | collective-permute-start | bytes 184328 | tf_op jit(solution)/shard_map/ppermute | solution.py:268
  63.9 4.7 %collective-permute-start.14 = (f32[5,12,128]{2,1,0:T(8,128)S(1)}, f32[5,12,128]{2,1,0:T(8,128)S(1)}, u32[]{:S(2)}, u32[]{:S(2)}) collective-permute-start(f32[5,12,128]{2,1,0:T(8,128)S(1)} %get-tuple-element.28), channel_id=1, source_target_pairs={{4,12},{8,0},{12,20},{16,8},{20,28},{24,16},{5,13},{9,1},{13,21},{... | collective-permute-start | bytes 92168 | tf_op jit(solution)/shard_map/ppermute | solution.py:268

commit v7 on v6

--- a/solution.py
+++ b/solution.py
@@ -198,29 +198,30 @@
 
 
 def far_grads(keys, others, sums, store, scratch):
-    heads = keys.shape[2] // HEAD_DIM
+    heads, slots = keys.shape[2] // HEAD_DIM, scratch.shape[0]
 
     def products(e):
         cols = columns(e)
         pair = jnp.concatenate([keys[0, :, cols], keys[1, :, cols]], axis=1)
         for i, (block, _, _) in enumerate(others):
-            scratch[e % 2, i] = dot(pair, corners(block[0, :, cols], block[1, :, cols]), NT)
+            scratch[e % slots, i] = dot(pair, corners(block[0, :, cols], block[1, :, cols]), NT)
 
     def finish(e):
         cols = columns(e)
         total = jnp.concatenate([sums[0, :, cols], sums[1, :, cols]], axis=1)
         for i, (block, stats, slot) in enumerate(others):
-            score, grad_weights = scratch[e % 2, i, :, :HEAD_DIM], scratch[e % 2, i, :, HEAD_DIM:]
+            score, grad_weights = scratch[e % slots, i, :, :HEAD_DIM], scratch[e % slots, i, :, HEAD_DIM:]
             weights = jnp.exp2(score * (SCALE * LOG2E) - stats[slot, e : e + 1, :])
             dscore = weights * (grad_weights - stats[0, e : e + 1, :]) * SCALE
             both = jnp.concatenate([dscore.astype(jnp.bfloat16), weights.astype(jnp.bfloat16)], axis=1)
             total += dot(both, corners(block[0, :, cols], block[1, :, cols]), NN)
         store(cols, total)
 
-    products(0)
+    for e in range(slots - 1):
+        products(e)
     for e in range(heads):
-        if e + 1 < heads:
-            products(e + 1)
+        if e + slots - 1 < heads:
+            products(e + slots - 1)
         finish(e)
 
 
@@ -330,7 +331,7 @@
         out_shape=(jax.ShapeDtypeStruct((tile, width), bf16),) * 2,
         in_specs=[vmem] * 4,
         out_specs=[vmem] * 2,
-        scratch_shapes=[pltpu.VMEM((2, 1, tile, 2 * HEAD_DIM), f32)],
+        scratch_shapes=[pltpu.VMEM((4, 1, tile, 2 * HEAD_DIM), f32)],
         compiler_params=params,
         cost_estimate=pl.CostEstimate(flops=30 * block, bytes_accessed=4 << 20, transcendentals=0),
         name="last_side",

time: 71.5 us -> 71 us (level)
  no operation moved by 1% of the time
where the time goes in v7:
time: 71 us; the launch traced here: 70.4 us
  starting transfers between devices  37.6 us (53%)
  waiting for transfers between devices  19 us (27%)
  Pallas kernels  12.9 us (18%)
  between operations  0.77 us (1%)
    ppermute x11, starting transfers between devices, move(): return lax.ppermute(block, 'tm', route)  23.9 us
    ppermute x11, waiting for transfers between devices, move(): return lax.ppermute(block, 'tm', route)  19 us
    pallas_call x1, Pallas kernels, per_device(): pl.pallas_call(functools.partial(query_kernel, n_tm, n_height), out_shape...  7.23 us
    ppermute x1, starting transfers between devices, per_device(): face_2 = lax.ppermute(after(key_value, qg_a), 'height', pairs_2)  6.01 us
    ppermute x1, starting transfers between devices, per_device(): back_1 = lax.ppermute(face_1_grads, 'height', pairs_1)  3.7 us
    ppermute x1, starting transfers between devices, per_device(): back_2 = lax.ppermute(face_2_grads, 'height', pairs_2)  3.05 us
    pallas_call x1, Pallas kernels, per_device(): pl.pallas_call(key_kernel, out_shape=jax.ShapeDtypeStruct((2, tile, width...  2.25 us
    pallas_call x1, Pallas kernels, per_device(): pl.pallas_call(last_kernel, out_shape=(jax.ShapeDtypeStruct((tile, width)...  1.82 us
  transfers between devices with their start and end apart: 15, of which 6 were waited for; matrix products, arithmetic and copies ran while one was open for 0% of the time, Pallas kernels for 13%

profile of v7, /device:TPU:1, one launch (start us, length us, event | category | flops | bytes accessed | tf_op | source)
XLA Modules:
  0.0 70.4 jit_solution(10110466444853218790)
XLA Ops:
  0.6 0.0 copy-start
  0.6 1.6 %pairs.1 = (bf16[2,128,1536]{2,1,0:T(8,128)(2,1)S(1)}, bf16[2,128,1536]{2,1,0:T(8,128)(2,1)S(1)}) custom-call(bf16[128,1536]{1,0:T(8,128)(2,1)} %bitcast.14, bf16[128,1536]{1,0:T(8,128)(2,1)} %bitcast.15, bf16[128,1536]{1,0:T(8,128)(2,1)} %bitcast.16, bf16[128,1536]{1,0:T(8,128)(2,1)} %bitcast.17), custom_call_target="tpu_custom_call" | custom-call | bytes 3145728 | tf_op jit(solution)/shard_map/pairs/pallas_call | solution.py:73
  2.2 2.1 %collective-permute-start.3 = (bf16[2,128,1536]{2,1,0:T(8,128)(2,1)S(1)}, bf16[2,128,1536]{2,1,0:T(8,128)(2,1)}, u32[]{:S(2)}, u32[]{:S(2)}) collective-permute-start(bf16[2,128,1536]{2,1,0:T(8,128)(2,1)S(1)} %get-tuple-element.20.own.keys), channel_id=1, source_target_pairs={{0,4},{4,0},{8,12},{12,8},{16,20},{20,16},{24,28},{28,24},{1,5},{5... | collective-permute-start | bytes 2359304 | tf_op jit(solution)/shard_map/ppermute | solution.py:269
  4.4 1.0 %collective-permute-start = (bf16[2,128,1536]{2,1,0:T(8,128)(2,1)S(1)}, bf16[2,128,1536]{2,1,0:T(8,128)(2,1)S(1)}, u32[]{:S(2)}, u32[]{:S(2)}) collective-permute-start(bf16[2,128,1536]{2,1,0:T(8,128)(2,1)S(1)} %get-tuple-element.20.own.keys), channel_id=1, source_target_pairs={{0,1},{1,0},{2,3},{3,2},{4,5},{5,4},{6,7},{7,6},{8,9},{9,8},{10,11... | collective-permute-start | bytes 2359304 | tf_op jit(solution)/shard_map/ppermute | solution.py:274
  5.3 1.3 %collective-permute-start.1 = (bf16[2,128,1536]{2,1,0:T(8,128)(2,1)S(1)}, bf16[2,128,1536]{2,1,0:T(8,128)(2,1)S(1)}, u32[]{:S(2)}, u32[]{:S(2)}) collective-permute-start(bf16[2,128,1536]{2,1,0:T(8,128)(2,1)S(1)} %get-tuple-element.26.mine), channel_id=1, source_target_pairs={{4,12},{8,0},{12,20},{16,8},{20,28},{24,16},{5,13},{9,1},{13,21},{... | collective-permute-start | bytes 2359304 | tf_op jit(solution)/shard_map/ppermute | solution.py:269
  6.6 4.9 %collective-permute-start.5 = (bf16[2,128,1536]{2,1,0:T(8,128)(2,1)S(1)}, bf16[2,128,1536]{2,1,0:T(8,128)(2,1)}, u32[]{:S(2)}, u32[]{:S(2)}) collective-permute-start(bf16[2,128,1536]{2,1,0:T(8,128)(2,1)S(1)} %get-tuple-element.20.own.keys), channel_id=1, source_target_pairs={{0,8},{8,16},{12,4},{16,24},{20,12},{28,20},{1,9},{9,17},{13,5},{1... | collective-permute-start | bytes 2359304 | tf_op jit(solution)/shard_map/ppermute | solution.py:269
  11.5 0.0 collective-permute-start.9
  11.5 10.2 %collective-permute-done.3.part = bf16[2,128,1536]{2,1,0:T(8,128)(2,1)} collective-permute-done((bf16[2,128,1536]{2,1,0:T(8,128)(2,1)S(1)}, bf16[2,128,1536]{2,1,0:T(8,128)(2,1)}, u32[]{:S(2)}, u32[]{:S(2)}) %collective-permute-start.3) | collective-permute-done | bytes 786464 | tf_op jit(solution)/shard_map/ppermute | solution.py:269
  21.7 0.0 collective-permute-done
  21.7 0.0 copy-start.1
  21.7 4.0 %collective-permute-start.6 = (bf16[2,128,1536]{2,1,0:T(8,128)(2,1)}, bf16[2,128,1536]{2,1,0:T(8,128)(2,1)}, u32[]{:S(2)}, u32[]{:S(2)}) collective-permute-start(bf16[2,128,1536]{2,1,0:T(8,128)(2,1)} %collective-permute-done.3.part), channel_id=1, source_target_pairs={{0,8},{8,16},{12,4},{16,24},{20,12},{28,20},{1,9},{9,17},{13,5},{1... | collective-permute-start | bytes 2359304 | tf_op jit(solution)/shard_map/ppermute | solution.py:269
  25.7 1.3 %collective-permute-start.4 = (bf16[2,128,1536]{2,1,0:T(8,128)(2,1)S(1)}, bf16[2,128,1536]{2,1,0:T(8,128)(2,1)}, u32[]{:S(2)}, u32[]{:S(2)}) collective-permute-start(bf16[2,128,1536]{2,1,0:T(8,128)(2,1)S(1)} %get-tuple-element.20.own.keys), channel_id=1, source_target_pairs={{4,12},{8,0},{12,20},{16,8},{20,28},{24,16},{5,13},{9,1},{13,21},{... | collective-permute-start | bytes 2359304 | tf_op jit(solution)/shard_map/ppermute | solution.py:269
  27.0 0.0 collective-permute-done.1.a
  27.0 6.0 %collective-permute-start.2 = (bf16[2,128,1536]{2,1,0:T(8,128)(2,1)S(1)}, bf16[2,128,1536]{2,1,0:T(8,128)(2,1)}, u32[]{:S(2)}, u32[]{:S(2)}) collective-permute-start(bf16[2,128,1536]{2,1,0:T(8,128)(2,1)S(1)} %get-tuple-element.20.own.keys), channel_id=1, source_target_pairs={{1,2},{2,1},{5,6},{6,5},{9,10},{10,9},{13,14},{14,13},{17,18},{18,... | collective-permute-start | bytes 2359304 | tf_op jit(solution)/shard_map/ppermute | solution.py:279
  33.1 0.0 copy-done.1
  33.1 0.0 copy-done
  33.1 0.1 copy.8.picks
  33.2 0.0 collective-permute-done.5.b
  33.2 4.3 %collective-permute-start.10 = (bf16[2,128,1536]{2,1,0:T(8,128)(2,1)S(1)}, bf16[2,128,1536]{2,1,0:T(8,128)(2,1)S(1)}, u32[]{:S(2)}, u32[]{:S(2)}) collective-permute-start(bf16[2,128,1536]{2,1,0:T(8,128)(2,1)S(1)} %get-tuple-element.26.mine), channel_id=1, source_target_pairs={{0,8},{8,16},{12,4},{16,24},{20,12},{28,20},{1,9},{9,17},{13,5},{1... | collective-permute-start | bytes 2359304 | tf_op jit(solution)/shard_map/ppermute | solution.py:269
  37.5 1.1 %collective-permute-done.9.part = bf16[2,128,1536]{2,1,0:T(8,128)(2,1)S(1)} collective-permute-done((bf16[2,128,1536]{2,1,0:T(8,128)(2,1)S(1)}, bf16[2,128,1536]{2,1,0:T(8,128)(2,1)S(1)}, u32[]{:S(2)}, u32[]{:S(2)}) %collective-permute-start.9) | collective-permute-done | bytes 786464 | tf_op jit(solution)/shard_map/ppermute | solution.py:269
  38.6 1.1 %collective-permute-start.11 = (bf16[2,128,1536]{2,1,0:T(8,128)(2,1)S(1)}, bf16[2,128,1536]{2,1,0:T(8,128)(2,1)S(1)}, u32[]{:S(2)}, u32[]{:S(2)}) collective-permute-start(bf16[2,128,1536]{2,1,0:T(8,128)(2,1)S(1)} %collective-permute-done.1.a), channel_id=1, source_target_pairs={{0,4},{4,0},{8,12},{12,8},{16,20},{20,16},{24,28},{28,24},{1,5},{5... | collective-permute-start | bytes 2359304 | tf_op jit(solution)/shard_map/ppermute | solution.py:269
  39.7 4.3 %collective-permute-done.6.outer = bf16[2,128,1536]{2,1,0:T(8,128)(2,1)} collective-permute-done((bf16[2,128,1536]{2,1,0:T(8,128)(2,1)}, bf16[2,128,1536]{2,1,0:T(8,128)(2,1)}, u32[]{:S(2)}, u32[]{:S(2)}) %collective-permute-start.6) | collective-permute-done | bytes 786464 | tf_op jit(solution)/shard_map/ppermute | solution.py:269
  44.0 0.0 collective-permute-done.4.a
  44.0 0.0 collective-permute-done.2
  44.0 7.2 %query_side.1 = (bf16[128,1536]{1,0:T(8,128)(2,1)}, f32[2,128,1536]{2,1,0:T(8,128)S(1)}, bf16[2,64,1536]{2,1,0:T(8,128)(2,1)S(1)}, bf16[2,64,1536]{2,1,0:T(8,128)(2,1)S(1)}, f32[5,12,128]{2,1,0:T(8,128)S(1)}) custom-call(bf16[2,128,1536]{2,1,0:T(8,128)(2,1)S(1)} %get-tuple-element.26.mine, bf16[2,128,1536]{2,1,0:T(8,128)(2,1)S(1)} %get-tuple-element.20.own.keys, ...), custom_call_target="tpu_custom_call" | custom-call | flops 10066329600 | bytes 4194304 | tf_op jit(solution)/shard_map/query_side/pallas_call | solution.py:287
  51.3 3.7 %collective-permute-start.7 = (bf16[2,64,1536]{2,1,0:T(8,128)(2,1)S(1)}, bf16[2,64,1536]{2,1,0:T(8,128)(2,1)S(1)}, u32[]{:S(2)}, u32[]{:S(2)}) collective-permute-start(bf16[2,64,1536]{2,1,0:T(8,128)(2,1)S(1)} %get-tuple-element.24), channel_id=1, source_target_pairs={{0,1},{1,0},{2,3},{3,2},{4,5},{5,4},{6,7},{7,6},{8,9},{9,8},{10,11... | collective-permute-start | bytes 1179656 | tf_op jit(solution)/shard_map/ppermute | solution.py:316
  55.0 3.0 %collective-permute-start.8 = (bf16[2,64,1536]{2,1,0:T(8,128)(2,1)S(1)}, bf16[2,64,1536]{2,1,0:T(8,128)(2,1)S(1)}, u32[]{:S(2)}, u32[]{:S(2)}) collective-permute-start(bf16[2,64,1536]{2,1,0:T(8,128)(2,1)S(1)} %get-tuple-element.25), channel_id=1, source_target_pairs={{1,2},{2,1},{5,6},{6,5},{9,10},{10,9},{13,14},{14,13},{17,18},{18,... | collective-permute-start | bytes 1179656 | tf_op jit(solution)/shard_map/ppermute | solution.py:317
  58.0 0.7 %collective-permute-start.12 = (f32[5,12,128]{2,1,0:T(8,128)S(1)}, f32[5,12,128]{2,1,0:T(8,128)S(1)}, u32[]{:S(2)}, u32[]{:S(2)}) collective-permute-start(f32[5,12,128]{2,1,0:T(8,128)S(1)} %get-tuple-element.28), channel_id=1, source_target_pairs={{0,4},{4,0},{8,12},{12,8},{16,20},{20,16},{24,28},{28,24},{1,5},{5... | collective-permute-start | bytes 92168 | tf_op jit(solution)/shard_map/ppermute | solution.py:269
  58.8 2.2 %collective-permute-done.12.of_part = f32[5,12,128]{2,1,0:T(8,128)S(1)} collective-permute-done((f32[5,12,128]{2,1,0:T(8,128)S(1)}, f32[5,12,128]{2,1,0:T(8,128)S(1)}, u32[]{:S(2)}, u32[]{:S(2)}) %collective-permute-start.12) | collective-permute-done | bytes 30752 | tf_op jit(solution)/shard_map/ppermute | solution.py:269
  61.0 2.9 %collective-permute-start.13 = (f32[2,5,12,128]{3,2,1,0:T(8,128)S(1)}, f32[2,5,12,128]{3,2,1,0:T(8,128)S(1)}, u32[]{:S(2)}, u32[]{:S(2)}) collective-permute-start(f32[2,5,12,128]{3,2,1,0:T(8,128)S(1)} %pad_maximum_fusion), channel_id=1, source_target_pairs={{0,8},{8,16},{12,4},{16,24},{20,12},{28,20},{1,9},{9,17},{13,5},{1... | collective-permute-start | bytes 184328 | tf_op jit(solution)/shard_map/ppermute | solution.py:269
  63.8 0.0 collective-permute-done.10.b
  63.9 1.3 %collective-permute-start.14 = (f32[5,12,128]{2,1,0:T(8,128)S(1)}, f32[5,12,128]{2,1,0:T(8,128)S(1)}, u32[]{:S(2)}, u32[]{:S(2)}) collective-permute-start(f32[5,12,128]{2,1,0:T(8,128)S(1)} %get-tuple-element.28), channel_id=1, source_target_pairs={{4,12},{8,0},{12,20},{16,8},{20,28},{24,16},{5,13},{9,1},{13,21},{... | collective-permute-start | bytes 92168 | tf_op jit(solution)/shard_map/ppermute | solution.py:269
  65.2 0.0 collective-permute-done.11.outer
  65.2 0.1 collective-permute-done.13.of_b
  65.3 0.0 collective-permute-done.7.face_1_grads
  65.3 0.0 collective-permute-done.8.face_2_grads
  65.3 2.2 %key_side.1.sums = f32[2,128,1536]{2,1,0:T(8,128)S(1)} custom-call(bf16[2,128,1536]{2,1,0:T(8,128)(2,1)S(1)} %get-tuple-element.20.own.keys, f32[2,128,1536]{2,1,0:T(8,128)S(1)} %get-tuple-element.23.own_grads, bf16[2,64,1536]{2,1,0:T(8,128)(2,1)S(1)} %collective-permute-done.7.face_1_grads, bf16[2,64,1536]{2,1,0:T(8,128)(2,1)S(1)} %collective-permute-done.8.face_2_grads, ...), custom_call_target="tpu_custom_call" | custom-call | flops 4026531840 | bytes 4194304 | tf_op jit(solution)/shard_map/key_side/pallas_call | solution.py:319
  67.6 1.0 %collective-permute-done.14.of_a = f32[5,12,128]{2,1,0:T(8,128)S(1)} collective-permute-done((f32[5,12,128]{2,1,0:T(8,128)S(1)}, f32[5,12,128]{2,1,0:T(8,128)S(1)}, u32[]{:S(2)}, u32[]{:S(2)}) %collective-permute-start.14) | collective-permute-done | bytes 30752 | tf_op jit(solution)/shard_map/ppermute | solution.py:269
  68.6 1.8 %last_side.1 = (bf16[128,1536]{1,0:T(8,128)(2,1)}, bf16[128,1536]{1,0:T(8,128)(2,1)}) custom-call(bf16[2,128,1536]{2,1,0:T(8,128)(2,1)S(1)} %get-tuple-element.20.own.keys, f32[2,128,1536]{2,1,0:T(8,128)S(1)} %key_side.1.sums, bf16[2,128,1536]{2,1,0:T(8,128)(2,1)S(1)} %collective-permute-done.1.a, f32[5,12,128]{2,1,0:T(8,128)S(1)} %collective-permute-done.14.of_a), custom_call_target="tpu_custom_call" | custom-call | flops 1509949440 | bytes 4194304 | tf_op jit(solution)/shard_map/last_side/pallas_call | solution.py:329
  (1 shorter events, 0.0 us)
Async XLA Ops:
  0.6 32.4 %copy-start = (s32[1,1,12,2]{2,3,1,0:T(2,128)S(1)}, s32[1,1,12,2]{2,3,1,0:T(2,128)}, u32[]{:S(2)}) copy-start(s32[1,1,12,2]{2,3,1,0:T(2,128)} %param.9) | copy-start | bytes 292
  2.2 19.5 %collective-permute-start.3 = (bf16[2,128,1536]{2,1,0:T(8,128)(2,1)S(1)}, bf16[2,128,1536]{2,1,0:T(8,128)(2,1)}, u32[]{:S(2)}, u32[]{:S(2)}) collective-permute-start(bf16[2,128,1536]{2,1,0:T(8,128)(2,1)S(1)} %get-tuple-element.20.own.keys), channel_id=1, source_target_pairs={{0,4},{4,0},{8,12},{12,8},{16,20},{20,16},{24,28},{28,24},{1,5},{5... | collective-permute-start | bytes 2359304 | tf_op jit(solution)/shard_map/ppermute | solution.py:269
  4.4 17.4 %collective-permute-start = (bf16[2,128,1536]{2,1,0:T(8,128)(2,1)S(1)}, bf16[2,128,1536]{2,1,0:T(8,128)(2,1)S(1)}, u32[]{:S(2)}, u32[]{:S(2)}) collective-permute-start(bf16[2,128,1536]{2,1,0:T(8,128)(2,1)S(1)} %get-tuple-element.20.own.keys), channel_id=1, source_target_pairs={{0,1},{1,0},{2,3},{3,2},{4,5},{5,4},{6,7},{7,6},{8,9},{9,8},{10,11... | collective-permute-start | bytes 2359304 | tf_op jit(solution)/shard_map/ppermute | solution.py:274
  5.3 21.7 %collective-permute-start.1 = (bf16[2,128,1536]{2,1,0:T(8,128)(2,1)S(1)}, bf16[2,128,1536]{2,1,0:T(8,128)(2,1)S(1)}, u32[]{:S(2)}, u32[]{:S(2)}) collective-permute-start(bf16[2,128,1536]{2,1,0:T(8,128)(2,1)S(1)} %get-tuple-element.26.mine), channel_id=1, source_target_pairs={{4,12},{8,0},{12,20},{16,8},{20,28},{24,16},{5,13},{9,1},{13,21},{... | collective-permute-start | bytes 2359304 | tf_op jit(solution)/shard_map/ppermute | solution.py:269
  6.6 26.6 %collective-permute-start.5 = (bf16[2,128,1536]{2,1,0:T(8,128)(2,1)S(1)}, bf16[2,128,1536]{2,1,0:T(8,128)(2,1)}, u32[]{:S(2)}, u32[]{:S(2)}) collective-permute-start(bf16[2,128,1536]{2,1,0:T(8,128)(2,1)S(1)} %get-tuple-element.20.own.keys), channel_id=1, source_target_pairs={{0,8},{8,16},{12,4},{16,24},{20,12},{28,20},{1,9},{9,17},{13,5},{1... | collective-permute-start | bytes 2359304 | tf_op jit(solution)/shard_map/ppermute | solution.py:269
  11.5 27.1 %collective-permute-start.9 = (bf16[2,128,1536]{2,1,0:T(8,128)(2,1)S(1)}, bf16[2,128,1536]{2,1,0:T(8,128)(2,1)S(1)}, u32[]{:S(2)}, u32[]{:S(2)}) collective-permute-start(bf16[2,128,1536]{2,1,0:T(8,128)(2,1)S(1)} %get-tuple-element.26.mine), channel_id=1, source_target_pairs={{0,4},{4,0},{8,12},{12,8},{16,20},{20,16},{24,28},{28,24},{1,5},{5... | collective-permute-start | bytes 2359304 | tf_op jit(solution)/shard_map/ppermute | solution.py:269
  21.7 11.3 %copy-start.1 = (bf16[2,128,1536]{2,1,0:T(8,128)(2,1)}, bf16[2,128,1536]{2,1,0:T(8,128)(2,1)S(1)}, u32[]{:S(2)}) copy-start(bf16[2,128,1536]{2,1,0:T(8,128)(2,1)S(1)} %collective-permute-done) | copy-start | bytes 2359300
  21.7 22.3 %collective-permute-start.6 = (bf16[2,128,1536]{2,1,0:T(8,128)(2,1)}, bf16[2,128,1536]{2,1,0:T(8,128)(2,1)}, u32[]{:S(2)}, u32[]{:S(2)}) collective-permute-start(bf16[2,128,1536]{2,1,0:T(8,128)(2,1)} %collective-permute-done.3.part), channel_id=1, source_target_pairs={{0,8},{8,16},{12,4},{16,24},{20,12},{28,20},{1,9},{9,17},{13,5},{1... | collective-permute-start | bytes 2359304 | tf_op jit(solution)/shard_map/ppermute | solution.py:269
  25.7 18.3 %collective-permute-start.4 = (bf16[2,128,1536]{2,1,0:T(8,128)(2,1)S(1)}, bf16[2,128,1536]{2,1,0:T(8,128)(2,1)}, u32[]{:S(2)}, u32[]{:S(2)}) collective-permute-start(bf16[2,128,1536]{2,1,0:T(8,128)(2,1)S(1)} %get-tuple-element.20.own.keys), channel_id=1, source_target_pairs={{4,12},{8,0},{12,20},{16,8},{20,28},{24,16},{5,13},{9,1},{13,21},{... | collective-permute-start | bytes 2359304 | tf_op jit(solution)/shard_map/ppermute | solution.py:269
  27.0 17.0 %collective-permute-start.2 = (bf16[2,128,1536]{2,1,0:T(8,128)(2,1)S(1)}, bf16[2,128,1536]{2,1,0:T(8,128)(2,1)}, u32[]{:S(2)}, u32[]{:S(2)}) collective-permute-start(bf16[2,128,1536]{2,1,0:T(8,128)(2,1)S(1)} %get-tuple-element.20.own.keys), channel_id=1, source_target_pairs={{1,2},{2,1},{5,6},{6,5},{9,10},{10,9},{13,14},{14,13},{17,18},{18,... | collective-permute-start | bytes 2359304 | tf_op jit(solution)/shard_map/ppermute | solution.py:279
  33.2 30.7 %collective-permute-start.10 = (bf16[2,128,1536]{2,1,0:T(8,128)(2,1)S(1)}, bf16[2,128,1536]{2,1,0:T(8,128)(2,1)S(1)}, u32[]{:S(2)}, u32[]{:S(2)}) collective-permute-start(bf16[2,128,1536]{2,1,0:T(8,128)(2,1)S(1)} %get-tuple-element.26.mine), channel_id=1, source_target_pairs={{0,8},{8,16},{12,4},{16,24},{20,12},{28,20},{1,9},{9,17},{13,5},{1... | collective-permute-start | bytes 2359304 | tf_op jit(solution)/shard_map/ppermute | solution.py:269
  38.6 26.6 %collective-permute-start.11 = (bf16[2,128,1536]{2,1,0:T(8,128)(2,1)S(1)}, bf16[2,128,1536]{2,1,0:T(8,128)(2,1)S(1)}, u32[]{:S(2)}, u32[]{:S(2)}) collective-permute-start(bf16[2,128,1536]{2,1,0:T(8,128)(2,1)S(1)} %collective-permute-done.1.a), channel_id=1, source_target_pairs={{0,4},{4,0},{8,12},{12,8},{16,20},{20,16},{24,28},{28,24},{1,5},{5... | collective-permute-start | bytes 2359304 | tf_op jit(solution)/shard_map/ppermute | solution.py:269
  51.3 14.0 %collective-permute-start.7 = (bf16[2,64,1536]{2,1,0:T(8,128)(2,1)S(1)}, bf16[2,64,1536]{2,1,0:T(8,128)(2,1)S(1)}, u32[]{:S(2)}, u32[]{:S(2)}) collective-permute-start(bf16[2,64,1536]{2,1,0:T(8,128)(2,1)S(1)} %get-tuple-element.24), channel_id=1, source_target_pairs={{0,1},{1,0},{2,3},{3,2},{4,5},{5,4},{6,7},{7,6},{8,9},{9,8},{10,11... | collective-permute-start | bytes 1179656 | tf_op jit(solution)/shard_map/ppermute | solution.py:316
  55.0 10.3 %collective-permute-start.8 = (bf16[2,64,1536]{2,1,0:T(8,128)(2,1)S(1)}, bf16[2,64,1536]{2,1,0:T(8,128)(2,1)S(1)}, u32[]{:S(2)}, u32[]{:S(2)}) collective-permute-start(bf16[2,64,1536]{2,1,0:T(8,128)(2,1)S(1)} %get-tuple-element.25), channel_id=1, source_target_pairs={{1,2},{2,1},{5,6},{6,5},{9,10},{10,9},{13,14},{14,13},{17,18},{18,... | collective-permute-start | bytes 1179656 | tf_op jit(solution)/shard_map/ppermute | solution.py:317
  58.0 2.9 %collective-permute-start.12 = (f32[5,12,128]{2,1,0:T(8,128)S(1)}, f32[5,12,128]{2,1,0:T(8,128)S(1)}, u32[]{:S(2)}, u32[]{:S(2)}) collective-permute-start(f32[5,12,128]{2,1,0:T(8,128)S(1)} %get-tuple-element.28), channel_id=1, source_target_pairs={{0,4},{4,0},{8,12},{12,8},{16,20},{20,16},{24,28},{28,24},{1,5},{5... | collective-permute-start | bytes 92168 | tf_op jit(solution)/shard_map/ppermute | solution.py:269
  61.0 4.3 %collective-permute-start.13 = (f32[2,5,12,128]{3,2,1,0:T(8,128)S(1)}, f32[2,5,12,128]{3,2,1,0:T(8,128)S(1)}, u32[]{:S(2)}, u32[]{:S(2)}) collective-permute-start(f32[2,5,12,128]{3,2,1,0:T(8,128)S(1)} %pad_maximum_fusion), channel_id=1, source_target_pairs={{0,8},{8,16},{12,4},{16,24},{20,12},{28,20},{1,9},{9,17},{13,5},{1... | collective-permute-start | bytes 184328 | tf_op jit(solution)/shard_map/ppermute | solution.py:269
  63.9 4.7 %collective-permute-start.14 = (f32[5,12,128]{2,1,0:T(8,128)S(1)}, f32[5,12,128]{2,1,0:T(8,128)S(1)}, u32[]{:S(2)}, u32[]{:S(2)}) collective-permute-start(f32[5,12,128]{2,1,0:T(8,128)S(1)} %get-tuple-element.28), channel_id=1, source_target_pairs={{4,12},{8,0},{12,20},{16,8},{20,28},{24,16},{5,13},{9,1},{13,21},{... | collective-permute-start | bytes 92168 | tf_op jit(solution)/shard_map/ppermute | solution.py:269
